TPU v7x, 128 devices: a whole 4x4x4 slice. The times are simulated.
128 devices in a mesh: pool: 16 (over y, x), tp: 8 (over z, core).
Axes of the slice: x: 4, y: 4, z: 4, core: 2. Of those that a mesh axis runs over, the one named last changes fastest.
Arguments:
- prompt_latent: bfloat16 [512, 384, 576], P('pool'), may hold values from -4 to 4
- prompt_lengths: int32 [512], replicated, may hold values from 192 to 384, as said below
- decode_slot: int32 [512], replicated, may hold values from 0 to 511, as said below
- new_latent: bfloat16 [4, 512, 576], P(None, 'pool'), may hold values from -4 to 4
- queries: bfloat16 [4, 512, 64, 192], P(None, 'pool', 'tp'), may hold values from -48 to 48
- w_uk: bfloat16 [64, 512, 128], P('tp'), may hold values from -0.25 to 0.25
- w_uv: bfloat16 [64, 512, 128], P('tp'), may hold values from -1.5 to 1.5
- w_out: bfloat16 [8192, 2560], P('tp'), may hold values from -0.0625 to 0.0625
Outputs:
- decoded: bfloat16 [512, 4, 2560], P('pool')
- context: bfloat16 [512, 384, 576], P('pool', 'tp')
Inputs may be any that keep to these rules, and one draw needn't show every extreme that they name: `prompt_lengths`: each block of 32 consecutive prefill slots holds a prompt of exactly 384 rows and one of exactly 192 rows. `decode_slot`: a one-to-one map of prefill slots onto decode slots; prefill slot g belongs to prefill owner g // 32 and decode slot i to decode owner i // 32; of one prefill owner's 32 slots at most 4 go to any one decode owner, and exactly 4 go to one of them.
All inputs are finite; a program needn't handle non-finite values.
Results may differ from a plain program's by a relative error of at most 0.02.
Values may be sent and summed in bfloat16 or wider, within the bound.
No kernel may reach another device: no remote copies, remote signals or barrier semaphores. Data moves between devices by JAX's collectives and lax.ppermute only.
A program may use at most 192 MiB of HBM per device.

v0:
```python
import math

import jax
import jax.numpy as jnp
from jax import lax
from jax.sharding import PartitionSpec as P

ROPE = 64
NOPE = 128


floor_score = -1e30


def attend(running, complete_query, key_row_block, allowed):
    peak, softmax_totals, summed = running
    latent_width = summed.shape[-1]
    logit_scores = jnp.einsum(
        "rqc,rkc->rqk", complete_query, key_row_block, preferred_element_type=jnp.float32
    ) * (1.0 / math.sqrt(NOPE + ROPE))
    masked = jnp.where(allowed, logit_scores, floor_score)
    peak_now = jnp.maximum(peak, jnp.max(masked, axis=-1))
    weights = jnp.where(allowed, jnp.exp(logit_scores - peak_now[..., None]), 0.0)
    factor = jnp.exp(peak - peak_now)
    softmax_totals = softmax_totals * factor + jnp.sum(weights, axis=-1)
    summed = summed * factor[..., None] + jnp.einsum(
        "rqk,rkc->rqc",
        weights.astype(jnp.bfloat16),
        key_row_block[..., :latent_width],
        preferred_element_type=jnp.float32,
    )
    return (peak_now, softmax_totals, summed)


def body(prompt_latent, prompt_lengths, decode_slot, new_latent, queries, w_uk, w_uv, w_out):
    pool_count = lax.axis_size("pool")
    tp_count = lax.axis_size("tp")
    pool_index = lax.axis_index("pool")
    tp_index = lax.axis_index("tp")
    step_count = new_latent.shape[0]
    slot_count = new_latent.shape[1]
    head_count = queries.shape[2]
    feature = prompt_latent.shape[2]
    prompt_span = prompt_latent.shape[1]
    piece_rows = prompt_span // tp_count
    latent_width = w_uk.shape[1]
    capacity = max(2, 2 * slot_count // pool_count)
    own_slots = lax.dynamic_slice_in_dim(decode_slot, pool_index * slot_count, slot_count)
    targets = own_slots // slot_count
    earlier = jnp.tril(jnp.ones((slot_count, slot_count), jnp.int32), -1)
    same_dest = (targets[:, None] == targets[None, :]).astype(jnp.int32)
    ranking = jnp.sum(same_dest * earlier, axis=1)
    placing = targets * capacity + ranking
    matches = placing[None, :] == jnp.arange(pool_count * capacity)[:, None]
    source_row = jnp.min(jnp.where(matches, jnp.arange(slot_count)[None, :], slot_count), axis=1)
    wanted = pool_index * slot_count + jnp.arange(slot_count)
    match_rows = decode_slot[None, :] == wanted[:, None]
    anchor = jnp.sum(jnp.where(match_rows, jnp.arange(decode_slot.shape[0])[None, :], 0), axis=1)
    arriving = (
        (decode_slot // slot_count == pool_index).astype(jnp.int32).reshape(pool_count, slot_count)
    )
    before = (jnp.cumsum(arriving, axis=1) - arriving).reshape(-1)
    arrival = anchor // slot_count * capacity + jnp.take(before, anchor)
    context_length = jnp.take(prompt_lengths, anchor)
    absorbed = jnp.einsum(
        "srhn,hcn->rshc", queries[..., :NOPE], w_uk, preferred_element_type=jnp.float32
    ).astype(jnp.bfloat16)
    rotary = jnp.transpose(queries[..., NOPE:], (1, 0, 2, 3))
    complete_query = jnp.concatenate([absorbed, rotary], axis=-1).reshape(
        slot_count, step_count * head_count, latent_width + ROPE
    )
    query_rows = step_count * head_count
    start_state = (
        jnp.full((slot_count, query_rows), floor_score, jnp.float32),
        jnp.zeros((slot_count, query_rows), jnp.float32),
        jnp.zeros((slot_count, query_rows, latent_width), jnp.float32),
    )
    outgoing = jnp.take(prompt_latent, source_row, axis=0, mode="fill", fill_value=0).reshape(
        pool_count, capacity, prompt_span, feature
    )
    incoming = lax.all_to_all(outgoing, "pool", split_axis=0, concat_axis=0, tiled=True)
    context = jnp.take(
        incoming.reshape(pool_count * capacity, prompt_span, feature), arrival, axis=0
    )
    position = jnp.arange(context.shape[1], dtype=jnp.int32)
    allowed = position[None, None, :] < context_length[:, None, None]
    running = attend(start_state, complete_query, context, allowed)
    own_piece = lax.dynamic_slice_in_dim(context, tp_index * piece_rows, piece_rows, 1)
    piece_position = tp_index * piece_rows + jnp.arange(piece_rows, dtype=jnp.int32)
    piece_valid = piece_position[None, :] < context_length[:, None]
    context_out = jnp.where(piece_valid[..., None], own_piece, jnp.zeros((), own_piece.dtype))
    fresh_rows = jnp.transpose(new_latent, (1, 0, 2))
    step_of = jnp.arange(query_rows, dtype=jnp.int32) // head_count
    causal_mask = (jnp.arange(step_count, dtype=jnp.int32)[None, :] <= step_of[:, None])[None, :, :]
    peak, softmax_totals, summed = attend(running, complete_query, fresh_rows, causal_mask)
    weighted_latent = (
        (summed / softmax_totals[..., None])
        .astype(jnp.bfloat16)
        .reshape(slot_count, step_count, head_count, latent_width)
    )
    head_out = jnp.einsum(
        "rshc,hcv->rshv", weighted_latent, w_uv, preferred_element_type=jnp.float32
    ).astype(jnp.bfloat16)
    partial_out = jnp.dot(
        head_out.reshape(slot_count * step_count, -1), w_out, preferred_element_type=jnp.float32
    )
    summed_out = lax.psum(partial_out.astype(jnp.bfloat16), "tp").astype(jnp.float32)
    return (summed_out.reshape(slot_count, step_count, -1).astype(jnp.bfloat16), context_out)


def solution(mesh):
    in_specs = (
        P("pool", None, None),
        P(),
        P(),
        P(None, "pool", None),
        P(None, "pool", "tp", None),
        P("tp", None, None),
        P("tp", None, None),
        P("tp", None),
    )
    out_specs = (P("pool", None, None), P("pool", "tp", None))
    return jax.shard_map(body, mesh=mesh, in_specs=in_specs, out_specs=out_specs, check_vma=False)
```

profile of v0, /device:TPU:1, one launch (start us, length us, event | category | flops | bytes accessed | tf_op | source)
XLA Modules:
  0.0 616.6 jit_solution(7634050160786747450)
XLA Ops:
  7.2 0.9 and_select_fusion.1
  8.4 17.0 %gather_fusion = bf16[64,384,576]{1,2,0:T(8,128)(2,1)} fusion(bf16[32,384,576]{1,2,0:T(8,128)(2,1)} %param.10, s32[1024]{0:T(1024)S(1)} %pad_clamp_fusion.1), kind=kCustom, calls=%fused_computation.2 | custom fusion | bytes 56623360 | tf_op jit(solution)/shard_map/jit(_take)/gather | solution.py:78
  25.4 19.6 %broadcast_select_fusion = bf16[16,4,384,576]{2,3,1,0:T(8,128)(2,1)} fusion(bf16[16,4,384,576]{2,3,1,0:T(8,128)(2,1)} %bitcast.50, pred[16,4]{1,0:T(8,128)(4,1)S(1)} %compare_and_fusion), kind=kLoop, calls=%fused_computation.4 | loop fusion | flops 14155776 | bytes 56623168 | tf_op jit(solution)/shard_map/jit(_take)/select_n | solution.py:78
  45.0 7.7 %all-to-all-start = ((bf16[16,4,384,576]{2,3,1,0:T(8,128)(2,1)}), bf16[16,4,384,576]{2,3,1,0:T(8,128)(2,1)}, u32[]{:S(2)}, u32[]{:S(2)}) async-start(bf16[16,4,384,576]{2,3,1,0:T(8,128)(2,1)} %broadcast_select_fusion), calls=%async_computation | async-start | bytes 56623104 | tf_op jit(solution)/shard_map/all_to_all | solution.py:81
  53.4 0.7 gather_fusion.3
  54.1 0.7 gather_fusion.2
  55.1 0.4 fusion.37
  55.9 0.9 copy-done.3
  56.9 0.9 select_reduce_fusion.1
  57.8 417.0 %all-to-all-done = bf16[16,4,384,576]{2,3,1,0:T(8,128)(2,1)} async-done(((bf16[16,4,384,576]{2,3,1,0:T(8,128)(2,1)}), bf16[16,4,384,576]{2,3,1,0:T(8,128)(2,1)}, u32[]{:S(2)}, u32[]{:S(2)}) %all-to-all-start) | async-done | bytes 28311584 | tf_op jit(solution)/shard_map/all_to_all | solution.py:81
  474.8 17.1 %gather_fusion.1 = bf16[32,384,576]{1,2,0:T(8,128)(2,1)} fusion(bf16[64,384,576]{1,2,0:T(8,128)(2,1)} %bitcast.9, s32[1024]{0:T(1024)S(1)} %pad_clamp_fusion), kind=kCustom, calls=%fused_computation.3 | custom fusion | bytes 28311680 | tf_op jit(solution)/shard_map/jit(_take)/gather | solution.py:82
  491.9 18.7 %copy.26 = bf16[32,384,576]{2,1,0:T(8,128)(2,1)} copy(bf16[32,384,576]{1,2,0:T(8,128)(2,1)} %gather_fusion.1) | data formatting | bytes 28311552 | tf_op jit(solution)/shard_map/jit(_take)/gather | solution.py:82
  510.6 13.7 %broadcast_select_fusion.1 = bf16[32,384,576]{2,1,0:T(8,128)(2,1)} fusion(bf16[32,384,576]{2,1,0:T(8,128)(2,1)} %copy.26, pred[32]{0:T(512)(128)(4,1)S(1)} %get-tuple-element.5), kind=kLoop, calls=%fused_computation.5 | loop fusion | flops 7077888 | bytes 28311584 | tf_op jit(solution)/shard_map/jit(_take)/select_n | solution.py:82
  524.4 10.7 %select_reduce_fusion = (f32[32,32]{1,0:T(8,128)S(1)}, f32[32,32,384]{2,1,0:T(8,128)S(1)}) fusion(pred[32,384]{1,0:T(8,128)(4,1)S(1)} %iota_compare_fusion, bf16[32,384,576]{2,1,0:T(8,128)(2,1)} %broadcast_select_fusion.1, bf16[32,4,8,576]{3,0,1,2:T(8,128)(2,1)} %copy-done.3), kind=kOutput, calls=%fused_computation.12 | convolution fusion | flops 454163456 | bytes 16924672 | tf_op jit(solution)/shard_map/rqc,rkc->rqk/dot_general | solution.py:18
  535.1 0.5 fusion.6
  535.6 5.9 fusion
  541.6 0.7 fusion.2
  542.3 0.5 copy-done.6
  542.8 1.3 fusion.8
  544.3 3.3 convolution_convert_fusion
  547.6 1.0 convert_element_type.42
  548.7 3.4 dynamic-slice_select_fusion
  552.1 55.5 %all-reduce.2.cloned.1.call-done = bf16[32,4,2560]{2,1,0:T(4,128)(2,1)} async-done(((bf16[32,4,2560]{2,1,0:T(4,128)(2,1)}), bf16[32,4,2560]{2,1,0:T(4,128)(2,1)}) %all-reduce.2.cloned.1.call-update) | async-done | bytes 655376 | tf_op jit(solution)/shard_map/psum | solution.py:107
  607.6 2.1 copy.64
  (51 shorter events, 2.0 us)
Async XLA Ops:
  7.2 47.9 %copy-start = (bf16[8,512,128]{2,1,0:T(8,128)(2,1)S(1)}, bf16[8,512,128]{2,1,0:T(8,128)(2,1)}, u32[]{:S(2)}) copy-start(bf16[8,512,128]{2,1,0:T(8,128)(2,1)} %param.15) | copy-start | bytes 3145732
  45.0 7.8 %copy-start.5 = (s32[512]{0:T(512)S(1)}, s32[512]{0:T(512)}, u32[]{:S(2)}) copy-start(s32[512]{0:T(512)} %param.12) | copy-start | bytes 6148
  45.0 9.1 %copy-start.2 = (s32[512]{0:T(512)S(1)}, s32[512]{0:T(512)}, u32[]{:S(2)}) copy-start(s32[512]{0:T(512)} %param.11) | copy-start | bytes 6148
  45.0 429.8 %all-to-all-start = ((bf16[16,4,384,576]{2,3,1,0:T(8,128)(2,1)}), bf16[16,4,384,576]{2,3,1,0:T(8,128)(2,1)}, u32[]{:S(2)}, u32[]{:S(2)}) async-start(bf16[16,4,384,576]{2,3,1,0:T(8,128)(2,1)} %broadcast_select_fusion), calls=%async_computation | async-start | bytes 56623104 | tf_op jit(solution)/shard_map/all_to_all | solution.py:81
  52.7 2.1 slice-start
  52.7 2.2 slice-start.1
  52.7 2.2 copy-start.4
  52.7 554.9 %all-reduce.2.cloned.1.call-start = ((), (), s32[]{:S(2)}) async-start(), calls=%async_computation.1 | async-start | bytes 1310720 | tf_op jit(solution)/shard_map/psum | solution.py:107
  55.8 1.1 copy-start.3
  541.5 1.2 copy-start.6
  548.7 61.0 %copy-start.1 = (bf16[8,512,128]{2,1,0:T(8,128)(2,1)S(1)}, bf16[8,512,128]{2,1,0:T(8,128)(2,1)}, u32[]{:S(2)}) copy-start(bf16[8,512,128]{2,1,0:T(8,128)(2,1)} %param.15) | copy-start | bytes 3145732
Sparse Core Ops, SparseCore 0:
  548.7 58.8 all-reduce.1
where the time goes:
time: 619 us; the launch traced here: 617 us
  waiting for transfers between devices  473 us (76%)
  local copies, waits for them, and re-layouts  59.4 us (10%)
  other arithmetic  39.3 us (6%)
  matrix products  23.3 us (4%)
  between operations  14.3 us (2%)
  starting transfers between devices  7.72 us (1%)
    all_to_all x1, waiting for transfers between devices, body(): lax.all_to_all(outgoing, 'pool', split_axis=0, concat_axis=0, tiled=True)  417 us
    psum x1, waiting for transfers between devices, body(): lax.psum(partial_out.astype(jnp.bfloat16), 'tp').astype(jnp.float32)  55.5 us
    gather x2, local copies, waits for them, and re-layouts, body(): jnp.take(incoming.reshape(pool_count * capacity, prompt_span, feature), a...  35.8 us
    select_n x2, other arithmetic, body(): jnp.take(prompt_latent, source_row, axis=0, mode='fill', fill_value=0)  19.6 us
    gather x1, local copies, waits for them, and re-layouts, body(): jnp.take(prompt_latent, source_row, axis=0, mode='fill', fill_value=0)  17 us
    select_n x1, other arithmetic, body(): jnp.take(incoming.reshape(pool_count * capacity, prompt_span, feature), a...  13.7 us
  transfers between devices with their start and end apart: 2, of which 2 were waited for; matrix products, arithmetic and copies ran while one was open for 1% of the time, Pallas kernels for 0%

commit v1 on v0

v1 whole, which is shorter than its diff:
```python
import math

import jax
import jax.numpy as jnp
from jax import lax
from jax.sharding import PartitionSpec as P

ROPE = 64
NOPE = 128
CAP = 4
FIRST_RANKS = 3
FLOOR = -1e30


def route(decode_slot, pool_index, pool_count, slot_count):
    targets = decode_slot // slot_count
    by_source = targets.reshape(pool_count, slot_count)
    earlier = jnp.tril(jnp.ones((slot_count, slot_count), jnp.int32), -1)
    own = lax.dynamic_slice_in_dim(by_source, pool_index, 1, 0)[0]
    same = (own[:, None] == own[None, :]).astype(jnp.int32)
    placing = own * CAP + jnp.sum(same * earlier, axis=1)
    cells = jnp.arange(pool_count * CAP)
    source_row = jnp.sum(
        jnp.where(placing[None, :] == cells[:, None], jnp.arange(slot_count)[None, :], 0), axis=1
    )
    arriving = (by_source == pool_index).astype(jnp.int32)
    before = jnp.cumsum(arriving, axis=1) - arriving
    cell = (jnp.arange(pool_count)[:, None] * CAP + before).reshape(-1)
    wanted = pool_index * slot_count + jnp.arange(slot_count)
    match = decode_slot[None, :] == wanted[:, None]
    arrival = jnp.sum(jnp.where(match, cell[None, :], 0), axis=1)
    decode_row = jnp.sum(
        jnp.where(arrival[None, :] == cells[:, None], jnp.arange(slot_count)[None, :], 0), axis=1
    )
    return placing, source_row, arrival, decode_row, match


def body(prompt_latent, prompt_lengths, decode_slot, new_latent, queries, w_uk, w_uv, w_out):
    pool_count = lax.axis_size("pool")
    tp_count = lax.axis_size("tp")
    pool_index = lax.axis_index("pool")
    tp_index = lax.axis_index("tp")
    steps, slots, heads, width = queries.shape
    span, feature = prompt_latent.shape[1:]
    piece = span // tp_count
    latent = w_uk.shape[1]
    out_width = w_out.shape[1]
    cells = pool_count * CAP
    placing, source_row, arrival, decode_row, match = route(
        decode_slot, pool_index, pool_count, slots
    )
    decode_lengths = jnp.sum(jnp.where(match, prompt_lengths[None, :], 0), axis=1)
    own_lengths = lax.dynamic_slice_in_dim(prompt_lengths, pool_index * slots, slots)

    q_out = jnp.take(queries, decode_row, axis=1).transpose(1, 0, 2, 3).reshape(cells, -1)
    n_out = jnp.take(new_latent, decode_row, axis=1).transpose(1, 0, 2).reshape(cells, -1)
    payload = jnp.concatenate([q_out, n_out], axis=1).reshape(pool_count, -1, 128)
    payload = lax.all_to_all(payload, "pool", split_axis=0, concat_axis=0, tiled=True)

    own_piece = lax.dynamic_slice_in_dim(prompt_latent, tp_index * piece, piece, 1)
    sending = jnp.take(own_piece, source_row, axis=0).reshape(
        pool_count, CAP, piece, feature
    )
    payload, first_send = lax.optimization_barrier((payload, sending[:, :FIRST_RANKS]))
    first = lax.all_to_all(first_send, "pool", split_axis=0, concat_axis=0, tiled=True)

    payload = jnp.take(payload.reshape(cells, -1), placing, axis=0)
    q_size = steps * heads * width
    q = payload[:, :q_size].reshape(slots, steps, heads, width)
    fresh = payload[:, q_size:].reshape(slots, steps, feature)

    absorbed = jnp.einsum(
        "rshn,hcn->rshc", q[..., :NOPE], w_uk, preferred_element_type=jnp.float32
    ).astype(jnp.bfloat16)
    full_q = jnp.concatenate([absorbed, q[..., NOPE:]], axis=-1).reshape(
        slots, steps * heads, feature
    )
    scale = 1.0 / math.sqrt(width)
    step_of = jnp.arange(steps * heads, dtype=jnp.int32) // heads
    s_prompt = scale * jnp.einsum(
        "rqc,rkc->rqk", full_q, prompt_latent, preferred_element_type=jnp.float32
    )
    s_fresh = scale * jnp.einsum(
        "rqc,rkc->rqk", full_q, fresh, preferred_element_type=jnp.float32
    )
    ok_prompt = jnp.arange(span)[None, None, :] < own_lengths[:, None, None]
    ok_fresh = (jnp.arange(steps)[None, :] <= step_of[:, None])[None]
    s_prompt = jnp.where(ok_prompt, s_prompt, FLOOR)
    s_fresh = jnp.where(ok_fresh, s_fresh, FLOOR)
    peak = jnp.maximum(jnp.max(s_prompt, -1), jnp.max(s_fresh, -1))[..., None]
    w_prompt = jnp.exp(s_prompt - peak)
    w_fresh = jnp.exp(s_fresh - peak)
    totals = jnp.sum(w_prompt, -1) + jnp.sum(w_fresh, -1)
    mixed = jnp.einsum(
        "rqk,rkc->rqc",
        w_prompt.astype(jnp.bfloat16),
        prompt_latent[..., :latent],
        preferred_element_type=jnp.float32,
    ) + jnp.einsum(
        "rqk,rkc->rqc",
        w_fresh.astype(jnp.bfloat16),
        fresh[..., :latent],
        preferred_element_type=jnp.float32,
    )
    mixed = (mixed / totals[..., None]).astype(jnp.bfloat16)
    mixed = mixed.reshape(slots, steps, heads, latent)
    head_out = jnp.einsum(
        "rshc,hcv->srhv", mixed, w_uv, preferred_element_type=jnp.float32
    ).astype(jnp.bfloat16)
    partial = jnp.dot(
        head_out.reshape(steps * slots, -1), w_out, preferred_element_type=jnp.float32
    )

    core = tp_index % 2
    z = tp_index // 2
    z_count = tp_count // 2
    half = steps * slots // 2
    block = out_width // z_count
    swap = [(i, i ^ 1) for i in range(tp_count)]

    def hop(d):
        return [(i, i ^ (2 * d)) for i in range(tp_count)]

    kept = lax.dynamic_slice_in_dim(partial, core * half, half, 0)
    given = lax.dynamic_slice_in_dim(partial, (1 - core) * half, half, 0).astype(jnp.bfloat16)
    pair = kept + lax.ppermute(given, "tp", swap).astype(jnp.float32)
    mine = lax.dynamic_slice_in_dim(pair, z * block, block, 1)
    pair16 = pair.astype(jnp.bfloat16)
    got = [
        lax.ppermute(
            lax.dynamic_slice_in_dim(pair16, (z ^ d) * block, block, 1), "tp", hop(d)
        )
        for d in range(1, z_count)
    ]
    for part in got:
        mine = mine + part.astype(jnp.float32)
    mine = mine.astype(jnp.bfloat16).reshape(steps // 2, slots, block)

    back = jnp.take(mine, source_row, axis=1).transpose(1, 0, 2)
    back = back.reshape(pool_count, CAP * steps // 2, block)
    back, first = lax.optimization_barrier((back, first))
    back = lax.all_to_all(back, "pool", split_axis=0, concat_axis=0, tiled=True)
    back, second_send = lax.optimization_barrier((back, sending[:, FIRST_RANKS:]))
    second = lax.all_to_all(second_send, "pool", split_axis=0, concat_axis=0, tiled=True)

    back = jnp.take(back.reshape(cells, steps // 2, block), arrival, axis=0)
    parts = jnp.stack([back] + [lax.ppermute(back, "tp", hop(d)) for d in range(1, z_count)])
    parts = jnp.take(parts, jnp.arange(z_count) ^ z, axis=0)
    row_half = parts.transpose(1, 2, 0, 3).reshape(slots, steps // 2, out_width)
    other_half = lax.ppermute(row_half, "tp", swap)
    decoded = jnp.concatenate(
        [
            jnp.where(core == 0, row_half, other_half),
            jnp.where(core == 0, other_half, row_half),
        ],
        axis=1,
    )

    owner, rank = arrival // CAP, arrival % CAP
    both = jnp.concatenate([first, second], axis=1).reshape(cells, piece, feature)
    context = jnp.take(both, owner * CAP + rank, axis=0)
    position = tp_index * piece + jnp.arange(piece, dtype=jnp.int32)
    valid = position[None, :] < decode_lengths[:, None]
    context = jnp.where(valid[..., None], context, jnp.zeros((), context.dtype))
    return decoded, context


def solution(mesh):
    in_specs = (
        P("pool", None, None),
        P(),
        P(),
        P(None, "pool", None),
        P(None, "pool", "tp", None),
        P("tp", None, None),
        P("tp", None, None),
        P("tp", None),
    )
    out_specs = (P("pool", None, None), P("pool", "tp", None))
    return jax.shard_map(body, mesh=mesh, in_specs=in_specs, out_specs=out_specs, check_vma=False)
```

time: 619 us -> 184 us (0.30)
  waiting for transfers between devices: 473 us -> 54.3 us
  starting transfers between devices: 7.72 us -> 37.1 us
  other arithmetic: 39.3 us -> 16.2 us
  between operations: 14.3 us -> 1.22 us
  local copies, waits for them, and re-layouts: 59.4 us -> 51.4 us
    all_to_all x1 -> x4, waiting for transfers between devices: 417 us -> 43.6 us  [the longest x1 22.4 us: body(): lax.all_to_all(first_send, 'pool', split_axis=0, concat_axis=0, tiled=True)]
    psum x1 -> x0, waiting for transfers between devices: 55.5 us -> none  [body(): lax.psum(partial_out.astype(jnp.bfloat16), 'tp').astype(jnp.float32)]
    select_n x8 -> x14, other arithmetic: 37.5 us -> 7.88 us  [the longest x1 4.56 us: body(): jnp.take(own_piece, source_row, axis=0)]
    gather x5 -> x9, local copies, waits for them, and re-layouts: 54.2 us -> 27.7 us  [the longest x2 18.2 us: body(): jnp.take(own_piece, source_row, axis=0)]
    ppermute x0 -> x8, starting transfers between devices: none -> 15.3 us  [the longest x1 5.32 us: body(): other_half = lax.ppermute(row_half, 'tp', swap)]
    all_to_all x1 -> x4, starting transfers between devices: 7.68 us -> 21.8 us  [the longest x1 7.59 us: body(): lax.all_to_all(payload, 'pool', split_axis=0, concat_axis=0, tiled=True)]
    ppermute x0 -> x8, waiting for transfers between devices: none -> 10.7 us  [the longest x3 5.49 us: body(): lax.ppermute(lax.dynamic_slice_in_dim(pair16, (z ^ d) * block, block, 1),...]
    dynamic_slice x0 -> x3, local copies, waits for them, and re-layouts: none -> 8.39 us  [the longest x1 7.59 us: body(): lax.dynamic_slice_in_dim(prompt_latent, tp_index * piece, piece, 1)]
  transfers between devices with their start and end apart: 2 -> 12, of which waited for: 2 -> 8; matrix products, arithmetic and copies ran while one was open for 1% -> 25% of each run, Pallas kernels for 0% -> 0%
where the time goes in v1:
time: 184 us; the launch traced here: 183 us
  waiting for transfers between devices  54.3 us (30%)
  local copies, waits for them, and re-layouts  51.4 us (28%)
  starting transfers between devices  37.1 us (20%)
  matrix products  22.6 us (12%)
  other arithmetic  16.2 us (9%)
    all_to_all x1, waiting for transfers between devices, body(): lax.all_to_all(first_send, 'pool', split_axis=0, concat_axis=0, tiled=True)  22.4 us
    gather x2, local copies, waits for them, and re-layouts, body(): jnp.take(own_piece, source_row, axis=0)  18.2 us
    all_to_all x1, waiting for transfers between devices, body(): lax.all_to_all(second_send, 'pool', split_axis=0, concat_axis=0, tiled=True)  16.5 us
    dot_general x1, matrix products, body(): jnp.einsum('rqk,rkc->rqc', w_prompt.astype(jnp.bfloat16), prompt_latent[....  10 us
    dynamic_slice x1, local copies, waits for them, and re-layouts, body(): lax.dynamic_slice_in_dim(prompt_latent, tp_index * piece, piece, 1)  7.59 us
    all_to_all x1, starting transfers between devices, body(): lax.all_to_all(payload, 'pool', split_axis=0, concat_axis=0, tiled=True)  7.59 us
    all_to_all x1, starting transfers between devices, body(): lax.all_to_all(first_send, 'pool', split_axis=0, concat_axis=0, tiled=True)  6.85 us
    dot_general x1, matrix products, body(): jnp.einsum('rqc,rkc->rqk', full_q, prompt_latent, preferred_element_type=...  6.84 us
  transfers between devices with their start and end apart: 12, of which 8 were waited for; matrix products, arithmetic and copies ran while one was open for 25% of the time, Pallas kernels for 0%

profile of v1, /device:TPU:1, one launch (start us, length us, event | category | flops | bytes accessed | tf_op | source)
XLA Modules:
  0.0 182.8 jit_solution(13564980763923422942)
XLA Ops:
  9.4 2.5 %reshape.379 = bf16[16,264,128]{2,1,0:T(8,128)(2,1)} reshape(bf16[64,8448]{1,0:T(8,128)(2,1)S(1)} %pad_maximum_fusion.2) | data formatting | bytes 2162688 | tf_op jit(solution)/shard_map/reshape | solution.py:57
  11.9 7.6 %all-to-all-start = ((bf16[16,264,128]{2,1,0:T(8,128)(2,1)}), bf16[16,264,128]{2,1,0:T(8,128)(2,1)S(1)}, u32[]{:S(2)}, u32[]{:S(2)}) async-start(bf16[16,264,128]{2,1,0:T(8,128)(2,1)} %reshape.379), calls=%async_computation | async-start | bytes 2162688 | tf_op jit(solution)/shard_map/all_to_all | solution.py:58
  19.6 7.6 %constant_dynamic-slice_fusion.2 = bf16[32,48,576]{1,2,0:T(8,128)(2,1)} fusion(bf16[32,384,576]{1,2,0:T(8,128)(2,1)} %param.8, s32[]{:T(128)S(6)} %select_n.303), kind=kLoop, calls=%fused_computation.100 | loop fusion | bytes 3538948 | tf_op jit(solution)/shard_map/dynamic_slice | solution.py:60
  27.2 8.3 %gather_fusion.2 = bf16[64,48,576]{1,2,0:T(8,128)(2,1)} fusion(bf16[32,48,576]{1,2,0:T(8,128)(2,1)} %constant_dynamic-slice_fusion.2, s32[1024]{0:T(1024)S(1)} %pad_clamp_fusion.4), kind=kCustom, calls=%fused_computation.2 | custom fusion | bytes 7078144 | tf_op jit(solution)/shard_map/jit(_take)/gather | solution.py:61
  35.4 9.9 %copy.36 = bf16[16,4,48,576]{3,2,1,0:T(8,128)(2,1)} copy(bf16[16,4,48,576]{2,3,1,0:T(8,128)(2,1)} %bitcast.98) | data formatting | bytes 7077888 | tf_op jit(solution)/shard_map/jit(_take)/gather | solution.py:61
  45.4 4.6 %broadcast_select_fusion = bf16[16,4,48,576]{3,2,1,0:T(8,128)(2,1)} fusion(bf16[16,4,48,576]{3,2,1,0:T(8,128)(2,1)} %copy.36, pred[16,4]{1,0:T(8,128)(4,1)S(1)} %compare_and_fusion), kind=kLoop, calls=%fused_computation.11 | loop fusion | flops 1769472 | bytes 7077952 | tf_op jit(solution)/shard_map/jit(_take)/select_n | solution.py:61
  50.0 3.7 %slice.48 = bf16[16,3,48,576]{3,2,1,0:T(8,128)(2,1)} slice(bf16[16,4,48,576]{3,2,1,0:T(8,128)(2,1)} %broadcast_select_fusion), slice={[0:16], [0:3], [0:48], [0:576]} | slice | bytes 5308416 | tf_op jit(solution)/shard_map/slice | solution.py:64
  58.6 6.8 %fusion.46 = (f32[32,32]{1,0:T(8,128)S(1)}, f32[32,32,384]{2,1,0:T(8,128)S(1)}) fusion(bf16[32,384,576]{1,2,0:T(8,128)(2,1)} %param.8, bf16[32,4,8,576]{3,0,1,2:T(8,128)(2,1)S(1)} %pad_maximum_fusion.1, pred[32,384]{1,0:T(8,128)(4,1)S(1)} %iota_compare_fusion), kind=kOutput, calls=%fused_computation.143 | convolution fusion | flops 454163456 | bytes 16924672 | tf_op jit(solution)/shard_map/rqc,rkc->rqk/dot_general | solution.py:80
  66.8 10.0 %fusion = f32[32,32,512]{2,1,0:T(8,128)} fusion(bf16[32,384,576]{1,2,0:T(8,128)(2,1)} %param.8, f32[32,32,384]{2,1,0:T(8,128)S(1)} %get-tuple-element.34, f32[32,32]{1,0:T(8,128)S(1)} %max.7), kind=kOutput, calls=%fused_computation.8 | convolution fusion | flops 403439616 | bytes 16257024 | tf_op jit(solution)/shard_map/rqk,rkc->rqc/dot_general | solution.py:94
  76.9 6.9 %all-to-all-start.1 = ((bf16[16,3,48,576]{3,2,1,0:T(8,128)(2,1)}), bf16[16,3,48,576]{3,2,1,0:T(8,128)(2,1)}, u32[]{:S(2)}, u32[]{:S(2)}) async-start(bf16[16,3,48,576]{3,2,1,0:T(8,128)(2,1)} %slice.48), calls=%async_computation.1 | async-start | bytes 5898240 | tf_op jit(solution)/shard_map/all_to_all | solution.py:65
  83.8 2.3 %fusion.5 = bf16[32,4,8,512]{3,2,1,0:T(8,128)(2,1)S(1)} fusion(f32[32,32,512]{2,1,0:T(8,128)} %fusion, f32[32,32]{1,0:T(8,128)S(1)} %add.309, bf16[32,4,576]{2,1,0:T(4,128)(2,1)S(1)} %reshape.383, f32[32,32,4]{1,2,0:T(4,128)S(1)} %get-tuple-element.36, f32[32,32]{1,0:T(8,128)S(1)} %max.7), kind=kOutput, calls=%fused_computation.20 | convolution fusion | flops 5775360 | bytes 3375104 | tf_op jit(solution)/shard_map/rqk,rkc->rqc/dot_general | solution.py:99
  93.2 2.0 %collective-permute-start.2 = (bf16[64,640]{1,0:T(8,128)(2,1)S(1)}, bf16[64,640]{1,0:T(8,128)(2,1)S(1)}, u32[]{:S(2)}, u32[]{:S(2)}) collective-permute-start(bf16[64,640]{1,0:T(8,128)(2,1)S(1)} %get-tuple-element.28), channel_id=1, source_target_pairs={{0,4},{1,5},{2,6},{3,7},{4,0},{5,1},{6,2},{7,3},{8,12},{9,13},{10,... | collective-permute-start | bytes 245768 | tf_op jit(solution)/shard_map/ppermute | solution.py:130
  95.7 3.6 %collective-permute-done.2 = bf16[64,640]{1,0:T(8,128)(2,1)S(1)} collective-permute-done((bf16[64,640]{1,0:T(8,128)(2,1)S(1)}, bf16[64,640]{1,0:T(8,128)(2,1)S(1)}, u32[]{:S(2)}, u32[]{:S(2)}) %collective-permute-start.2) | collective-permute-done | bytes 81952 | tf_op jit(solution)/shard_map/ppermute | solution.py:130
  103.2 22.4 %all-to-all-done.1 = bf16[16,3,48,576]{3,2,1,0:T(8,128)(2,1)} async-done(((bf16[16,3,48,576]{3,2,1,0:T(8,128)(2,1)}), bf16[16,3,48,576]{3,2,1,0:T(8,128)(2,1)}, u32[]{:S(2)}, u32[]{:S(2)}) %all-to-all-start.1) | async-done | bytes 2654240 | tf_op jit(solution)/shard_map/all_to_all | solution.py:65
  125.5 3.7 %all-to-all-start.2 = ((bf16[16,8,640]{2,1,0:T(8,128)(2,1)}), bf16[16,8,640]{2,1,0:T(8,128)(2,1)S(1)}, u32[]{:S(2)}, u32[]{:S(2)}) async-start(bf16[16,8,640]{2,1,0:T(8,128)(2,1)} %reshape.387), calls=%async_computation.2 | async-start | bytes 327680 | tf_op jit(solution)/shard_map/all_to_all | solution.py:142
  129.3 2.2 %slice.54 = bf16[16,1,48,576]{3,2,1,0:T(8,128)(2,1)} slice(bf16[16,4,48,576]{3,2,1,0:T(8,128)(2,1)} %broadcast_select_fusion), slice={[0:16], [3:4], [0:48], [0:576]} | slice | bytes 1769472 | tf_op jit(solution)/shard_map/slice | solution.py:143
  131.5 4.8 %all-to-all-done.2 = bf16[16,8,640]{2,1,0:T(8,128)(2,1)S(1)} async-done(((bf16[16,8,640]{2,1,0:T(8,128)(2,1)}), bf16[16,8,640]{2,1,0:T(8,128)(2,1)S(1)}, u32[]{:S(2)}, u32[]{:S(2)}) %all-to-all-start.2) | async-done | bytes 163872 | tf_op jit(solution)/shard_map/all_to_all | solution.py:142
  138.9 2.1 %collective-permute-start.5 = (bf16[32,2,640]{2,1,0:T(2,128)(2,1)S(1)}, bf16[32,2,640]{2,1,0:T(2,128)(2,1)S(1)}, u32[]{:S(2)}, u32[]{:S(2)}) collective-permute-start(bf16[32,2,640]{2,1,0:T(2,128)(2,1)S(1)} %broadcast_select_fusion.7), channel_id=1, source_target_pairs={{0,4},{1,5},{2,6},{3,7},{4,0},{5,1},{6,2},{7,3},{8,12},{9,13},{10,... | collective-permute-start | bytes 245768 | tf_op jit(solution)/shard_map/ppermute | solution.py:147
  141.6 2.1 %collective-permute-done.5 = bf16[32,2,640]{2,1,0:T(2,128)(2,1)S(1)} collective-permute-done((bf16[32,2,640]{2,1,0:T(2,128)(2,1)S(1)}, bf16[32,2,640]{2,1,0:T(2,128)(2,1)S(1)}, u32[]{:S(2)}, u32[]{:S(2)}) %collective-permute-start.5) | collective-permute-done | bytes 81952 | tf_op jit(solution)/shard_map/ppermute | solution.py:147
  146.9 5.3 %collective-permute-start.7 = (bf16[32,2,2560]{2,0,1:T(8,128)(2,1)S(1)}, bf16[32,2,2560]{2,0,1:T(8,128)(2,1)S(1)}, u32[]{:S(2)}, u32[]{:S(2)}) collective-permute-start(bf16[32,2,2560]{2,0,1:T(8,128)(2,1)S(1)} %bitcast.102), channel_id=1, source_target_pairs={{0,1},{1,0},{2,3},{3,2},{4,5},{5,4},{6,7},{7,6},{8,9},{9,8},{10,11... | collective-permute-start | bytes 983048 | tf_op jit(solution)/shard_map/ppermute | solution.py:150
  152.3 3.6 %all-to-all-start.3 = ((bf16[16,1,48,576]{3,2,1,0:T(8,128)(2,1)}), bf16[16,1,48,576]{3,2,1,0:T(8,128)(2,1)S(1)}, u32[]{:S(2)}, u32[]{:S(2)}) async-start(bf16[16,1,48,576]{3,2,1,0:T(8,128)(2,1)} %slice.54), calls=%async_computation.3 | async-start | bytes 1966080 | tf_op jit(solution)/shard_map/all_to_all | solution.py:144
  157.5 16.5 %all-to-all-done.3 = bf16[16,1,48,576]{3,2,1,0:T(8,128)(2,1)S(1)} async-done(((bf16[16,1,48,576]{3,2,1,0:T(8,128)(2,1)}), bf16[16,1,48,576]{3,2,1,0:T(8,128)(2,1)S(1)}, u32[]{:S(2)}, u32[]{:S(2)}) %all-to-all-start.3) | async-done | bytes 884768 | tf_op jit(solution)/shard_map/all_to_all | solution.py:144
  174.0 4.2 %pad_maximum_fusion = bf16[16,4,48,576]{3,2,1,0:T(8,128)(2,1)} fusion(bf16[16,1,48,576]{3,2,1,0:T(8,128)(2,1)S(1)} %all-to-all-done.3, bf16[16,3,48,576]{3,2,1,0:T(8,128)(2,1)} %all-to-all-done.1), kind=kLoop, calls=%fused_computation.10 | loop fusion | flops 1769472 | bytes 7077888 | tf_op jit(solution)/shard_map/concatenate | solution.py:160
  178.2 3.0 %gather_fusion.7 = bf16[32,48,576]{2,1,0:T(8,128)(2,1)S(1)} fusion(bf16[64,48,576]{2,1,0:T(8,128)(2,1)} %bitcast.99, s32[1024]{0:T(1024)S(1)} %pad_clamp_fusion), kind=kCustom, calls=%fused_computation.7 | custom fusion | bytes 3539072 | tf_op jit(solution)/shard_map/jit(_take)/gather | solution.py:161
  (112 shorter events, 35.9 us)
Async XLA Ops:
  0.6 57.4 %copy-start = (bf16[8,512,128]{2,1,0:T(8,128)(2,1)S(1)}, bf16[8,512,128]{2,1,0:T(8,128)(2,1)}, u32[]{:S(2)}) copy-start(bf16[8,512,128]{2,1,0:T(8,128)(2,1)} %param.13) | copy-start | bytes 3145732
  5.7 1.3 copy-start.2
  11.9 42.7 %all-to-all-start = ((bf16[16,264,128]{2,1,0:T(8,128)(2,1)}), bf16[16,264,128]{2,1,0:T(8,128)(2,1)S(1)}, u32[]{:S(2)}, u32[]{:S(2)}) async-start(bf16[16,264,128]{2,1,0:T(8,128)(2,1)} %reshape.379), calls=%async_computation | async-start | bytes 2162688 | tf_op jit(solution)/shard_map/all_to_all | solution.py:58
  76.9 10.7 %slice-start = ((s8[5242880]{0:T(1024)(128)(4,1)}), s8[1048576]{0:T(1024)(128)(4,1)S(1)}, s32[]{:S(2)}) async-start(s8[5242880]{0:T(1024)(128)(4,1)} %bitcast.100), calls=%async_computation.4 | async-start | bytes 2097152
  76.9 48.6 %all-to-all-start.1 = ((bf16[16,3,48,576]{3,2,1,0:T(8,128)(2,1)}), bf16[16,3,48,576]{3,2,1,0:T(8,128)(2,1)}, u32[]{:S(2)}, u32[]{:S(2)}) async-start(bf16[16,3,48,576]{3,2,1,0:T(8,128)(2,1)} %slice.48), calls=%async_computation.1 | async-start | bytes 5898240 | tf_op jit(solution)/shard_map/all_to_all | solution.py:65
  83.8 2.3 %copy-start.3 = (bf16[8,512,128]{2,1,0:T(8,128)(2,1)S(1)}, bf16[8,512,128]{2,1,0:T(8,128)(2,1)}, u32[]{:S(2)}) copy-start(bf16[8,512,128]{2,1,0:T(8,128)(2,1)} %param.14) | copy-start | bytes 3145732
  83.8 3.8 %slice-start.1 = ((s8[5242880]{0:T(1024)(128)(4,1)}), s8[4194304]{0:T(1024)(128)(4,1)S(1)}, s32[]{:S(2)}) async-start(s8[5242880]{0:T(1024)(128)(4,1)} %bitcast.100), calls=%async_computation.5 | async-start | bytes 8388608
  88.5 2.8 %collective-permute-start = (bf16[64,2560]{1,0:T(8,128)(2,1)S(1)}, bf16[64,2560]{1,0:T(8,128)(2,1)S(1)}, u32[]{:S(2)}, u32[]{:S(2)}) collective-permute-start(bf16[64,2560]{1,0:T(8,128)(2,1)S(1)} %dynamic-slice_convert_fusion), channel_id=1, source_target_pairs={{0,1},{1,0},{2,3},{3,2},{4,5},{5,4},{6,7},{7,6},{8,9},{9,8},{10,11... | collective-permute-start | bytes 983048 | tf_op jit(solution)/shard_map/ppermute | solution.py:126
  91.5 4.2 %collective-permute-start.1 = (bf16[64,640]{1,0:T(8,128)(2,1)S(1)}, bf16[64,640]{1,0:T(8,128)(2,1)S(1)}, u32[]{:S(2)}, u32[]{:S(2)}) collective-permute-start(bf16[64,640]{1,0:T(8,128)(2,1)S(1)} %get-tuple-element.26), channel_id=1, source_target_pairs={{0,2},{1,3},{2,0},{3,1},{4,6},{5,7},{6,4},{7,5},{8,10},{9,11},{10,... | collective-permute-start | bytes 245768 | tf_op jit(solution)/shard_map/ppermute | solution.py:130
  93.2 6.1 %collective-permute-start.2 = (bf16[64,640]{1,0:T(8,128)(2,1)S(1)}, bf16[64,640]{1,0:T(8,128)(2,1)S(1)}, u32[]{:S(2)}, u32[]{:S(2)}) collective-permute-start(bf16[64,640]{1,0:T(8,128)(2,1)S(1)} %get-tuple-element.28), channel_id=1, source_target_pairs={{0,4},{1,5},{2,6},{3,7},{4,0},{5,1},{6,2},{7,3},{8,12},{9,13},{10,... | collective-permute-start | bytes 245768 | tf_op jit(solution)/shard_map/ppermute | solution.py:130
  95.2 5.9 %collective-permute-start.3 = (bf16[64,640]{1,0:T(8,128)(2,1)S(1)}, bf16[64,640]{1,0:T(8,128)(2,1)S(1)}, u32[]{:S(2)}, u32[]{:S(2)}) collective-permute-start(bf16[64,640]{1,0:T(8,128)(2,1)S(1)} %get-tuple-element.27), channel_id=1, source_target_pairs={{0,6},{1,7},{2,4},{3,5},{4,2},{5,3},{6,0},{7,1},{8,14},{9,15},{10,... | collective-permute-start | bytes 245768 | tf_op jit(solution)/shard_map/ppermute | solution.py:130
  125.5 10.7 %all-to-all-start.2 = ((bf16[16,8,640]{2,1,0:T(8,128)(2,1)}), bf16[16,8,640]{2,1,0:T(8,128)(2,1)S(1)}, u32[]{:S(2)}, u32[]{:S(2)}) async-start(bf16[16,8,640]{2,1,0:T(8,128)(2,1)} %reshape.387), calls=%async_computation.2 | async-start | bytes 327680 | tf_op jit(solution)/shard_map/all_to_all | solution.py:142
  137.2 4.4 %collective-permute-start.4 = (bf16[32,2,640]{2,1,0:T(2,128)(2,1)S(1)}, bf16[32,2,640]{2,1,0:T(2,128)(2,1)S(1)}, u32[]{:S(2)}, u32[]{:S(2)}) collective-permute-start(bf16[32,2,640]{2,1,0:T(2,128)(2,1)S(1)} %broadcast_select_fusion.7), channel_id=1, source_target_pairs={{0,2},{1,3},{2,0},{3,1},{4,6},{5,7},{6,4},{7,5},{8,10},{9,11},{10,... | collective-permute-start | bytes 245768 | tf_op jit(solution)/shard_map/ppermute | solution.py:147
  138.9 4.8 %collective-permute-start.5 = (bf16[32,2,640]{2,1,0:T(2,128)(2,1)S(1)}, bf16[32,2,640]{2,1,0:T(2,128)(2,1)S(1)}, u32[]{:S(2)}, u32[]{:S(2)}) collective-permute-start(bf16[32,2,640]{2,1,0:T(2,128)(2,1)S(1)} %broadcast_select_fusion.7), channel_id=1, source_target_pairs={{0,4},{1,5},{2,6},{3,7},{4,0},{5,1},{6,2},{7,3},{8,12},{9,13},{10,... | collective-permute-start | bytes 245768 | tf_op jit(solution)/shard_map/ppermute | solution.py:147
  141.0 4.5 %collective-permute-start.6 = (bf16[32,2,640]{2,1,0:T(2,128)(2,1)S(1)}, bf16[32,2,640]{2,1,0:T(2,128)(2,1)S(1)}, u32[]{:S(2)}, u32[]{:S(2)}) collective-permute-start(bf16[32,2,640]{2,1,0:T(2,128)(2,1)S(1)} %broadcast_select_fusion.7), channel_id=1, source_target_pairs={{0,6},{1,7},{2,4},{3,5},{4,2},{5,3},{6,0},{7,1},{8,14},{9,15},{10,... | collective-permute-start | bytes 245768 | tf_op jit(solution)/shard_map/ppermute | solution.py:147
  146.9 9.1 %collective-permute-start.7 = (bf16[32,2,2560]{2,0,1:T(8,128)(2,1)S(1)}, bf16[32,2,2560]{2,0,1:T(8,128)(2,1)S(1)}, u32[]{:S(2)}, u32[]{:S(2)}) collective-permute-start(bf16[32,2,2560]{2,0,1:T(8,128)(2,1)S(1)} %bitcast.102), channel_id=1, source_target_pairs={{0,1},{1,0},{2,3},{3,2},{4,5},{5,4},{6,7},{7,6},{8,9},{9,8},{10,11... | collective-permute-start | bytes 983048 | tf_op jit(solution)/shard_map/ppermute | solution.py:150
  152.3 21.7 %all-to-all-start.3 = ((bf16[16,1,48,576]{3,2,1,0:T(8,128)(2,1)}), bf16[16,1,48,576]{3,2,1,0:T(8,128)(2,1)S(1)}, u32[]{:S(2)}, u32[]{:S(2)}) async-start(bf16[16,1,48,576]{3,2,1,0:T(8,128)(2,1)} %slice.54), calls=%async_computation.3 | async-start | bytes 1966080 | tf_op jit(solution)/shard_map/all_to_all | solution.py:144
  181.2 1.6 copy-start.1

commit v2 on v1

v2 whole, which is shorter than its diff:
```python
import functools
import math

import jax
import jax.numpy as jnp
from jax import lax
from jax.experimental import pallas as pl
from jax.experimental.pallas import tpu as pltpu
from jax.sharding import PartitionSpec as P

ROPE = 64
NOPE = 128
CAP = 4
FIRST_RANKS = 3
GROUP = 2
FLOOR = -1e30
BF16 = jnp.bfloat16
F32 = jnp.float32

VMEM_LIMIT = 48 * 1024 * 1024
SMEM_SPEC = pl.BlockSpec(memory_space=pltpu.SMEM)
VMEM_SPEC = pl.BlockSpec(memory_space=pltpu.VMEM)
ANY_SPEC = pl.BlockSpec(memory_space=pl.ANY)
NT = (((1,), (1,)), ((), ()))


def params(**kw):
    return pltpu.CompilerParams(vmem_limit_bytes=VMEM_LIMIT, **kw)


def cost(flops=1000, bytes_accessed=1000):
    return pl.CostEstimate(flops=flops, bytes_accessed=bytes_accessed, transcendentals=0)


def route(decode_slot, pool_index, pool_count, slot_count):
    targets = decode_slot // slot_count
    by_source = targets.reshape(pool_count, slot_count)
    earlier = jnp.tril(jnp.ones((slot_count, slot_count), jnp.int32), -1)
    own = lax.dynamic_slice_in_dim(by_source, pool_index, 1, 0)[0]
    same = (own[:, None] == own[None, :]).astype(jnp.int32)
    placing = own * CAP + jnp.sum(same * earlier, axis=1)
    arriving = (by_source == pool_index).astype(jnp.int32)
    before = jnp.cumsum(arriving, axis=1) - arriving
    cell = (jnp.arange(pool_count)[:, None] * CAP + before).reshape(-1)
    wanted = pool_index * slot_count + jnp.arange(slot_count)
    match = decode_slot[None, :] == wanted[:, None]
    arrival = jnp.sum(jnp.where(match, cell[None, :], 0), axis=1)
    return placing, arrival, match


def pack_queries_kernel(arrival, q_ref, n_ref, out_ref, new_rows, tails):
    steps, slots, heads, width = q_ref.shape
    rows = steps * heads
    blocks = n_ref.shape[2] // 128
    new_rows[...] = n_ref[...].astype(F32)
    tails[...] = jnp.zeros(tails.shape, F32)

    def one(j, carry):
        dest, rank = arrival[j] // CAP, arrival[j] % CAP
        x = q_ref[:, j].astype(F32)
        nope = x[:, :, :NOPE].reshape(rows, NOPE)
        rope = x[:, :, NOPE:].reshape(rows, ROPE)
        rope = jnp.concatenate([rope[: rows // 2], rope[rows // 2 :]], axis=1)
        fresh = jnp.concatenate([new_rows[s, pl.ds(j, 1), :] for s in range(steps)], axis=0)
        body = [fresh[:, 128 * b : 128 * b + 128] for b in range(blocks)]
        last = fresh[:, 128 * blocks :]
        cell = jnp.concatenate([nope, rope] + body, axis=0)
        out_ref[dest, pl.ds(pl.multiple_of(rank * 64, 64), 64), :] = cell.astype(BF16)
        tails[pl.ds(dest * 8 + rank * 2, 2), :] = jnp.concatenate(
            [last[: steps // 2], last[steps // 2 :]], axis=1
        )
        return carry

    lax.fori_loop(0, slots, one, 0)
    out_ref[:, 256:264, :] = tails[...].reshape(out_ref.shape[0], 8, 128).astype(BF16)


def pack_queries(arrival, queries, new_latent, pool_count):
    return pl.pallas_call(
        pack_queries_kernel,
        out_shape=jax.ShapeDtypeStruct((pool_count, 264, 128), BF16),
        in_specs=[SMEM_SPEC, VMEM_SPEC, VMEM_SPEC],
        out_specs=VMEM_SPEC,
        scratch_shapes=[
            pltpu.VMEM(new_latent.shape, F32),
            pltpu.VMEM((pool_count * 8, 128), F32),
        ],
        compiler_params=params(),
        cost_estimate=cost(),
        name="pack_queries",
    )(arrival, queries, new_latent)


def pack_context_kernel(placing, where, p_ref, first_ref, second_ref, buf, sems):
    slots, piece, feature = buf.shape
    blocks = feature // 128
    chunk = slots // sems.shape[0]
    start = pl.multiple_of(where[0] * piece, 16)
    copies = [
        pltpu.make_async_copy(
            p_ref.at[pl.ds(k * chunk, chunk), pl.ds(start, piece), :],
            buf.at[pl.ds(k * chunk, chunk)],
            sems.at[k],
        )
        for k in range(sems.shape[0])
    ]
    for copy in copies:
        copy.start()
    for k, copy in enumerate(copies):
        copy.wait()

        def one(n, carry):
            g = k * chunk + n
            dest, rank = placing[g] // CAP, placing[g] % CAP

            def put(ref, at):
                for b in range(blocks):
                    ref[(*at, pl.ds(b * piece, piece), slice(None))] = buf[
                        g, :, 128 * b : 128 * b + 128
                    ]
                last = buf[g, :, 128 * blocks :].astype(F32)
                last = jnp.concatenate([last[: piece // 2], last[piece // 2 :]], axis=1)
                ref[(*at, pl.ds(blocks * piece, piece // 2), slice(None))] = last.astype(BF16)

            @pl.when(rank < FIRST_RANKS)
            def _():
                put(first_ref, (dest, rank))

            @pl.when(rank >= FIRST_RANKS)
            def _():
                put(second_ref, (dest, rank - FIRST_RANKS))

            return carry

        lax.fori_loop(0, chunk, one, 0)


def pack_context(placing, where, prompt_latent, piece, pool_count):
    slots, _, feature = prompt_latent.shape
    rows = piece * feature // 128
    return pl.pallas_call(
        pack_context_kernel,
        out_shape=(
            jax.ShapeDtypeStruct((pool_count, FIRST_RANKS, rows, 128), BF16),
            jax.ShapeDtypeStruct((pool_count, CAP - FIRST_RANKS, rows, 128), BF16),
        ),
        in_specs=[SMEM_SPEC, SMEM_SPEC, ANY_SPEC],
        out_specs=(VMEM_SPEC, VMEM_SPEC),
        scratch_shapes=[
            pltpu.VMEM((slots, piece, feature), BF16),
            pltpu.SemaphoreType.DMA((4,)),
        ],
        compiler_params=params(),
        cost_estimate=cost(),
        name="pack_context",
    )(placing, where, prompt_latent)


def unpack_piece(packed, row, first_row, length, piece, feature):
    blocks = feature // 128
    parts = [packed[(*row, pl.ds(b * piece, piece), slice(None))] for b in range(blocks)]
    last = packed[(*row, pl.ds(blocks * piece, piece // 2), slice(None))].astype(F32)
    last = jnp.concatenate([last[:, :64], last[:, 64:]], axis=0).astype(BF16)
    whole = jnp.concatenate(parts + [last], axis=1)
    position = first_row + lax.broadcasted_iota(jnp.int32, whole.shape, 0)
    return jnp.where(position < length, whole.astype(F32), 0.0).astype(BF16)


def place_kernel(low, high, keep, arrival, lengths, where, packed, *rest):
    out_ref, inbox, outbox, in_sems, out_sems = rest[-5:]
    slots, piece, feature = out_ref.shape
    first_row = where[0] * piece

    def copy_in(j):
        owner, rank = arrival[j] // CAP, arrival[j] % CAP
        rank = jnp.clip(rank - low, 0, high - low - 1)
        return pltpu.make_async_copy(packed.at[owner, rank], inbox.at[j], in_sems.at[j])

    def copy_out(j):
        return pltpu.make_async_copy(outbox.at[j], out_ref.at[j], out_sems.at[j])

    def each(action):
        def step(j, carry):
            rank = arrival[j] % CAP

            @pl.when((rank >= low) & (rank < high))
            def _():
                action(j)

            return carry

        lax.fori_loop(0, slots, step, 0)

    def work(j):
        copy_in(j).wait()
        outbox[j] = unpack_piece(inbox, (j,), first_row, lengths[j], piece, feature)
        copy_out(j).start()

    each(lambda j: copy_in(j).start())
    each(work)
    each(lambda j: copy_out(j).wait())


def place(low, high, arrival, lengths, where, packed, piece, feature, context=None):
    slots = arrival.shape[0]
    rows = packed.shape[2]
    args = [arrival, lengths, where, packed] + ([] if context is None else [context])
    return pl.pallas_call(
        functools.partial(place_kernel, low, high, context is not None),
        out_shape=jax.ShapeDtypeStruct((slots, piece, feature), BF16),
        in_specs=[SMEM_SPEC] * 3 + [ANY_SPEC] * (len(args) - 3),
        out_specs=ANY_SPEC,
        scratch_shapes=[
            pltpu.VMEM((slots, rows, 128), BF16),
            pltpu.VMEM((slots, piece, feature), BF16),
            pltpu.SemaphoreType.DMA((slots,)),
            pltpu.SemaphoreType.DMA((slots,)),
        ],
        input_output_aliases={} if context is None else {4: 0},
        compiler_params=params(),
        cost_estimate=cost(),
        name="place_context",
    )(*args)


def attention_kernel(
    placing, lengths, where, payload, p_ref, w_uk, w_uv_hbm, w_out_hbm,
    given_ref, kept_ref,
    q_nope, q_rope, acc, fresh, tails, fresh_score, total, w_uv, w_out, head_out, sems,
):
    steps = 4
    heads, latent, nope = w_uk.shape
    group, span, feature = p_ref.shape
    slots = placing.shape[0]
    chunks = latent // 128
    per_step = slots * heads
    many = slots * steps
    scale = 1.0 / math.sqrt(nope + ROPE)
    at = pl.program_id(0)
    copy_uv = pltpu.make_async_copy(w_uv_hbm, w_uv, sems.at[0])
    copy_out = pltpu.make_async_copy(w_out_hbm, w_out, sems.at[1])

    def spread(ref, i, lead=()):
        return jnp.concatenate(
            [
                ref[(*lead, pl.ds(pl.multiple_of(per_step * s + heads * i, 8), heads), slice(None))]
                for s in range(steps)
            ],
            axis=0,
        )

    def collect(ref, i, value, lead=()):
        for s in range(steps):
            ref[(*lead, pl.ds(pl.multiple_of(per_step * s + heads * i, 8), heads), slice(None))] = (
                value[heads * s : heads * s + heads]
            )

    @pl.when(at == 0)
    def _():
        copy_uv.start()
        copy_out.start()
        tails[...] = payload[:, 256:264, :].astype(F32).reshape(tails.shape)

        def one(i, carry):
            dest, rank = placing[i] // CAP, placing[i] % CAP
            cell = payload[dest, pl.ds(pl.multiple_of(rank * 64, 64), 64), :].astype(F32)
            collect(q_nope, i, cell[:32])
            rope = jnp.concatenate([cell[32:48, :64], cell[32:48, 64:]], axis=0)
            collect(q_rope, i, jnp.concatenate([rope, jnp.zeros_like(rope)], axis=1))
            for b in range(chunks):
                fresh[b, pl.ds(steps * i, steps), :] = cell[48 + 4 * b : 52 + 4 * b]
            last = tails[pl.ds(dest * 8 + rank * 2, 2), :]
            last = jnp.concatenate([last[:, :64], last[:, 64:]], axis=0)
            fresh[chunks, pl.ds(steps * i, steps), :] = jnp.concatenate(
                [last, jnp.zeros_like(last)], axis=1
            )
            return carry

        lax.fori_loop(0, slots, one, 0)
        for h in range(heads):
            rows = pl.ds(h, many, stride=heads)
            a = lax.dot_general(
                q_nope[rows, :].astype(BF16), w_uk[h], NT, preferred_element_type=F32
            )
            a = a.astype(BF16).astype(F32)
            for c in range(chunks):
                acc[c, rows, :] = a[:, 128 * c : 128 * c + 128]
        keys = jnp.concatenate([fresh[b] for b in range(chunks + 1)], axis=1).astype(BF16)

        def score(k, carry):
            rows = pl.ds(pl.multiple_of(k * 128, 128), 128)
            q = jnp.concatenate(
                [acc[c, rows, :] for c in range(chunks)] + [q_rope[rows, :]], axis=1
            ).astype(BF16)
            fresh_score[rows, :] = scale * lax.dot_general(
                q, keys, NT, preferred_element_type=F32
            )
            return carry

        lax.fori_loop(0, per_step * steps // 128, score, 0)

    for n in range(group):
        i = at * group + n
        q = jnp.concatenate(
            [spread(acc, i, (c,)) for c in range(chunks)] + [spread(q_rope, i)[:, :ROPE]], axis=1
        ).astype(BF16)
        keys = p_ref[n]
        s_prompt = scale * lax.dot_general(q, keys, NT, preferred_element_type=F32)
        s_fresh = spread(fresh_score, i)
        column = lax.broadcasted_iota(jnp.int32, s_prompt.shape, 1)
        s_prompt = jnp.where(column < lengths[i], s_prompt, FLOOR)
        step_of = lax.broadcasted_iota(jnp.int32, s_fresh.shape, 0) // heads
        column = lax.broadcasted_iota(jnp.int32, s_fresh.shape, 1) - steps * i
        s_fresh = jnp.where((column >= 0) & (column <= step_of), s_fresh, FLOOR)
        peak = jnp.maximum(
            jnp.max(s_prompt, axis=1, keepdims=True), jnp.max(s_fresh, axis=1, keepdims=True)
        )
        w_prompt = jnp.exp(s_prompt - peak)
        w_fresh = jnp.exp(s_fresh - peak)
        sums = jnp.sum(w_prompt, axis=1, keepdims=True) + jnp.sum(w_fresh, axis=1, keepdims=True)
        mixed = jnp.dot(
            w_prompt.astype(BF16), keys[:, :latent], preferred_element_type=F32
        )
        for c in range(chunks):
            collect(acc, i, mixed[:, 128 * c : 128 * c + 128], (c,))
        collect(fresh_score, i, w_fresh)
        collect(total, i, jnp.broadcast_to(sums, s_fresh.shape))

    @pl.when(at == pl.num_programs(0) - 1)
    def _():
        values = jnp.concatenate([fresh[b] for b in range(chunks)], axis=1).astype(BF16)
        copy_uv.wait()
        for h in range(heads):
            rows = pl.ds(h, many, stride=heads)
            mixed = jnp.dot(
                fresh_score[rows, :].astype(BF16), values, preferred_element_type=F32
            )
            mixed = mixed + jnp.concatenate([acc[c, rows, :] for c in range(chunks)], axis=1)
            part = total[rows, :]
            mixed = (mixed / jnp.concatenate([part] * chunks, axis=1)).astype(BF16)
            head_out[:, h * 128 : h * 128 + 128] = jnp.dot(
                mixed, w_uv[h], preferred_element_type=F32
            ).astype(BF16)
        copy_out.wait()
        half = many // 2
        core = where[0] % 2
        mine = head_out[pl.ds(pl.multiple_of(core * half, half), half), :]
        theirs = head_out[pl.ds(pl.multiple_of((1 - core) * half, half), half), :]
        for b in range(w_out.shape[1] // 512):
            at_b = slice(b * 512, b * 512 + 512)
            given_ref[:, at_b] = jnp.dot(
                theirs, w_out[:, at_b], preferred_element_type=F32
            ).astype(BF16)
            kept_ref[:, at_b] = jnp.dot(mine, w_out[:, at_b], preferred_element_type=F32)


def attention(placing, lengths, where, payload, prompt_latent, w_uk, w_uv, w_out, steps):
    slots, span, feature = prompt_latent.shape
    heads, latent, nope = w_uk.shape
    width = w_out.shape[1]
    rows = steps * slots * heads
    half = steps * slots // 2
    chunks = latent // 128

    def whole(x):
        return pl.BlockSpec(x.shape, lambda i: (0,) * x.ndim, pipeline_mode=pl.Buffered(1))

    def whole_out(shape):
        return pl.BlockSpec(shape, lambda i: (0, 0), pipeline_mode=pl.Buffered(1))

    return pl.pallas_call(
        attention_kernel,
        grid=(slots // GROUP,),
        out_shape=(
            jax.ShapeDtypeStruct((half, width), BF16),
            jax.ShapeDtypeStruct((half, width), F32),
        ),
        in_specs=[
            SMEM_SPEC,
            SMEM_SPEC,
            SMEM_SPEC,
            whole(payload),
            pl.BlockSpec((GROUP, span, feature), lambda i: (i, 0, 0)),
            whole(w_uk),
            ANY_SPEC,
            ANY_SPEC,
        ],
        out_specs=(
            pl.BlockSpec((half, width), lambda i: (0, 0)),
            pl.BlockSpec((half, width), lambda i: (0, 0)),
        ),
        scratch_shapes=[
            pltpu.VMEM((rows, 128), F32),
            pltpu.VMEM((rows, 128), F32),
            pltpu.VMEM((chunks, rows, 128), F32),
            pltpu.VMEM((chunks + 1, steps * slots, 128), F32),
            pltpu.VMEM((payload.shape[0] * 8, 128), F32),
            pltpu.VMEM((rows, 128), F32),
            pltpu.VMEM((rows, 128), F32),
            pltpu.VMEM(w_uv.shape, BF16),
            pltpu.VMEM(w_out.shape, BF16),
            pltpu.VMEM((steps * slots, heads * 128), BF16),
            pltpu.SemaphoreType.DMA((2,)),
        ],
        compiler_params=params(dimension_semantics=("arbitrary",)),
        cost_estimate=cost(),
        name="attention",
    )(placing, lengths, where, payload, prompt_latent, w_uk, w_uv, w_out)


def exchange(x):
    return lax.all_to_all(x, "pool", split_axis=0, concat_axis=0, tiled=True)


def body(prompt_latent, prompt_lengths, decode_slot, new_latent, queries, w_uk, w_uv, w_out):
    pool_count = lax.axis_size("pool")
    tp_count = lax.axis_size("tp")
    pool_index = lax.axis_index("pool")
    tp_index = lax.axis_index("tp")
    steps, slots, heads, width = queries.shape
    span, feature = prompt_latent.shape[1:]
    piece = span // tp_count
    out_width = w_out.shape[1]
    cells = pool_count * CAP
    where = tp_index.astype(jnp.int32).reshape(1)
    placing, arrival, match = route(decode_slot, pool_index, pool_count, slots)
    decode_lengths = jnp.sum(jnp.where(match, prompt_lengths[None, :], 0), axis=1)
    own_lengths = lax.dynamic_slice_in_dim(prompt_lengths, pool_index * slots, slots)

    payload = exchange(pack_queries(arrival, queries, new_latent, pool_count))
    first_send, second_send = pack_context(placing, where, prompt_latent, piece, pool_count)
    payload, first_send = lax.optimization_barrier((payload, first_send))
    first = exchange(first_send)

    given, kept = attention(
        placing, own_lengths, where, payload, prompt_latent, w_uk, w_uv, w_out, steps
    )

    core = tp_index % 2
    z = tp_index // 2
    z_count = tp_count // 2
    block = out_width // z_count
    swap = [(i, i ^ 1) for i in range(tp_count)]

    def hop(d):
        return [(i, i ^ (2 * d)) for i in range(tp_count)]

    pair = kept + lax.ppermute(given, "tp", swap).astype(F32)
    mine = lax.dynamic_slice_in_dim(pair, z * block, block, 1)
    pair16 = pair.astype(BF16)
    got = [
        lax.ppermute(
            lax.dynamic_slice_in_dim(pair16, (z ^ d) * block, block, 1), "tp", hop(d)
        )
        for d in range(1, z_count)
    ]
    for part in got:
        mine = mine + part.astype(F32)
    mine = mine.astype(BF16).reshape(steps // 2, slots, block)

    grid_cells = jnp.arange(cells)
    source_row = jnp.sum(
        jnp.where(placing[None, :] == grid_cells[:, None], jnp.arange(slots)[None, :], 0), axis=1
    )
    back = jnp.take(mine, source_row, axis=1).transpose(1, 0, 2)
    back = back.reshape(pool_count, CAP * steps // 2, block)
    back, first = lax.optimization_barrier((back, first))
    back = exchange(back)
    back, second_send = lax.optimization_barrier((back, second_send))
    second = exchange(second_send)
    context = place(0, FIRST_RANKS, arrival, decode_lengths, where, first, piece, feature)

    back = jnp.take(back.reshape(cells, steps // 2, block), arrival, axis=0)
    parts = jnp.stack([back] + [lax.ppermute(back, "tp", hop(d)) for d in range(1, z_count)])
    parts = jnp.take(parts, jnp.arange(z_count) ^ z, axis=0)
    row_half = parts.transpose(1, 2, 0, 3).reshape(slots, steps // 2, out_width)
    other_half = lax.ppermute(row_half, "tp", swap)
    decoded = jnp.concatenate(
        [
            jnp.where(core == 0, row_half, other_half),
            jnp.where(core == 0, other_half, row_half),
        ],
        axis=1,
    )
    context = place(
        FIRST_RANKS, CAP, arrival, decode_lengths, where, second, piece, feature, context
    )
    return decoded, context


def solution(mesh):
    in_specs = (
        P("pool", None, None),
        P(),
        P(),
        P(None, "pool", None),
        P(None, "pool", "tp", None),
        P("tp", None, None),
        P("tp", None, None),
        P("tp", None),
    )
    out_specs = (P("pool", None, None), P("pool", "tp", None))
    return jax.shard_map(body, mesh=mesh, in_specs=in_specs, out_specs=out_specs, check_vma=False)
```

time: 184 us -> 155 us (0.84)
  Pallas kernels: 0 us -> 46.1 us
  waiting for transfers between devices: 54.3 us -> 30.8 us
  matrix products: 22.6 us -> 0 us
  local copies, waits for them, and re-layouts: 51.4 us -> 32.5 us
  other arithmetic: 16.2 us -> 4.28 us
    pallas_call x0 -> x5, Pallas kernels: none -> 46.1 us  [the longest x1 26.9 us: attention(): pl.pallas_call(attention_kernel, grid=(slots // GROUP,), out_shape=(jax.S...]
    unnamed x14 -> x16, local copies, waits for them, and re-layouts: 1.5 us -> 28.2 us
    gather x6 -> x0, local copies, waits for them, and re-layouts: 25.4 us -> none  [the longest x2 18.2 us: body(): jnp.take(own_piece, source_row, axis=0)]
    dot_general x7 -> x0, matrix products: 22.6 us -> none  [the longest x1 10 us: body(): jnp.einsum('rqk,rkc->rqc', w_prompt.astype(jnp.bfloat16), prompt_latent[....]
    all_to_all x4, waiting for transfers between devices: 43.6 us -> 21.9 us  [exchange(): return lax.all_to_all(x, 'pool', split_axis=0, concat_axis=0, tiled=True)]
    dynamic_slice x1 -> x0, local copies, waits for them, and re-layouts: 7.59 us -> none  [body(): lax.dynamic_slice_in_dim(prompt_latent, tp_index * piece, piece, 1)]
    select_n x8 -> x0, other arithmetic: 6.52 us -> none  [the longest x1 4.56 us: body(): jnp.take(own_piece, source_row, axis=0)]
    slice x6 -> x0, local copies, waits for them, and re-layouts: 6.07 us -> none  [the longest x1 3.7 us: body(): sending[:, :FIRST_RANKS]]
  transfers between devices with their start and end apart: 12 -> 12, of which waited for: 8 -> 7; matrix products, arithmetic and copies ran while one was open for 25% -> 15% of each run, Pallas kernels for 0% -> 25%
where the time goes in v2:
time: 155 us; the launch traced here: 153 us
  Pallas kernels  46.1 us (30%)
  starting transfers between devices  38.6 us (25%)
  local copies, waits for them, and re-layouts  32.5 us (21%)
  waiting for transfers between devices  30.8 us (20%)
  other arithmetic  4.28 us (3%)
    unnamed x16, local copies, waits for them, and re-layouts  28.2 us
    pallas_call x1, Pallas kernels, attention(): pl.pallas_call(attention_kernel, grid=(slots // GROUP,), out_shape=(jax.S...  26.9 us
    all_to_all x4, starting transfers between devices, exchange(): return lax.all_to_all(x, 'pool', split_axis=0, concat_axis=0, tiled=True)  24.8 us
    all_to_all x4, waiting for transfers between devices, exchange(): return lax.all_to_all(x, 'pool', split_axis=0, concat_axis=0, tiled=True)  21.9 us
    pallas_call x2, Pallas kernels, place(): pl.pallas_call(functools.partial(place_kernel, low, high, context is not...  10.1 us
    pallas_call x1, Pallas kernels, pack_context(): pl.pallas_call(pack_context_kernel, out_shape=(jax.ShapeDtypeStruct((pool...  4.93 us
    ppermute x3, starting transfers between devices, body(): lax.ppermute(lax.dynamic_slice_in_dim(pair16, (z ^ d) * block, block, 1),...  4.5 us
    ppermute x1, starting transfers between devices, body(): other_half = lax.ppermute(row_half, 'tp', swap)  4.36 us
  transfers between devices with their start and end apart: 12, of which 7 were waited for; matrix products, arithmetic and copies ran while one was open for 15% of the time, Pallas kernels for 25%

profile of v2, /device:TPU:1, one launch (start us, length us, event | category | flops | bytes accessed | tf_op | source)
XLA Modules:
  0.0 153.2 jit_solution(9927650123987028143)
XLA Ops:
  5.4 4.1 %pack_queries.1 = bf16[16,264,128]{2,1,0:T(8,128)(2,1)} custom-call(s32[32]{0:T(128)S(1)} %get-tuple-element.29.arrival, bf16[4,32,8,192]{3,2,1,0:T(8,128)(2,1)S(1)} %copy-done.5, bf16[4,32,576]{2,1,0:T(8,128)(2,1)S(1)} %copy-done.6), custom_call_target="tpu_custom_call" | custom-call | flops 1000 | bytes 1000 | tf_op jit(solution)/shard_map/pack_queries/pallas_call | solution.py:79
  9.5 7.6 %all-to-all-start = ((bf16[16,264,128]{2,1,0:T(8,128)(2,1)}), bf16[16,264,128]{2,1,0:T(8,128)(2,1)S(1)}, u32[]{:S(2)}, u32[]{:S(2)}) async-start(bf16[16,264,128]{2,1,0:T(8,128)(2,1)} %pack_queries.1), calls=%async_computation | async-start | bytes 2162688 | tf_op jit(solution)/shard_map/all_to_all | solution.py:412
  17.1 18.8 %copy.24.p_ref = bf16[32,384,576]{2,1,0:T(8,128)(2,1)} copy(bf16[32,384,576]{1,2,0:T(8,128)(2,1)} %param.8) | data formatting | bytes 28311552 | tf_op args[0]
  36.1 4.9 %pack_context.1 = (bf16[16,3,216,128]{3,2,1,0:T(8,128)(2,1)S(1)}, bf16[16,1,216,128]{3,2,1,0:T(8,128)(2,1)}) custom-call(s32[32]{0:T(128)S(1)} %multiply_add_fusion.placing, s32[1]{0:T(128)} %bitcast.3.where, bf16[32,384,576]{2,1,0:T(8,128)(2,1)} %copy.24.p_ref), custom_call_target="tpu_custom_call" | custom-call | flops 1000 | bytes 1000 | tf_op jit(solution)/shard_map/pack_context/pallas_call | solution.py:141
  41.0 1.5 copy-done.2
  44.4 6.6 %all-to-all-start.1 = ((bf16[16,3,216,128]{3,2,1,0:T(8,128)(2,1)}), bf16[16,3,216,128]{3,2,1,0:T(8,128)(2,1)S(1)}, u32[]{:S(2)}, u32[]{:S(2)}) async-start(bf16[16,3,216,128]{3,2,1,0:T(8,128)(2,1)} %copy-done.2), calls=%async_computation.1 | async-start | bytes 5308416 | tf_op jit(solution)/shard_map/all_to_all | solution.py:412
  51.1 1.2 copy-done.1
  52.3 1.2 copy-done.3
  54.8 26.9 %attention.1 = (bf16[64,2560]{1,0:T(8,128)(2,1)S(1)}, f32[64,2560]{1,0:T(8,128)S(1)}) custom-call(s32[32]{0:T(128)S(1)} %multiply_add_fusion.placing, s32[32]{0:T(128)S(1)} %dynamic_slice.19.lengths, s32[1]{0:T(128)} %bitcast.3.where, bf16[16,264,128]{2,1,0:T(8,128)(2,1)S(1)} %copy-done.1, bf16[32,384,576]{2,1,0:T(8,128)(2,1)} %copy.24.p_ref, ...), custom_call_target="tpu_custom_call" | custom-call | flops 1000 | bytes 1000 | tf_op jit(solution)/shard_map/attention/pallas_call | solution.py:371
  81.7 1.6 %collective-permute-start = (bf16[64,2560]{1,0:T(8,128)(2,1)S(1)}, bf16[64,2560]{1,0:T(8,128)(2,1)S(1)}, u32[]{:S(2)}, u32[]{:S(2)}) collective-permute-start(bf16[64,2560]{1,0:T(8,128)(2,1)S(1)} %get-tuple-element.15), channel_id=1, source_target_pairs={{0,1},{1,0},{2,3},{3,2},{4,5},{5,4},{6,7},{7,6},{8,9},{9,8},{10,11... | collective-permute-start | bytes 983048 | tf_op jit(solution)/shard_map/ppermute | solution.py:448
  83.3 1.2 collective-permute-done
  84.7 3.8 %collective-permute-start.3 = (bf16[64,640]{1,0:T(8,128)(2,1)S(1)}, bf16[64,640]{1,0:T(8,128)(2,1)S(1)}, u32[]{:S(2)}, u32[]{:S(2)}) collective-permute-start(bf16[64,640]{1,0:T(8,128)(2,1)S(1)} %get-tuple-element.35), channel_id=1, source_target_pairs={{0,6},{1,7},{2,4},{3,5},{4,2},{5,3},{6,0},{7,1},{8,14},{9,15},{10,... | collective-permute-start | bytes 245768 | tf_op jit(solution)/shard_map/ppermute | solution.py:452
  89.2 2.5 %collective-permute-done.3 = bf16[64,640]{1,0:T(8,128)(2,1)S(1)} collective-permute-done((bf16[64,640]{1,0:T(8,128)(2,1)S(1)}, bf16[64,640]{1,0:T(8,128)(2,1)S(1)}, u32[]{:S(2)}, u32[]{:S(2)}) %collective-permute-start.3) | collective-permute-done | bytes 81952 | tf_op jit(solution)/shard_map/ppermute | solution.py:452
  91.6 1.7 %collective-permute-done.2 = bf16[64,640]{1,0:T(8,128)(2,1)S(1)} collective-permute-done((bf16[64,640]{1,0:T(8,128)(2,1)S(1)}, bf16[64,640]{1,0:T(8,128)(2,1)S(1)}, u32[]{:S(2)}, u32[]{:S(2)}) %collective-permute-start.2) | collective-permute-done | bytes 81952 | tf_op jit(solution)/shard_map/ppermute | solution.py:452
  95.3 6.9 %all-to-all-start.2 = ((bf16[16,8,640]{2,1,0:T(8,128)(2,1)}), bf16[16,8,640]{2,1,0:T(8,128)(2,1)S(1)}, u32[]{:S(2)}, u32[]{:S(2)}) async-start(bf16[16,8,640]{2,1,0:T(8,128)(2,1)} %reshape.114), calls=%async_computation.2 | async-start | bytes 327680 | tf_op jit(solution)/shard_map/all_to_all | solution.py:412
  102.3 7.0 %all-to-all-done.2 = bf16[16,8,640]{2,1,0:T(8,128)(2,1)S(1)} async-done(((bf16[16,8,640]{2,1,0:T(8,128)(2,1)}), bf16[16,8,640]{2,1,0:T(8,128)(2,1)S(1)}, u32[]{:S(2)}, u32[]{:S(2)}) %all-to-all-start.2) | async-done | bytes 163872 | tf_op jit(solution)/shard_map/all_to_all | solution.py:412
  110.2 2.3 %collective-permute-start.6 = (bf16[32,2,640]{2,1,0:T(2,128)(2,1)S(1)}, bf16[32,2,640]{2,1,0:T(2,128)(2,1)S(1)}, u32[]{:S(2)}, u32[]{:S(2)}) collective-permute-start(bf16[32,2,640]{2,1,0:T(2,128)(2,1)S(1)} %broadcast_select_fusion.3), channel_id=1, source_target_pairs={{0,6},{1,7},{2,4},{3,5},{4,2},{5,3},{6,0},{7,1},{8,14},{9,15},{10,... | collective-permute-start | bytes 245768 | tf_op jit(solution)/shard_map/ppermute | solution.py:474
  114.8 2.5 %collective-permute-done.5 = bf16[32,2,640]{2,1,0:T(2,128)(2,1)S(1)} collective-permute-done((bf16[32,2,640]{2,1,0:T(2,128)(2,1)S(1)}, bf16[32,2,640]{2,1,0:T(2,128)(2,1)S(1)}, u32[]{:S(2)}, u32[]{:S(2)}) %collective-permute-start.5) | collective-permute-done | bytes 81952 | tf_op jit(solution)/shard_map/ppermute | solution.py:474
  118.7 4.4 %collective-permute-start.7 = (bf16[32,2,2560]{2,0,1:T(8,128)(2,1)S(1)}, bf16[32,2,2560]{2,0,1:T(8,128)(2,1)S(1)}, u32[]{:S(2)}, u32[]{:S(2)}) collective-permute-start(bf16[32,2,2560]{2,0,1:T(8,128)(2,1)S(1)} %bitcast.31), channel_id=1, source_target_pairs={{0,1},{1,0},{2,3},{3,2},{4,5},{5,4},{6,7},{7,6},{8,9},{9,8},{10,11... | collective-permute-start | bytes 983048 | tf_op jit(solution)/shard_map/ppermute | solution.py:477
  123.0 7.1 %place_context.2.rest_0_ = bf16[32,48,576]{2,1,0:T(8,128)(2,1)} custom-call(s32[32]{0:T(128)S(1)} %get-tuple-element.29.arrival, s32[32]{0:T(128)S(1)} %get-tuple-element.28.lengths, s32[1]{0:T(128)} %bitcast.3.where, bf16[16,3,216,128]{3,2,1,0:T(8,128)(2,1)S(1)} %all-to-all-done.1.packed), custom_call_target="tpu_custom_call" | custom-call | flops 1000 | bytes 1000 | tf_op jit(solution)/shard_map/place_context/pallas_call | solution.py:208
  130.1 3.6 %all-to-all-start.3 = ((bf16[16,1,216,128]{3,2,1,0:T(8,128)(2,1)}), bf16[16,1,216,128]{3,2,1,0:T(8,128)(2,1)S(1)}, u32[]{:S(2)}, u32[]{:S(2)}) async-start(bf16[16,1,216,128]{3,2,1,0:T(8,128)(2,1)} %get-tuple-element.20), calls=%async_computation.3 | async-start | bytes 1769472 | tf_op jit(solution)/shard_map/all_to_all | solution.py:412
  133.9 1.3 copy.29
  135.3 14.9 %all-to-all-done.3.packed = bf16[16,1,216,128]{3,2,1,0:T(8,128)(2,1)S(1)} async-done(((bf16[16,1,216,128]{3,2,1,0:T(8,128)(2,1)}), bf16[16,1,216,128]{3,2,1,0:T(8,128)(2,1)S(1)}, u32[]{:S(2)}, u32[]{:S(2)}) %all-to-all-start.3) | async-done | bytes 884768 | tf_op jit(solution)/shard_map/all_to_all | solution.py:412
  150.2 3.1 %place_context.3 = bf16[32,48,576]{2,1,0:T(8,128)(2,1)} custom-call(s32[32]{0:T(128)S(1)} %get-tuple-element.29.arrival, s32[32]{0:T(128)S(1)} %get-tuple-element.28.lengths, s32[1]{0:T(128)} %bitcast.3.where, bf16[16,1,216,128]{3,2,1,0:T(8,128)(2,1)S(1)} %all-to-all-done.3.packed, ...), custom_call_target="tpu_custom_call", output_to_operand_aliasing={{}: (4, {})} | custom-call | flops 1000 | bytes 1000 | tf_op jit(solution)/shard_map/place_context/pallas_call | solution.py:208
  (66 shorter events, 15.6 us)
Async XLA Ops:
  3.4 1.0 copy-start.5
  4.5 0.9 copy-start.6
  9.5 33.9 %all-to-all-start = ((bf16[16,264,128]{2,1,0:T(8,128)(2,1)}), bf16[16,264,128]{2,1,0:T(8,128)(2,1)S(1)}, u32[]{:S(2)}, u32[]{:S(2)}) async-start(bf16[16,264,128]{2,1,0:T(8,128)(2,1)} %pack_queries.1), calls=%async_computation | async-start | bytes 2162688 | tf_op jit(solution)/shard_map/all_to_all | solution.py:412
  41.0 1.5 copy-start.2
  43.4 1.0 copy-start
  44.4 50.9 %all-to-all-start.1 = ((bf16[16,3,216,128]{3,2,1,0:T(8,128)(2,1)}), bf16[16,3,216,128]{3,2,1,0:T(8,128)(2,1)S(1)}, u32[]{:S(2)}, u32[]{:S(2)}) async-start(bf16[16,3,216,128]{3,2,1,0:T(8,128)(2,1)} %copy-done.2), calls=%async_computation.1 | async-start | bytes 5308416 | tf_op jit(solution)/shard_map/all_to_all | solution.py:412
  51.1 1.2 copy-start.1
  52.3 1.2 copy-start.3
  53.5 1.2 copy-start.4
  81.7 2.9 %collective-permute-start = (bf16[64,2560]{1,0:T(8,128)(2,1)S(1)}, bf16[64,2560]{1,0:T(8,128)(2,1)S(1)}, u32[]{:S(2)}, u32[]{:S(2)}) collective-permute-start(bf16[64,2560]{1,0:T(8,128)(2,1)S(1)} %get-tuple-element.15), channel_id=1, source_target_pairs={{0,1},{1,0},{2,3},{3,2},{4,5},{5,4},{6,7},{7,6},{8,9},{9,8},{10,11... | collective-permute-start | bytes 983048 | tf_op jit(solution)/shard_map/ppermute | solution.py:448
  84.7 7.0 %collective-permute-start.3 = (bf16[64,640]{1,0:T(8,128)(2,1)S(1)}, bf16[64,640]{1,0:T(8,128)(2,1)S(1)}, u32[]{:S(2)}, u32[]{:S(2)}) collective-permute-start(bf16[64,640]{1,0:T(8,128)(2,1)S(1)} %get-tuple-element.35), channel_id=1, source_target_pairs={{0,6},{1,7},{2,4},{3,5},{4,2},{5,3},{6,0},{7,1},{8,14},{9,15},{10,... | collective-permute-start | bytes 245768 | tf_op jit(solution)/shard_map/ppermute | solution.py:452
  88.5 4.8 %collective-permute-start.2 = (bf16[64,640]{1,0:T(8,128)(2,1)S(1)}, bf16[64,640]{1,0:T(8,128)(2,1)S(1)}, u32[]{:S(2)}, u32[]{:S(2)}) collective-permute-start(bf16[64,640]{1,0:T(8,128)(2,1)S(1)} %get-tuple-element.36), channel_id=1, source_target_pairs={{0,4},{1,5},{2,6},{3,7},{4,0},{5,1},{6,2},{7,3},{8,12},{9,13},{10,... | collective-permute-start | bytes 245768 | tf_op jit(solution)/shard_map/ppermute | solution.py:452
  88.5 4.8 %collective-permute-start.1 = (bf16[64,640]{1,0:T(8,128)(2,1)S(1)}, bf16[64,640]{1,0:T(8,128)(2,1)S(1)}, u32[]{:S(2)}, u32[]{:S(2)}) collective-permute-start(bf16[64,640]{1,0:T(8,128)(2,1)S(1)} %get-tuple-element.34), channel_id=1, source_target_pairs={{0,2},{1,3},{2,0},{3,1},{4,6},{5,7},{6,4},{7,5},{8,10},{9,11},{10,... | collective-permute-start | bytes 245768 | tf_op jit(solution)/shard_map/ppermute | solution.py:452
  95.3 14.0 %all-to-all-start.2 = ((bf16[16,8,640]{2,1,0:T(8,128)(2,1)}), bf16[16,8,640]{2,1,0:T(8,128)(2,1)S(1)}, u32[]{:S(2)}, u32[]{:S(2)}) async-start(bf16[16,8,640]{2,1,0:T(8,128)(2,1)} %reshape.114), calls=%async_computation.2 | async-start | bytes 327680 | tf_op jit(solution)/shard_map/all_to_all | solution.py:412
  110.2 4.6 %collective-permute-start.6 = (bf16[32,2,640]{2,1,0:T(2,128)(2,1)S(1)}, bf16[32,2,640]{2,1,0:T(2,128)(2,1)S(1)}, u32[]{:S(2)}, u32[]{:S(2)}) collective-permute-start(bf16[32,2,640]{2,1,0:T(2,128)(2,1)S(1)} %broadcast_select_fusion.3), channel_id=1, source_target_pairs={{0,6},{1,7},{2,4},{3,5},{4,2},{5,3},{6,0},{7,1},{8,14},{9,15},{10,... | collective-permute-start | bytes 245768 | tf_op jit(solution)/shard_map/ppermute | solution.py:474
  112.5 4.8 %collective-permute-start.5 = (bf16[32,2,640]{2,1,0:T(2,128)(2,1)S(1)}, bf16[32,2,640]{2,1,0:T(2,128)(2,1)S(1)}, u32[]{:S(2)}, u32[]{:S(2)}) collective-permute-start(bf16[32,2,640]{2,1,0:T(2,128)(2,1)S(1)} %broadcast_select_fusion.3), channel_id=1, source_target_pairs={{0,4},{1,5},{2,6},{3,7},{4,0},{5,1},{6,2},{7,3},{8,12},{9,13},{10,... | collective-permute-start | bytes 245768 | tf_op jit(solution)/shard_map/ppermute | solution.py:474
  113.0 4.3 %collective-permute-start.4 = (bf16[32,2,640]{2,1,0:T(2,128)(2,1)S(1)}, bf16[32,2,640]{2,1,0:T(2,128)(2,1)S(1)}, u32[]{:S(2)}, u32[]{:S(2)}) collective-permute-start(bf16[32,2,640]{2,1,0:T(2,128)(2,1)S(1)} %broadcast_select_fusion.3), channel_id=1, source_target_pairs={{0,2},{1,3},{2,0},{3,1},{4,6},{5,7},{6,4},{7,5},{8,10},{9,11},{10,... | collective-permute-start | bytes 245768 | tf_op jit(solution)/shard_map/ppermute | solution.py:474
  118.7 15.1 %collective-permute-start.7 = (bf16[32,2,2560]{2,0,1:T(8,128)(2,1)S(1)}, bf16[32,2,2560]{2,0,1:T(8,128)(2,1)S(1)}, u32[]{:S(2)}, u32[]{:S(2)}) collective-permute-start(bf16[32,2,2560]{2,0,1:T(8,128)(2,1)S(1)} %bitcast.31), channel_id=1, source_target_pairs={{0,1},{1,0},{2,3},{3,2},{4,5},{5,4},{6,7},{7,6},{8,9},{9,8},{10,11... | collective-permute-start | bytes 983048 | tf_op jit(solution)/shard_map/ppermute | solution.py:477
  130.1 20.0 %all-to-all-start.3 = ((bf16[16,1,216,128]{3,2,1,0:T(8,128)(2,1)}), bf16[16,1,216,128]{3,2,1,0:T(8,128)(2,1)S(1)}, u32[]{:S(2)}, u32[]{:S(2)}) async-start(bf16[16,1,216,128]{3,2,1,0:T(8,128)(2,1)} %get-tuple-element.20), calls=%async_computation.3 | async-start | bytes 1769472 | tf_op jit(solution)/shard_map/all_to_all | solution.py:412

commit v3 on v2

--- a/solution.py
+++ b/solution.py
@@ -12,12 +12,12 @@
 NOPE = 128
 CAP = 4
 FIRST_RANKS = 3
-GROUP = 2
+GROUP = 4
 FLOOR = -1e30
 BF16 = jnp.bfloat16
 F32 = jnp.float32
 
-VMEM_LIMIT = 48 * 1024 * 1024
+VMEM_LIMIT = 60 * 1024 * 1024
 SMEM_SPEC = pl.BlockSpec(memory_space=pltpu.SMEM)
 VMEM_SPEC = pl.BlockSpec(memory_space=pltpu.VMEM)
 ANY_SPEC = pl.BlockSpec(memory_space=pl.ANY)
@@ -92,13 +92,15 @@
 
 
 def pack_context_kernel(placing, where, p_ref, first_ref, second_ref, buf, sems):
-    slots, piece, feature = buf.shape
+    slots, feature, window = buf.shape
     blocks = feature // 128
+    piece = first_ref.shape[2] * 128 // feature
     chunk = slots // sems.shape[0]
-    start = pl.multiple_of(where[0] * piece, 16)
+    row = where[0] * piece
+    start = pl.multiple_of(jnp.where(row + piece > window, p_ref.shape[2] - window, 0), 128)
     copies = [
         pltpu.make_async_copy(
-            p_ref.at[pl.ds(k * chunk, chunk), pl.ds(start, piece), :],
+            p_ref.at[pl.ds(k * chunk, chunk), :, pl.ds(start, window)],
             buf.at[pl.ds(k * chunk, chunk)],
             sems.at[k],
         )
@@ -106,37 +108,39 @@
     ]
     for copy in copies:
         copy.start()
+    pick = lax.broadcasted_iota(jnp.int32, (piece, window), 1) - (
+        row - start + lax.broadcasted_iota(jnp.int32, (piece, window), 0)
+    )
+    pick = jnp.where(pick == 0, 1.0, 0.0).astype(BF16)
+
     for k, copy in enumerate(copies):
         copy.wait()
 
         def one(n, carry):
             g = k * chunk + n
             dest, rank = placing[g] // CAP, placing[g] % CAP
-
-            def put(ref, at):
-                for b in range(blocks):
-                    ref[(*at, pl.ds(b * piece, piece), slice(None))] = buf[
-                        g, :, 128 * b : 128 * b + 128
-                    ]
-                last = buf[g, :, 128 * blocks :].astype(F32)
-                last = jnp.concatenate([last[: piece // 2], last[piece // 2 :]], axis=1)
-                ref[(*at, pl.ds(blocks * piece, piece // 2), slice(None))] = last.astype(BF16)
+            turned = lax.dot_general(pick, buf[g], NT, preferred_element_type=F32)
+            last = turned[:, 128 * blocks :]
+            last = jnp.concatenate([last[: piece // 2], last[piece // 2 :]], axis=1)
+            cell = jnp.concatenate(
+                [turned[:, 128 * b : 128 * b + 128] for b in range(blocks)] + [last], axis=0
+            ).astype(BF16)
 
             @pl.when(rank < FIRST_RANKS)
             def _():
-                put(first_ref, (dest, rank))
+                first_ref[dest, rank] = cell
 
             @pl.when(rank >= FIRST_RANKS)
             def _():
-                put(second_ref, (dest, rank - FIRST_RANKS))
+                second_ref[dest, rank - FIRST_RANKS] = cell
 
             return carry
 
-        lax.fori_loop(0, chunk, one, 0)
+        lax.fori_loop(0, chunk, one, 0, unroll=2)
 
 
 def pack_context(placing, where, prompt_latent, piece, pool_count):
-    slots, _, feature = prompt_latent.shape
+    slots, feature, _ = prompt_latent.shape
     rows = piece * feature // 128
     return pl.pallas_call(
         pack_context_kernel,
@@ -147,7 +151,7 @@
         in_specs=[SMEM_SPEC, SMEM_SPEC, ANY_SPEC],
         out_specs=(VMEM_SPEC, VMEM_SPEC),
         scratch_shapes=[
-            pltpu.VMEM((slots, piece, feature), BF16),
+            pltpu.VMEM((slots, feature, 256), BF16),
             pltpu.SemaphoreType.DMA((4,)),
         ],
         compiler_params=params(),
@@ -224,21 +228,33 @@
 
 
 def attention_kernel(
-    placing, lengths, where, payload, p_ref, w_uk, w_uv_hbm, w_out_hbm,
+    placing, lengths, where, payload_hbm, p_hbm, w_uk_hbm, w_uv_hbm, w_out_hbm,
     given_ref, kept_ref,
-    q_nope, q_rope, acc, fresh, tails, fresh_score, total, w_uv, w_out, head_out, sems,
+    payload, prompt, w_uk, w_uv, w_out,
+    q_nope, q_rope, acc, fresh, tails, fresh_score, total, head_out, sems,
 ):
     steps = 4
     heads, latent, nope = w_uk.shape
-    group, span, feature = p_ref.shape
-    slots = placing.shape[0]
+    slots, feature, span = prompt.shape
     chunks = latent // 128
     per_step = slots * heads
     many = slots * steps
     scale = 1.0 / math.sqrt(nope + ROPE)
-    at = pl.program_id(0)
-    copy_uv = pltpu.make_async_copy(w_uv_hbm, w_uv, sems.at[0])
-    copy_out = pltpu.make_async_copy(w_out_hbm, w_out, sems.at[1])
+    copy_payload = pltpu.make_async_copy(payload_hbm, payload, sems.at[0])
+    copy_uk = pltpu.make_async_copy(w_uk_hbm, w_uk, sems.at[1])
+    copy_uv = pltpu.make_async_copy(w_uv_hbm, w_uv, sems.at[2])
+    copy_out = pltpu.make_async_copy(w_out_hbm, w_out, sems.at[3])
+
+    def copy_prompt(k):
+        part = pl.ds(k * GROUP, GROUP)
+        return pltpu.make_async_copy(p_hbm.at[part], prompt.at[part], sems.at[4 + k])
+
+    copy_payload.start()
+    copy_uk.start()
+    for k in range(slots // GROUP):
+        copy_prompt(k).start()
+    copy_uv.start()
+    copy_out.start()
 
     def spread(ref, i, lead=()):
         return jnp.concatenate(
@@ -255,57 +271,51 @@
                 value[heads * s : heads * s + heads]
             )
 
-    @pl.when(at == 0)
-    def _():
-        copy_uv.start()
-        copy_out.start()
-        tails[...] = payload[:, 256:264, :].astype(F32).reshape(tails.shape)
-
-        def one(i, carry):
-            dest, rank = placing[i] // CAP, placing[i] % CAP
-            cell = payload[dest, pl.ds(pl.multiple_of(rank * 64, 64), 64), :].astype(F32)
-            collect(q_nope, i, cell[:32])
-            rope = jnp.concatenate([cell[32:48, :64], cell[32:48, 64:]], axis=0)
-            collect(q_rope, i, jnp.concatenate([rope, jnp.zeros_like(rope)], axis=1))
-            for b in range(chunks):
-                fresh[b, pl.ds(steps * i, steps), :] = cell[48 + 4 * b : 52 + 4 * b]
-            last = tails[pl.ds(dest * 8 + rank * 2, 2), :]
-            last = jnp.concatenate([last[:, :64], last[:, 64:]], axis=0)
-            fresh[chunks, pl.ds(steps * i, steps), :] = jnp.concatenate(
-                [last, jnp.zeros_like(last)], axis=1
-            )
-            return carry
-
-        lax.fori_loop(0, slots, one, 0)
-        for h in range(heads):
-            rows = pl.ds(h, many, stride=heads)
-            a = lax.dot_general(
-                q_nope[rows, :].astype(BF16), w_uk[h], NT, preferred_element_type=F32
-            )
-            a = a.astype(BF16).astype(F32)
-            for c in range(chunks):
-                acc[c, rows, :] = a[:, 128 * c : 128 * c + 128]
-        keys = jnp.concatenate([fresh[b] for b in range(chunks + 1)], axis=1).astype(BF16)
-
-        def score(k, carry):
-            rows = pl.ds(pl.multiple_of(k * 128, 128), 128)
-            q = jnp.concatenate(
-                [acc[c, rows, :] for c in range(chunks)] + [q_rope[rows, :]], axis=1
-            ).astype(BF16)
-            fresh_score[rows, :] = scale * lax.dot_general(
-                q, keys, NT, preferred_element_type=F32
-            )
-            return carry
-
-        lax.fori_loop(0, per_step * steps // 128, score, 0)
-
-    for n in range(group):
-        i = at * group + n
+    copy_payload.wait()
+    tails[...] = payload[:, 256:264, :].astype(F32).reshape(tails.shape)
+
+    def unpack(i, carry):
+        dest, rank = placing[i] // CAP, placing[i] % CAP
+        cell = payload[dest, pl.ds(pl.multiple_of(rank * 64, 64), 64), :].astype(F32)
+        collect(q_nope, i, cell[:32])
+        rope = jnp.concatenate([cell[32:48, :64], cell[32:48, 64:]], axis=0)
+        collect(q_rope, i, jnp.concatenate([rope, jnp.zeros_like(rope)], axis=1))
+        for b in range(chunks):
+            fresh[b, pl.ds(steps * i, steps), :] = cell[48 + 4 * b : 52 + 4 * b]
+        last = tails[pl.ds(dest * 8 + rank * 2, 2), :]
+        last = jnp.concatenate([last[:, :64], last[:, 64:]], axis=0)
+        fresh[chunks, pl.ds(steps * i, steps), :] = jnp.concatenate(
+            [last, jnp.zeros_like(last)], axis=1
+        )
+        return carry
+
+    lax.fori_loop(0, slots, unpack, 0, unroll=4)
+    copy_uk.wait()
+    for h in range(heads):
+        rows = pl.ds(h, many, stride=heads)
+        a = lax.dot_general(
+            q_nope[rows, :].astype(BF16), w_uk[h], NT, preferred_element_type=F32
+        )
+        a = a.astype(BF16).astype(F32)
+        for c in range(chunks):
+            acc[c, rows, :] = a[:, 128 * c : 128 * c + 128]
+    keys = jnp.concatenate([fresh[b] for b in range(chunks + 1)], axis=1).astype(BF16)
+
+    def score(k, carry):
+        rows = pl.ds(pl.multiple_of(k * 128, 128), 128)
+        q = jnp.concatenate(
+            [acc[c, rows, :] for c in range(chunks)] + [q_rope[rows, :]], axis=1
+        ).astype(BF16)
+        fresh_score[rows, :] = scale * lax.dot_general(q, keys, NT, preferred_element_type=F32)
+        return carry
+
+    lax.fori_loop(0, per_step * steps // 128, score, 0)
+
+    def one(i):
         q = jnp.concatenate(
             [spread(acc, i, (c,)) for c in range(chunks)] + [spread(q_rope, i)[:, :ROPE]], axis=1
         ).astype(BF16)
-        keys = p_ref[n]
-        s_prompt = scale * lax.dot_general(q, keys, NT, preferred_element_type=F32)
+        s_prompt = scale * jnp.dot(q, prompt[i], preferred_element_type=F32)
         s_fresh = spread(fresh_score, i)
         column = lax.broadcasted_iota(jnp.int32, s_prompt.shape, 1)
         s_prompt = jnp.where(column < lengths[i], s_prompt, FLOOR)
@@ -318,78 +328,67 @@
         w_prompt = jnp.exp(s_prompt - peak)
         w_fresh = jnp.exp(s_fresh - peak)
         sums = jnp.sum(w_prompt, axis=1, keepdims=True) + jnp.sum(w_fresh, axis=1, keepdims=True)
-        mixed = jnp.dot(
-            w_prompt.astype(BF16), keys[:, :latent], preferred_element_type=F32
+        mixed = lax.dot_general(
+            w_prompt.astype(BF16), prompt[i, :latent], NT, preferred_element_type=F32
         )
         for c in range(chunks):
             collect(acc, i, mixed[:, 128 * c : 128 * c + 128], (c,))
         collect(fresh_score, i, w_fresh)
         collect(total, i, jnp.broadcast_to(sums, s_fresh.shape))
 
-    @pl.when(at == pl.num_programs(0) - 1)
-    def _():
-        values = jnp.concatenate([fresh[b] for b in range(chunks)], axis=1).astype(BF16)
-        copy_uv.wait()
-        for h in range(heads):
-            rows = pl.ds(h, many, stride=heads)
-            mixed = jnp.dot(
-                fresh_score[rows, :].astype(BF16), values, preferred_element_type=F32
-            )
-            mixed = mixed + jnp.concatenate([acc[c, rows, :] for c in range(chunks)], axis=1)
-            part = total[rows, :]
-            mixed = (mixed / jnp.concatenate([part] * chunks, axis=1)).astype(BF16)
-            head_out[:, h * 128 : h * 128 + 128] = jnp.dot(
-                mixed, w_uv[h], preferred_element_type=F32
-            ).astype(BF16)
-        copy_out.wait()
-        half = many // 2
-        core = where[0] % 2
-        mine = head_out[pl.ds(pl.multiple_of(core * half, half), half), :]
-        theirs = head_out[pl.ds(pl.multiple_of((1 - core) * half, half), half), :]
-        for b in range(w_out.shape[1] // 512):
-            at_b = slice(b * 512, b * 512 + 512)
-            given_ref[:, at_b] = jnp.dot(
-                theirs, w_out[:, at_b], preferred_element_type=F32
-            ).astype(BF16)
-            kept_ref[:, at_b] = jnp.dot(mine, w_out[:, at_b], preferred_element_type=F32)
+    def attend(k, carry):
+        copy_prompt(k).wait()
+        for n in range(GROUP):
+            one(k * GROUP + n)
+        return carry
+
+    lax.fori_loop(0, slots // GROUP, attend, 0)
+
+    values = jnp.concatenate([fresh[b] for b in range(chunks)], axis=1).astype(BF16)
+    copy_uv.wait()
+    for h in range(heads):
+        rows = pl.ds(h, many, stride=heads)
+        mixed = jnp.dot(fresh_score[rows, :].astype(BF16), values, preferred_element_type=F32)
+        mixed = mixed + jnp.concatenate([acc[c, rows, :] for c in range(chunks)], axis=1)
+        part = total[rows, :]
+        mixed = (mixed / jnp.concatenate([part] * chunks, axis=1)).astype(BF16)
+        head_out[:, h * 128 : h * 128 + 128] = jnp.dot(
+            mixed, w_uv[h], preferred_element_type=F32
+        ).astype(BF16)
+    copy_out.wait()
+    half = many // 2
+    core = where[0] % 2
+    mine = head_out[pl.ds(pl.multiple_of(core * half, half), half), :]
+    theirs = head_out[pl.ds(pl.multiple_of((1 - core) * half, half), half), :]
+    for b in range(w_out.shape[1] // 512):
+        at_b = slice(b * 512, b * 512 + 512)
+        given_ref[:, at_b] = jnp.dot(theirs, w_out[:, at_b], preferred_element_type=F32).astype(
+            BF16
+        )
+        kept_ref[:, at_b] = jnp.dot(mine, w_out[:, at_b], preferred_element_type=F32)
 
 
 def attention(placing, lengths, where, payload, prompt_latent, w_uk, w_uv, w_out, steps):
-    slots, span, feature = prompt_latent.shape
+    slots, feature, span = prompt_latent.shape
     heads, latent, nope = w_uk.shape
     width = w_out.shape[1]
     rows = steps * slots * heads
     half = steps * slots // 2
     chunks = latent // 128
-
-    def whole(x):
-        return pl.BlockSpec(x.shape, lambda i: (0,) * x.ndim, pipeline_mode=pl.Buffered(1))
-
-    def whole_out(shape):
-        return pl.BlockSpec(shape, lambda i: (0, 0), pipeline_mode=pl.Buffered(1))
-
     return pl.pallas_call(
         attention_kernel,
-        grid=(slots // GROUP,),
         out_shape=(
             jax.ShapeDtypeStruct((half, width), BF16),
             jax.ShapeDtypeStruct((half, width), F32),
         ),
-        in_specs=[
-            SMEM_SPEC,
-            SMEM_SPEC,
-            SMEM_SPEC,
-            whole(payload),
-            pl.BlockSpec((GROUP, span, feature), lambda i: (i, 0, 0)),
-            whole(w_uk),
-            ANY_SPEC,
-            ANY_SPEC,
-        ],
-        out_specs=(
-            pl.BlockSpec((half, width), lambda i: (0, 0)),
-            pl.BlockSpec((half, width), lambda i: (0, 0)),
-        ),
+        in_specs=[SMEM_SPEC] * 3 + [ANY_SPEC] * 5,
+        out_specs=(VMEM_SPEC, VMEM_SPEC),
         scratch_shapes=[
+            pltpu.VMEM(payload.shape, BF16),
+            pltpu.VMEM(prompt_latent.shape, BF16),
+            pltpu.VMEM(w_uk.shape, BF16),
+            pltpu.VMEM(w_uv.shape, BF16),
+            pltpu.VMEM(w_out.shape, BF16),
             pltpu.VMEM((rows, 128), F32),
             pltpu.VMEM((rows, 128), F32),
             pltpu.VMEM((chunks, rows, 128), F32),
@@ -397,12 +396,10 @@
             pltpu.VMEM((payload.shape[0] * 8, 128), F32),
             pltpu.VMEM((rows, 128), F32),
             pltpu.VMEM((rows, 128), F32),
-            pltpu.VMEM(w_uv.shape, BF16),
-            pltpu.VMEM(w_out.shape, BF16),
             pltpu.VMEM((steps * slots, heads * 128), BF16),
-            pltpu.SemaphoreType.DMA((2,)),
+            pltpu.SemaphoreType.DMA((4 + slots // GROUP,)),
         ],
-        compiler_params=params(dimension_semantics=("arbitrary",)),
+        compiler_params=params(),
         cost_estimate=cost(),
         name="attention",
     )(placing, lengths, where, payload, prompt_latent, w_uk, w_uv, w_out)
@@ -417,6 +414,7 @@
     tp_count = lax.axis_size("tp")
     pool_index = lax.axis_index("pool")
     tp_index = lax.axis_index("tp")
+    latent_t = prompt_latent.transpose(0, 2, 1)
     steps, slots, heads, width = queries.shape
     span, feature = prompt_latent.shape[1:]
     piece = span // tp_count
@@ -428,12 +426,12 @@
     own_lengths = lax.dynamic_slice_in_dim(prompt_lengths, pool_index * slots, slots)
 
     payload = exchange(pack_queries(arrival, queries, new_latent, pool_count))
-    first_send, second_send = pack_context(placing, where, prompt_latent, piece, pool_count)
+    first_send, second_send = pack_context(placing, where, latent_t, piece, pool_count)
     payload, first_send = lax.optimization_barrier((payload, first_send))
     first = exchange(first_send)
 
     given, kept = attention(
-        placing, own_lengths, where, payload, prompt_latent, w_uk, w_uv, w_out, steps
+        placing, own_lengths, where, payload, latent_t, w_uk, w_uv, w_out, steps
     )
 
     core = tp_index % 2

time: 155 us -> 135 us (0.87)
  local copies, waits for them, and re-layouts: 32.5 us -> 8.11 us
  other arithmetic: 4.28 us -> 6.5 us
    unnamed x16 -> x9, local copies, waits for them, and re-layouts: 28.2 us -> 3.26 us
    pallas_call x1, Pallas kernels: 4.93 us -> 13.3 us  [pack_context(): pl.pallas_call(pack_context_kernel, out_shape=(jax.ShapeDtypeStruct((pool...]
    pallas_call x1, Pallas kernels: 26.9 us -> 21.3 us  [attention(): pl.pallas_call(attention_kernel, out_shape=(jax.ShapeDtypeStruct((half, w...]
    pallas_call x2, Pallas kernels: 10.1 us -> 8.21 us  [place(): pl.pallas_call(functools.partial(place_kernel, low, high, context is not...]
    ppermute x3, waiting for transfers between devices: 4.12 us -> 5.88 us  [body(): lax.ppermute(lax.dynamic_slice_in_dim(pair16, (z ^ d) * block, block, 1),...]
  transfers between devices with their start and end apart: 12 -> 12, of which waited for: 7 -> 8; matrix products, arithmetic and copies ran while one was open for 15% -> 5% of each run, Pallas kernels for 25% -> 30%
where the time goes in v3:
time: 135 us; the launch traced here: 134 us
  Pallas kernels  47.4 us (35%)
  starting transfers between devices  38.6 us (29%)
  waiting for transfers between devices  32.2 us (24%)
  local copies, waits for them, and re-layouts  8.11 us (6%)
  other arithmetic  6.5 us (5%)
    all_to_all x4, starting transfers between devices, exchange(): return lax.all_to_all(x, 'pool', split_axis=0, concat_axis=0, tiled=True)  24 us
    all_to_all x4, waiting for transfers between devices, exchange(): return lax.all_to_all(x, 'pool', split_axis=0, concat_axis=0, tiled=True)  22.6 us
    pallas_call x1, Pallas kernels, attention(): pl.pallas_call(attention_kernel, out_shape=(jax.ShapeDtypeStruct((half, w...  21.3 us
    pallas_call x1, Pallas kernels, pack_context(): pl.pallas_call(pack_context_kernel, out_shape=(jax.ShapeDtypeStruct((pool...  13.3 us
    pallas_call x2, Pallas kernels, place(): pl.pallas_call(functools.partial(place_kernel, low, high, context is not...  8.21 us
    ppermute x3, waiting for transfers between devices, body(): lax.ppermute(lax.dynamic_slice_in_dim(pair16, (z ^ d) * block, block, 1),...  5.88 us
    ppermute x3, starting transfers between devices, body(): lax.ppermute(lax.dynamic_slice_in_dim(pair16, (z ^ d) * block, block, 1),...  5.02 us
    pallas_call x1, Pallas kernels, pack_queries(): pl.pallas_call(pack_queries_kernel, out_shape=jax.ShapeDtypeStruct((pool_...  4.64 us
  transfers between devices with their start and end apart: 12, of which 8 were waited for; matrix products, arithmetic and copies ran while one was open for 5% of the time, Pallas kernels for 30%

profile of v3, /device:TPU:1, one launch (start us, length us, event | category | flops | bytes accessed | tf_op | source)
XLA Modules:
  0.0 133.8 jit_solution(8827862019556233729)
XLA Ops:
  2.5 1.4 %fusion.1 = (s32[32]{0:T(128)}, s32[32]{0:T(128)}) fusion(s32[512]{0:T(512)} %param.9, s32[512]{0:T(512)} %param.10, s32[32]{0:T(128)S(1)} %iota_add_fusion.1, s32[512]{0:T(512)S(1)} %subtract_add_fusion), kind=kLoop, calls=%fused_computation.16 | loop fusion | flops 81856 | bytes 6528 | tf_op jit(solution)/shard_map/reduce_sum | solution.py:425
  4.0 4.6 %pack_queries.1 = bf16[16,264,128]{2,1,0:T(8,128)(2,1)} custom-call(s32[32]{0:T(128)} %get-tuple-element.29.arrival, bf16[4,32,8,192]{3,2,1,0:T(8,128)(2,1)} %q_ref.1, bf16[4,32,576]{2,1,0:T(8,128)(2,1)} %n_ref.1), custom_call_target="tpu_custom_call" | custom-call | flops 1000 | bytes 1000 | tf_op jit(solution)/shard_map/pack_queries/pallas_call | solution.py:79
  8.6 7.6 %all-to-all-start = ((bf16[16,264,128]{2,1,0:T(8,128)(2,1)}), bf16[16,264,128]{2,1,0:T(8,128)(2,1)S(1)}, u32[]{:S(2)}, u32[]{:S(2)}) async-start(bf16[16,264,128]{2,1,0:T(8,128)(2,1)} %pack_queries.1), calls=%async_computation | async-start | bytes 2162688 | tf_op jit(solution)/shard_map/all_to_all | solution.py:409
  17.0 13.3 %pack_context.1 = (bf16[16,3,216,128]{3,2,1,0:T(8,128)(2,1)}, bf16[16,1,216,128]{3,2,1,0:T(8,128)(2,1)}) custom-call(s32[32]{0:T(128)} %multiply_add_fusion.placing, s32[1]{0:T(128)} %bitcast.3.where, bf16[32,576,384]{2,1,0:T(8,128)(2,1)} %bitcast.32), custom_call_target="tpu_custom_call" | custom-call | flops 1000 | bytes 1000 | tf_op jit(solution)/shard_map/pack_context/pallas_call | solution.py:145
  30.3 1.3 dynamic_slice.19.lengths
  33.5 5.9 %all-to-all-start.1 = ((bf16[16,3,216,128]{3,2,1,0:T(8,128)(2,1)}), bf16[16,3,216,128]{3,2,1,0:T(8,128)(2,1)S(1)}, u32[]{:S(2)}, u32[]{:S(2)}) async-start(bf16[16,3,216,128]{3,2,1,0:T(8,128)(2,1)} %get-tuple-element.16), calls=%async_computation.1 | async-start | bytes 5308416 | tf_op jit(solution)/shard_map/all_to_all | solution.py:409
  39.5 21.3 %attention.1 = (bf16[64,2560]{1,0:T(8,128)(2,1)}, f32[64,2560]{1,0:T(8,128)}) custom-call(s32[32]{0:T(128)} %multiply_add_fusion.placing, s32[32]{0:T(128)} %dynamic_slice.19.lengths, s32[1]{0:T(128)} %bitcast.3.where, bf16[16,264,128]{2,1,0:T(8,128)(2,1)} %copy-done.1, bf16[32,576,384]{2,1,0:T(8,128)(2,1)} %bitcast.33, bf16[8,512,128]{2,1,0:T(8,128)(2,1)} %w_uk_hbm.1, ...), custom_call_target="tpu_custom_call" | custom-call | flops 1000 | bytes 1000 | tf_op jit(solution)/shard_map/attention/pallas_call | solution.py:378
  60.8 1.6 %collective-permute-start = (bf16[64,2560]{1,0:T(8,128)(2,1)}, bf16[64,2560]{1,0:T(8,128)(2,1)S(1)}, u32[]{:S(2)}, u32[]{:S(2)}) collective-permute-start(bf16[64,2560]{1,0:T(8,128)(2,1)} %get-tuple-element.15), channel_id=1, source_target_pairs={{0,1},{1,0},{2,3},{3,2},{4,5},{5,4},{6,7},{7,6},{8,9},{9,8},{10,11... | collective-permute-start | bytes 983048 | tf_op jit(solution)/shard_map/ppermute | solution.py:446
  62.4 1.5 %collective-permute-done = bf16[64,2560]{1,0:T(8,128)(2,1)S(1)} collective-permute-done((bf16[64,2560]{1,0:T(8,128)(2,1)}, bf16[64,2560]{1,0:T(8,128)(2,1)S(1)}, u32[]{:S(2)}, u32[]{:S(2)}) %collective-permute-start) | collective-permute-done | bytes 327712 | tf_op jit(solution)/shard_map/ppermute | solution.py:446
  65.1 1.7 %collective-permute-start.1 = (bf16[64,640]{1,0:T(8,128)(2,1)S(1)}, bf16[64,640]{1,0:T(8,128)(2,1)S(1)}, u32[]{:S(2)}, u32[]{:S(2)}) collective-permute-start(bf16[64,640]{1,0:T(8,128)(2,1)S(1)} %get-tuple-element.34), channel_id=1, source_target_pairs={{0,2},{1,3},{2,0},{3,1},{4,6},{5,7},{6,4},{7,5},{8,10},{9,11},{10,... | collective-permute-start | bytes 245768 | tf_op jit(solution)/shard_map/ppermute | solution.py:450
  66.8 3.3 %collective-permute-start.2 = (bf16[64,640]{1,0:T(8,128)(2,1)S(1)}, bf16[64,640]{1,0:T(8,128)(2,1)S(1)}, u32[]{:S(2)}, u32[]{:S(2)}) collective-permute-start(bf16[64,640]{1,0:T(8,128)(2,1)S(1)} %get-tuple-element.36), channel_id=1, source_target_pairs={{0,4},{1,5},{2,6},{3,7},{4,0},{5,1},{6,2},{7,3},{8,12},{9,13},{10,... | collective-permute-start | bytes 245768 | tf_op jit(solution)/shard_map/ppermute | solution.py:450
  70.1 3.9 %collective-permute-done.2 = bf16[64,640]{1,0:T(8,128)(2,1)S(1)} collective-permute-done((bf16[64,640]{1,0:T(8,128)(2,1)S(1)}, bf16[64,640]{1,0:T(8,128)(2,1)S(1)}, u32[]{:S(2)}, u32[]{:S(2)}) %collective-permute-start.2) | collective-permute-done | bytes 81952 | tf_op jit(solution)/shard_map/ppermute | solution.py:450
  74.0 1.9 %collective-permute-done.3 = bf16[64,640]{1,0:T(8,128)(2,1)S(1)} collective-permute-done((bf16[64,640]{1,0:T(8,128)(2,1)S(1)}, bf16[64,640]{1,0:T(8,128)(2,1)S(1)}, u32[]{:S(2)}, u32[]{:S(2)}) %collective-permute-start.3) | collective-permute-done | bytes 81952 | tf_op jit(solution)/shard_map/ppermute | solution.py:450
  78.0 6.9 %all-to-all-start.2 = ((bf16[16,8,640]{2,1,0:T(8,128)(2,1)}), bf16[16,8,640]{2,1,0:T(8,128)(2,1)S(1)}, u32[]{:S(2)}, u32[]{:S(2)}) async-start(bf16[16,8,640]{2,1,0:T(8,128)(2,1)} %reshape.114), calls=%async_computation.2 | async-start | bytes 327680 | tf_op jit(solution)/shard_map/all_to_all | solution.py:409
  84.9 7.0 %all-to-all-done.2 = bf16[16,8,640]{2,1,0:T(8,128)(2,1)S(1)} async-done(((bf16[16,8,640]{2,1,0:T(8,128)(2,1)}), bf16[16,8,640]{2,1,0:T(8,128)(2,1)S(1)}, u32[]{:S(2)}, u32[]{:S(2)}) %all-to-all-start.2) | async-done | bytes 163872 | tf_op jit(solution)/shard_map/all_to_all | solution.py:409
  93.0 1.7 %collective-permute-start.5 = (bf16[32,2,640]{2,1,0:T(2,128)(2,1)S(1)}, bf16[32,2,640]{2,1,0:T(2,128)(2,1)S(1)}, u32[]{:S(2)}, u32[]{:S(2)}) collective-permute-start(bf16[32,2,640]{2,1,0:T(2,128)(2,1)S(1)} %broadcast_select_fusion.3), channel_id=1, source_target_pairs={{0,4},{1,5},{2,6},{3,7},{4,0},{5,1},{6,2},{7,3},{8,12},{9,13},{10,... | collective-permute-start | bytes 245768 | tf_op jit(solution)/shard_map/ppermute | solution.py:472
  94.7 2.1 %collective-permute-start.6 = (bf16[32,2,640]{2,1,0:T(2,128)(2,1)S(1)}, bf16[32,2,640]{2,1,0:T(2,128)(2,1)S(1)}, u32[]{:S(2)}, u32[]{:S(2)}) collective-permute-start(bf16[32,2,640]{2,1,0:T(2,128)(2,1)S(1)} %broadcast_select_fusion.3), channel_id=1, source_target_pairs={{0,6},{1,7},{2,4},{3,5},{4,2},{5,3},{6,0},{7,1},{8,14},{9,15},{10,... | collective-permute-start | bytes 245768 | tf_op jit(solution)/shard_map/ppermute | solution.py:472
  97.9 1.3 %collective-permute-done.6 = bf16[32,2,640]{2,1,0:T(2,128)(2,1)S(1)} collective-permute-done((bf16[32,2,640]{2,1,0:T(2,128)(2,1)S(1)}, bf16[32,2,640]{2,1,0:T(2,128)(2,1)S(1)}, u32[]{:S(2)}, u32[]{:S(2)}) %collective-permute-start.6) | collective-permute-done | bytes 81952 | tf_op jit(solution)/shard_map/ppermute | solution.py:472
  100.6 4.0 %collective-permute-start.7 = (bf16[32,2,2560]{2,0,1:T(8,128)(2,1)S(1)}, bf16[32,2,2560]{2,0,1:T(8,128)(2,1)S(1)}, u32[]{:S(2)}, u32[]{:S(2)}) collective-permute-start(bf16[32,2,2560]{2,0,1:T(8,128)(2,1)S(1)} %bitcast.34), channel_id=1, source_target_pairs={{0,1},{1,0},{2,3},{3,2},{4,5},{5,4},{6,7},{7,6},{8,9},{9,8},{10,11... | collective-permute-start | bytes 983048 | tf_op jit(solution)/shard_map/ppermute | solution.py:475
  104.6 5.0 %place_context.2.rest_0_ = bf16[32,48,576]{2,1,0:T(8,128)(2,1)} custom-call(s32[32]{0:T(128)} %get-tuple-element.29.arrival, s32[32]{0:T(128)} %get-tuple-element.28.lengths, s32[1]{0:T(128)} %bitcast.3.where, bf16[16,3,216,128]{3,2,1,0:T(8,128)(2,1)} %copy-done), custom_call_target="tpu_custom_call" | custom-call | flops 1000 | bytes 1000 | tf_op jit(solution)/shard_map/place_context/pallas_call | solution.py:212
  109.7 3.6 %all-to-all-start.3 = ((bf16[16,1,216,128]{3,2,1,0:T(8,128)(2,1)}), bf16[16,1,216,128]{3,2,1,0:T(8,128)(2,1)S(1)}, u32[]{:S(2)}, u32[]{:S(2)}) async-start(bf16[16,1,216,128]{3,2,1,0:T(8,128)(2,1)} %get-tuple-element.20), calls=%async_computation.3 | async-start | bytes 1769472 | tf_op jit(solution)/shard_map/all_to_all | solution.py:409
  113.5 1.3 %copy.21 = bf16[32,4,2560]{2,1,0:T(4,128)(2,1)} copy(bf16[32,4,2560]{2,0,1:T(8,128)(2,1)S(1)} %pad_maximum_fusion) | data formatting | bytes 1310720
  114.8 14.9 %all-to-all-done.3.packed = bf16[16,1,216,128]{3,2,1,0:T(8,128)(2,1)S(1)} async-done(((bf16[16,1,216,128]{3,2,1,0:T(8,128)(2,1)}), bf16[16,1,216,128]{3,2,1,0:T(8,128)(2,1)S(1)}, u32[]{:S(2)}, u32[]{:S(2)}) %all-to-all-start.3) | async-done | bytes 884768 | tf_op jit(solution)/shard_map/all_to_all | solution.py:409
  130.6 3.2 %place_context.3 = bf16[32,48,576]{2,1,0:T(8,128)(2,1)} custom-call(s32[32]{0:T(128)} %get-tuple-element.29.arrival, s32[32]{0:T(128)} %get-tuple-element.28.lengths, s32[1]{0:T(128)} %bitcast.3.where, bf16[16,1,216,128]{3,2,1,0:T(8,128)(2,1)} %copy-done.2, bf16[32,48,576]{2,1,0:T(8,128)(2,1)} %place_context.2.rest_0_), custom_call_target="tpu_custom_call", output_to_operand_aliasing={{}: (4, {})} | custom-call | flops 1000 | bytes 1000 | tf_op jit(solution)/shard_map/place_context/pallas_call | solution.py:212
  (59 shorter events, 12.3 us)
Async XLA Ops:
  8.6 23.9 %all-to-all-start = ((bf16[16,264,128]{2,1,0:T(8,128)(2,1)}), bf16[16,264,128]{2,1,0:T(8,128)(2,1)S(1)}, u32[]{:S(2)}, u32[]{:S(2)}) async-start(bf16[16,264,128]{2,1,0:T(8,128)(2,1)} %pack_queries.1), calls=%async_computation | async-start | bytes 2162688 | tf_op jit(solution)/shard_map/all_to_all | solution.py:409
  32.5 1.0 copy-start.1
  32.5 6.9 %copy-start.3 = (s32[32]{0:T(128)S(1)}, s32[32]{0:T(128)}, u32[]{:S(2)}) copy-start(s32[32]{0:T(128)} %get-tuple-element.29.arrival) | copy-start | bytes 388
  33.5 44.4 %all-to-all-start.1 = ((bf16[16,3,216,128]{3,2,1,0:T(8,128)(2,1)}), bf16[16,3,216,128]{3,2,1,0:T(8,128)(2,1)S(1)}, u32[]{:S(2)}, u32[]{:S(2)}) async-start(bf16[16,3,216,128]{3,2,1,0:T(8,128)(2,1)} %get-tuple-element.16), calls=%async_computation.1 | async-start | bytes 5308416 | tf_op jit(solution)/shard_map/all_to_all | solution.py:409
  60.8 3.1 %collective-permute-start = (bf16[64,2560]{1,0:T(8,128)(2,1)}, bf16[64,2560]{1,0:T(8,128)(2,1)S(1)}, u32[]{:S(2)}, u32[]{:S(2)}) collective-permute-start(bf16[64,2560]{1,0:T(8,128)(2,1)} %get-tuple-element.15), channel_id=1, source_target_pairs={{0,1},{1,0},{2,3},{3,2},{4,5},{5,4},{6,7},{7,6},{8,9},{9,8},{10,11... | collective-permute-start | bytes 983048 | tf_op jit(solution)/shard_map/ppermute | solution.py:446
  65.1 5.0 %collective-permute-start.1 = (bf16[64,640]{1,0:T(8,128)(2,1)S(1)}, bf16[64,640]{1,0:T(8,128)(2,1)S(1)}, u32[]{:S(2)}, u32[]{:S(2)}) collective-permute-start(bf16[64,640]{1,0:T(8,128)(2,1)S(1)} %get-tuple-element.34), channel_id=1, source_target_pairs={{0,2},{1,3},{2,0},{3,1},{4,6},{5,7},{6,4},{7,5},{8,10},{9,11},{10,... | collective-permute-start | bytes 245768 | tf_op jit(solution)/shard_map/ppermute | solution.py:450
  66.8 7.3 %collective-permute-start.2 = (bf16[64,640]{1,0:T(8,128)(2,1)S(1)}, bf16[64,640]{1,0:T(8,128)(2,1)S(1)}, u32[]{:S(2)}, u32[]{:S(2)}) collective-permute-start(bf16[64,640]{1,0:T(8,128)(2,1)S(1)} %get-tuple-element.36), channel_id=1, source_target_pairs={{0,4},{1,5},{2,6},{3,7},{4,0},{5,1},{6,2},{7,3},{8,12},{9,13},{10,... | collective-permute-start | bytes 245768 | tf_op jit(solution)/shard_map/ppermute | solution.py:450
  70.1 5.9 %collective-permute-start.3 = (bf16[64,640]{1,0:T(8,128)(2,1)S(1)}, bf16[64,640]{1,0:T(8,128)(2,1)S(1)}, u32[]{:S(2)}, u32[]{:S(2)}) collective-permute-start(bf16[64,640]{1,0:T(8,128)(2,1)S(1)} %get-tuple-element.35), channel_id=1, source_target_pairs={{0,6},{1,7},{2,4},{3,5},{4,2},{5,3},{6,0},{7,1},{8,14},{9,15},{10,... | collective-permute-start | bytes 245768 | tf_op jit(solution)/shard_map/ppermute | solution.py:450
  78.0 26.7 %copy-start = (bf16[16,3,216,128]{3,2,1,0:T(8,128)(2,1)}, bf16[16,3,216,128]{3,2,1,0:T(8,128)(2,1)S(1)}, u32[]{:S(2)}) copy-start(bf16[16,3,216,128]{3,2,1,0:T(8,128)(2,1)S(1)} %all-to-all-done.1.packed) | copy-start | bytes 7962628
  78.0 14.0 %all-to-all-start.2 = ((bf16[16,8,640]{2,1,0:T(8,128)(2,1)}), bf16[16,8,640]{2,1,0:T(8,128)(2,1)S(1)}, u32[]{:S(2)}, u32[]{:S(2)}) async-start(bf16[16,8,640]{2,1,0:T(8,128)(2,1)} %reshape.114), calls=%async_computation.2 | async-start | bytes 327680 | tf_op jit(solution)/shard_map/all_to_all | solution.py:409
  92.9 4.1 %collective-permute-start.4 = (bf16[32,2,640]{2,1,0:T(2,128)(2,1)S(1)}, bf16[32,2,640]{2,1,0:T(2,128)(2,1)S(1)}, u32[]{:S(2)}, u32[]{:S(2)}) collective-permute-start(bf16[32,2,640]{2,1,0:T(2,128)(2,1)S(1)} %broadcast_select_fusion.3), channel_id=1, source_target_pairs={{0,2},{1,3},{2,0},{3,1},{4,6},{5,7},{6,4},{7,5},{8,10},{9,11},{10,... | collective-permute-start | bytes 245768 | tf_op jit(solution)/shard_map/ppermute | solution.py:472
  93.0 4.9 %collective-permute-start.5 = (bf16[32,2,640]{2,1,0:T(2,128)(2,1)S(1)}, bf16[32,2,640]{2,1,0:T(2,128)(2,1)S(1)}, u32[]{:S(2)}, u32[]{:S(2)}) collective-permute-start(bf16[32,2,640]{2,1,0:T(2,128)(2,1)S(1)} %broadcast_select_fusion.3), channel_id=1, source_target_pairs={{0,4},{1,5},{2,6},{3,7},{4,0},{5,1},{6,2},{7,3},{8,12},{9,13},{10,... | collective-permute-start | bytes 245768 | tf_op jit(solution)/shard_map/ppermute | solution.py:472
  94.7 4.5 %collective-permute-start.6 = (bf16[32,2,640]{2,1,0:T(2,128)(2,1)S(1)}, bf16[32,2,640]{2,1,0:T(2,128)(2,1)S(1)}, u32[]{:S(2)}, u32[]{:S(2)}) collective-permute-start(bf16[32,2,640]{2,1,0:T(2,128)(2,1)S(1)} %broadcast_select_fusion.3), channel_id=1, source_target_pairs={{0,6},{1,7},{2,4},{3,5},{4,2},{5,3},{6,0},{7,1},{8,14},{9,15},{10,... | collective-permute-start | bytes 245768 | tf_op jit(solution)/shard_map/ppermute | solution.py:472
  100.6 12.7 %collective-permute-start.7 = (bf16[32,2,2560]{2,0,1:T(8,128)(2,1)S(1)}, bf16[32,2,2560]{2,0,1:T(8,128)(2,1)S(1)}, u32[]{:S(2)}, u32[]{:S(2)}) collective-permute-start(bf16[32,2,2560]{2,0,1:T(8,128)(2,1)S(1)} %bitcast.34), channel_id=1, source_target_pairs={{0,1},{1,0},{2,3},{3,2},{4,5},{5,4},{6,7},{7,6},{8,9},{9,8},{10,11... | collective-permute-start | bytes 983048 | tf_op jit(solution)/shard_map/ppermute | solution.py:475
  109.7 20.0 %all-to-all-start.3 = ((bf16[16,1,216,128]{3,2,1,0:T(8,128)(2,1)}), bf16[16,1,216,128]{3,2,1,0:T(8,128)(2,1)S(1)}, u32[]{:S(2)}, u32[]{:S(2)}) async-start(bf16[16,1,216,128]{3,2,1,0:T(8,128)(2,1)} %get-tuple-element.20), calls=%async_computation.3 | async-start | bytes 1769472 | tf_op jit(solution)/shard_map/all_to_all | solution.py:409
  129.7 0.9 copy-start.2

commit v4 on v3

--- a/solution.py
+++ b/solution.py
@@ -17,46 +17,58 @@
 BF16 = jnp.bfloat16
 F32 = jnp.float32
 
-VMEM_LIMIT = 60 * 1024 * 1024
+MIB = 1024 * 1024
 SMEM_SPEC = pl.BlockSpec(memory_space=pltpu.SMEM)
 VMEM_SPEC = pl.BlockSpec(memory_space=pltpu.VMEM)
 ANY_SPEC = pl.BlockSpec(memory_space=pl.ANY)
 NT = (((1,), (1,)), ((), ()))
 
 
-def params(**kw):
-    return pltpu.CompilerParams(vmem_limit_bytes=VMEM_LIMIT, **kw)
+def params(mib=16):
+    return pltpu.CompilerParams(vmem_limit_bytes=mib * MIB)
 
 
 def cost(flops=1000, bytes_accessed=1000):
     return pl.CostEstimate(flops=flops, bytes_accessed=bytes_accessed, transcendentals=0)
 
 
-def route(decode_slot, pool_index, pool_count, slot_count):
-    targets = decode_slot // slot_count
-    by_source = targets.reshape(pool_count, slot_count)
-    earlier = jnp.tril(jnp.ones((slot_count, slot_count), jnp.int32), -1)
-    own = lax.dynamic_slice_in_dim(by_source, pool_index, 1, 0)[0]
-    same = (own[:, None] == own[None, :]).astype(jnp.int32)
-    placing = own * CAP + jnp.sum(same * earlier, axis=1)
-    arriving = (by_source == pool_index).astype(jnp.int32)
-    before = jnp.cumsum(arriving, axis=1) - arriving
-    cell = (jnp.arange(pool_count)[:, None] * CAP + before).reshape(-1)
-    wanted = pool_index * slot_count + jnp.arange(slot_count)
-    match = decode_slot[None, :] == wanted[:, None]
-    arrival = jnp.sum(jnp.where(match, cell[None, :], 0), axis=1)
-    return placing, arrival, match
-
-
-def pack_queries_kernel(arrival, q_ref, n_ref, out_ref, new_rows, tails):
+def split(cell):
+    return cell // CAP, cell % CAP
+
+
+def pack_queries_kernel(
+    decode_slot, prompt_lengths, where, q_hbm, n_hbm,
+    out_ref, arrival, lengths,
+    q_ref, n_ref, new_rows, tails, sems,
+):
     steps, slots, heads, width = q_ref.shape
     rows = steps * heads
     blocks = n_ref.shape[2] // 128
+    copy_n = pltpu.make_async_copy(n_hbm, n_ref, sems.at[0])
+    copy_q = pltpu.make_async_copy(q_hbm, q_ref, sems.at[1])
+    copy_n.start()
+    copy_q.start()
+    first = where[1] * slots
+
+    def locate(p, carry):
+        rank = jnp.int32(0)
+        for k in range(slots):
+            inner = decode_slot[p * slots + k] - first
+            hit = (inner >= 0) & (inner < slots)
+            at = jnp.where(hit, inner, slots)
+            arrival[at] = p * CAP + rank
+            lengths[at] = prompt_lengths[p * slots + k]
+            rank = rank + hit.astype(jnp.int32)
+        return carry
+
+    lax.fori_loop(0, out_ref.shape[0], locate, 0)
+    tails[...] = jnp.zeros(tails.shape, F32)
+    copy_n.wait()
     new_rows[...] = n_ref[...].astype(F32)
-    tails[...] = jnp.zeros(tails.shape, F32)
+    copy_q.wait()
 
     def one(j, carry):
-        dest, rank = arrival[j] // CAP, arrival[j] % CAP
+        dest, rank = split(arrival[j])
         x = q_ref[:, j].astype(F32)
         nope = x[:, :, :NOPE].reshape(rows, NOPE)
         rope = x[:, :, NOPE:].reshape(rows, ROPE)
@@ -71,27 +83,37 @@
         )
         return carry
 
-    lax.fori_loop(0, slots, one, 0)
+    lax.fori_loop(0, slots, one, 0, unroll=4)
     out_ref[:, 256:264, :] = tails[...].reshape(out_ref.shape[0], 8, 128).astype(BF16)
 
 
-def pack_queries(arrival, queries, new_latent, pool_count):
+def pack_queries(decode_slot, prompt_lengths, where, queries, new_latent, pool_count):
+    slots = queries.shape[1]
     return pl.pallas_call(
         pack_queries_kernel,
-        out_shape=jax.ShapeDtypeStruct((pool_count, 264, 128), BF16),
-        in_specs=[SMEM_SPEC, VMEM_SPEC, VMEM_SPEC],
-        out_specs=VMEM_SPEC,
+        out_shape=(
+            jax.ShapeDtypeStruct((pool_count, 264, 128), BF16),
+            jax.ShapeDtypeStruct((slots + 8,), jnp.int32),
+            jax.ShapeDtypeStruct((slots + 8,), jnp.int32),
+        ),
+        in_specs=[SMEM_SPEC] * 3 + [ANY_SPEC] * 2,
+        out_specs=(VMEM_SPEC, SMEM_SPEC, SMEM_SPEC),
         scratch_shapes=[
+            pltpu.VMEM(queries.shape, BF16),
+            pltpu.VMEM(new_latent.shape, BF16),
             pltpu.VMEM(new_latent.shape, F32),
             pltpu.VMEM((pool_count * 8, 128), F32),
+            pltpu.SemaphoreType.DMA((2,)),
         ],
-        compiler_params=params(),
+        compiler_params=params(60),
         cost_estimate=cost(),
         name="pack_queries",
-    )(arrival, queries, new_latent)
-
-
-def pack_context_kernel(placing, where, p_ref, first_ref, second_ref, buf, sems):
+    )(decode_slot, prompt_lengths, where, queries, new_latent)
+
+
+def pack_context_kernel(
+    decode_slot, where, p_ref, first_ref, second_ref, placing, counts, buf, sems
+):
     slots, feature, window = buf.shape
     blocks = feature // 128
     piece = first_ref.shape[2] * 128 // feature
@@ -108,6 +130,14 @@
     ]
     for copy in copies:
         copy.start()
+    bits = slots.bit_length() - 1
+    for p in range(counts.shape[0]):
+        counts[p] = 0
+    for g in range(slots):
+        owner = decode_slot[where[1] * slots + g] >> bits
+        rank = counts[owner]
+        counts[owner] = rank + 1
+        placing[g] = owner * CAP + rank
     pick = lax.broadcasted_iota(jnp.int32, (piece, window), 1) - (
         row - start + lax.broadcasted_iota(jnp.int32, (piece, window), 0)
     )
@@ -118,7 +148,7 @@
 
         def one(n, carry):
             g = k * chunk + n
-            dest, rank = placing[g] // CAP, placing[g] % CAP
+            dest, rank = split(placing[g])
             turned = lax.dot_general(pick, buf[g], NT, preferred_element_type=F32)
             last = turned[:, 128 * blocks :]
             last = jnp.concatenate([last[: piece // 2], last[piece // 2 :]], axis=1)
@@ -132,32 +162,34 @@
 
             @pl.when(rank >= FIRST_RANKS)
             def _():
-                second_ref[dest, rank - FIRST_RANKS] = cell
+                second_ref[dest] = cell
 
             return carry
 
         lax.fori_loop(0, chunk, one, 0, unroll=2)
 
 
-def pack_context(placing, where, prompt_latent, piece, pool_count):
+def pack_context(decode_slot, where, prompt_latent, piece, pool_count):
     slots, feature, _ = prompt_latent.shape
     rows = piece * feature // 128
     return pl.pallas_call(
         pack_context_kernel,
         out_shape=(
             jax.ShapeDtypeStruct((pool_count, FIRST_RANKS, rows, 128), BF16),
-            jax.ShapeDtypeStruct((pool_count, CAP - FIRST_RANKS, rows, 128), BF16),
+            jax.ShapeDtypeStruct((pool_count, rows, 128), BF16),
+            jax.ShapeDtypeStruct((slots,), jnp.int32),
         ),
         in_specs=[SMEM_SPEC, SMEM_SPEC, ANY_SPEC],
-        out_specs=(VMEM_SPEC, VMEM_SPEC),
+        out_specs=(VMEM_SPEC, VMEM_SPEC, SMEM_SPEC),
         scratch_shapes=[
+            pltpu.SMEM((pool_count,), jnp.int32),
             pltpu.VMEM((slots, feature, 256), BF16),
             pltpu.SemaphoreType.DMA((4,)),
         ],
-        compiler_params=params(),
+        compiler_params=params(60),
         cost_estimate=cost(),
         name="pack_context",
-    )(placing, where, prompt_latent)
+    )(decode_slot, where, prompt_latent)
 
 
 def unpack_piece(packed, row, first_row, length, piece, feature):
@@ -170,22 +202,25 @@
     return jnp.where(position < length, whole.astype(F32), 0.0).astype(BF16)
 
 
-def place_kernel(low, high, keep, arrival, lengths, where, packed, *rest):
+def place_kernel(low, high, arrival, lengths, where, packed, *rest):
     out_ref, inbox, outbox, in_sems, out_sems = rest[-5:]
     slots, piece, feature = out_ref.shape
     first_row = where[0] * piece
 
     def copy_in(j):
-        owner, rank = arrival[j] // CAP, arrival[j] % CAP
-        rank = jnp.clip(rank - low, 0, high - low - 1)
-        return pltpu.make_async_copy(packed.at[owner, rank], inbox.at[j], in_sems.at[j])
+        owner, rank = split(arrival[j])
+        if high - low == 1:
+            source = packed.at[owner]
+        else:
+            source = packed.at[owner, jnp.clip(rank - low, 0, high - low - 1)]
+        return pltpu.make_async_copy(source, inbox.at[j], in_sems.at[j])
 
     def copy_out(j):
         return pltpu.make_async_copy(outbox.at[j], out_ref.at[j], out_sems.at[j])
 
     def each(action):
         def step(j, carry):
-            rank = arrival[j] % CAP
+            rank = split(arrival[j])[1]
 
             @pl.when((rank >= low) & (rank < high))
             def _():
@@ -206,11 +241,11 @@
 
 
 def place(low, high, arrival, lengths, where, packed, piece, feature, context=None):
-    slots = arrival.shape[0]
-    rows = packed.shape[2]
+    slots = arrival.shape[0] - 8
+    rows = packed.shape[-2]
     args = [arrival, lengths, where, packed] + ([] if context is None else [context])
     return pl.pallas_call(
-        functools.partial(place_kernel, low, high, context is not None),
+        functools.partial(place_kernel, low, high),
         out_shape=jax.ShapeDtypeStruct((slots, piece, feature), BF16),
         in_specs=[SMEM_SPEC] * 3 + [ANY_SPEC] * (len(args) - 3),
         out_specs=ANY_SPEC,
@@ -222,7 +257,7 @@
         ],
         input_output_aliases={} if context is None else {4: 0},
         compiler_params=params(),
-        cost_estimate=cost(),
+        cost_estimate=cost(bytes_accessed=12_000_000 if context is None else 1000),
         name="place_context",
     )(*args)
 
@@ -240,6 +275,7 @@
     per_step = slots * heads
     many = slots * steps
     scale = 1.0 / math.sqrt(nope + ROPE)
+    first = where[1] * slots
     copy_payload = pltpu.make_async_copy(payload_hbm, payload, sems.at[0])
     copy_uk = pltpu.make_async_copy(w_uk_hbm, w_uk, sems.at[1])
     copy_uv = pltpu.make_async_copy(w_uv_hbm, w_uv, sems.at[2])
@@ -275,7 +311,7 @@
     tails[...] = payload[:, 256:264, :].astype(F32).reshape(tails.shape)
 
     def unpack(i, carry):
-        dest, rank = placing[i] // CAP, placing[i] % CAP
+        dest, rank = split(placing[i])
         cell = payload[dest, pl.ds(pl.multiple_of(rank * 64, 64), 64), :].astype(F32)
         collect(q_nope, i, cell[:32])
         rope = jnp.concatenate([cell[32:48, :64], cell[32:48, 64:]], axis=0)
@@ -318,7 +354,7 @@
         s_prompt = scale * jnp.dot(q, prompt[i], preferred_element_type=F32)
         s_fresh = spread(fresh_score, i)
         column = lax.broadcasted_iota(jnp.int32, s_prompt.shape, 1)
-        s_prompt = jnp.where(column < lengths[i], s_prompt, FLOOR)
+        s_prompt = jnp.where(column < lengths[first + i], s_prompt, FLOOR)
         step_of = lax.broadcasted_iota(jnp.int32, s_fresh.shape, 0) // heads
         column = lax.broadcasted_iota(jnp.int32, s_fresh.shape, 1) - steps * i
         s_fresh = jnp.where((column >= 0) & (column <= step_of), s_fresh, FLOOR)
@@ -399,12 +435,153 @@
             pltpu.VMEM((steps * slots, heads * 128), BF16),
             pltpu.SemaphoreType.DMA((4 + slots // GROUP,)),
         ],
-        compiler_params=params(),
+        compiler_params=params(60),
         cost_estimate=cost(),
         name="attention",
     )(placing, lengths, where, payload, prompt_latent, w_uk, w_uv, w_out)
 
 
+def share_kernel(where, kept, swapped, mine, *parts):
+    block = mine.shape[1]
+    z = where[0] >> 1
+    for d, part in enumerate((mine,) + parts):
+        at = pl.ds(pl.multiple_of((z ^ d) * block, 128), block)
+        part[...] = (kept[:, at] + swapped[:, at].astype(F32)).astype(part.dtype)
+
+
+def share(where, kept, swapped, z_count):
+    rows, width = kept.shape
+    block = width // z_count
+    return pl.pallas_call(
+        share_kernel,
+        out_shape=(jax.ShapeDtypeStruct((rows, block), F32),)
+        + (jax.ShapeDtypeStruct((rows, block), BF16),) * (z_count - 1),
+        in_specs=[SMEM_SPEC] + [VMEM_SPEC] * 2,
+        out_specs=(VMEM_SPEC,) * z_count,
+        compiler_params=params(),
+        cost_estimate=cost(),
+        name="share",
+    )(where, kept, swapped)
+
+
+def pack_back_kernel(placing, second, mine, *rest):
+    parts, (out_ref, total, rows) = rest[:-3], rest[-3:]
+    slots = placing.shape[0]
+    blocks = mine.shape[1] // 128
+    steps = mine.shape[0] // slots
+    context_rows = second.shape[1]
+    whole = mine[...]
+    for part in parts:
+        whole = whole + part[...].astype(F32)
+    for b in range(blocks):
+        total[b] = whole[:, 128 * b : 128 * b + 128]
+    out_ref[:, :context_rows, :] = second[...]
+    rows[...] = jnp.zeros(rows.shape, F32)
+
+    def one(i, carry):
+        dest, rank = split(placing[i])
+        for s in range(steps):
+            for b in range(blocks):
+                at = dest * (8 * blocks) + 8 * b + steps * rank + s
+                rows[pl.ds(at, 1), :] = total[b, pl.ds(slots * s + i, 1), :]
+        return carry
+
+    lax.fori_loop(0, slots, one, 0, unroll=4)
+    out_ref[:, context_rows:, :] = (
+        rows[...].reshape(out_ref.shape[0], 8 * blocks, 128).astype(BF16)
+    )
+
+
+def pack_back(placing, second, mine, parts):
+    pool_count, context_rows, _ = second.shape
+    blocks = mine.shape[1] // 128
+    return pl.pallas_call(
+        pack_back_kernel,
+        out_shape=jax.ShapeDtypeStruct((pool_count, context_rows + 8 * blocks, 128), BF16),
+        in_specs=[SMEM_SPEC] + [VMEM_SPEC] * (2 + len(parts)),
+        out_specs=VMEM_SPEC,
+        scratch_shapes=[
+            pltpu.VMEM((blocks, mine.shape[0], 128), F32),
+            pltpu.VMEM((pool_count * 8 * blocks, 128), F32),
+        ],
+        compiler_params=params(),
+        cost_estimate=cost(),
+        name="pack_back",
+    )(placing, second, mine, *parts)
+
+
+def unpack_back_kernel(steps, arrival, packed, out_ref, rows, total):
+    slots = out_ref.shape[0] // steps
+    blocks = out_ref.shape[1] // 128
+    first = packed.shape[1] - 8 * blocks
+    rows[...] = packed[:, first:, :].astype(F32).reshape(rows.shape)
+
+    def one(j, carry):
+        owner, rank = split(arrival[j])
+        for b in range(blocks):
+            at = owner * (8 * blocks) + 8 * b + steps * rank
+            total[b, pl.ds(steps * j, steps), :] = rows[pl.ds(at, steps), :]
+        return carry
+
+    lax.fori_loop(0, slots, one, 0, unroll=4)
+    for b in range(blocks):
+        out_ref[:, 128 * b : 128 * b + 128] = total[b].astype(BF16)
+
+
+def unpack_back(arrival, packed, steps, slots, block):
+    return pl.pallas_call(
+        functools.partial(unpack_back_kernel, steps),
+        out_shape=jax.ShapeDtypeStruct((steps * slots, block), BF16),
+        in_specs=[SMEM_SPEC, VMEM_SPEC],
+        out_specs=VMEM_SPEC,
+        scratch_shapes=[
+            pltpu.VMEM((packed.shape[0] * 8 * (block // 128), 128), F32),
+            pltpu.VMEM((block // 128, steps * slots, 128), F32),
+        ],
+        compiler_params=params(),
+        cost_estimate=cost(),
+        name="unpack_back",
+    )(arrival, packed)
+
+
+def assemble_kernel(where, *rest):
+    parts, (out_ref, part, whole) = rest[:-3], rest[-3:]
+    slots, steps, width = out_ref.shape
+    z_count = len(parts) // 2
+    block = width // z_count
+    core, z = where[0] & 1, where[0] >> 1
+    for n, ref in enumerate(parts):
+        side = core if n < z_count else 1 - core
+        start = (z ^ (n % z_count)) * (block // 128)
+        for b in range(block // 128):
+            part[...] = ref[:, 128 * b : 128 * b + 128].astype(F32)
+            for s in range(steps // 2):
+                whole[start + b, pl.ds((steps // 2) * side + s, slots, stride=steps), :] = part[
+                    pl.ds(s, slots, stride=steps // 2), :
+                ]
+    for j in range(slots):
+        for b in range(width // 128):
+            out_ref[j, :, 128 * b : 128 * b + 128] = whole[
+                b, steps * j : steps * j + steps, :
+            ].astype(BF16)
+
+
+def assemble(where, parts, slots, steps, width):
+    return pl.pallas_call(
+        assemble_kernel,
+        out_shape=jax.ShapeDtypeStruct((slots, steps, width), BF16),
+        in_specs=[SMEM_SPEC] + [VMEM_SPEC] * len(parts),
+        out_specs=VMEM_SPEC,
+        scratch_shapes=[
+            pltpu.VMEM((parts[0].shape[0], 128), F32),
+            pltpu.VMEM((width // 128, slots * steps, 128), F32),
+        ],
+        compiler_params=params(),
+        cost_estimate=cost(),
+        name="assemble",
+    )(where, *parts)
+
+
 def exchange(x):
     return lax.all_to_all(x, "pool", split_axis=0, concat_axis=0, tiled=True)
 
@@ -412,77 +589,44 @@
 def body(prompt_latent, prompt_lengths, decode_slot, new_latent, queries, w_uk, w_uv, w_out):
     pool_count = lax.axis_size("pool")
     tp_count = lax.axis_size("tp")
-    pool_index = lax.axis_index("pool")
     tp_index = lax.axis_index("tp")
     latent_t = prompt_latent.transpose(0, 2, 1)
     steps, slots, heads, width = queries.shape
     span, feature = prompt_latent.shape[1:]
     piece = span // tp_count
     out_width = w_out.shape[1]
-    cells = pool_count * CAP
-    where = tp_index.astype(jnp.int32).reshape(1)
-    placing, arrival, match = route(decode_slot, pool_index, pool_count, slots)
-    decode_lengths = jnp.sum(jnp.where(match, prompt_lengths[None, :], 0), axis=1)
-    own_lengths = lax.dynamic_slice_in_dim(prompt_lengths, pool_index * slots, slots)
-
-    payload = exchange(pack_queries(arrival, queries, new_latent, pool_count))
-    first_send, second_send = pack_context(placing, where, latent_t, piece, pool_count)
-    payload, first_send = lax.optimization_barrier((payload, first_send))
-    first = exchange(first_send)
+    z_count = tp_count // 2
+    where = jnp.stack([tp_index, lax.axis_index("pool")]).astype(jnp.int32)
+    swap = [(i, i ^ 1) for i in range(tp_count)]
+    hops = [[(i, i ^ (2 * d)) for i in range(tp_count)] for d in range(1, z_count)]
+
+    payload, arrival, lengths = pack_queries(
+        decode_slot, prompt_lengths, where, queries, new_latent, pool_count
+    )
+    payload = exchange(payload)
+    first, second, placing = pack_context(decode_slot, where, latent_t, piece, pool_count)
+    payload, first = lax.optimization_barrier((payload, first))
+    first = exchange(first)
 
     given, kept = attention(
-        placing, own_lengths, where, payload, latent_t, w_uk, w_uv, w_out, steps
+        placing, prompt_lengths, where, payload, latent_t, w_uk, w_uv, w_out, steps
     )
 
-    core = tp_index % 2
-    z = tp_index // 2
-    z_count = tp_count // 2
-    block = out_width // z_count
-    swap = [(i, i ^ 1) for i in range(tp_count)]
-
-    def hop(d):
-        return [(i, i ^ (2 * d)) for i in range(tp_count)]
-
-    pair = kept + lax.ppermute(given, "tp", swap).astype(F32)
-    mine = lax.dynamic_slice_in_dim(pair, z * block, block, 1)
-    pair16 = pair.astype(BF16)
-    got = [
-        lax.ppermute(
-            lax.dynamic_slice_in_dim(pair16, (z ^ d) * block, block, 1), "tp", hop(d)
-        )
-        for d in range(1, z_count)
-    ]
-    for part in got:
-        mine = mine + part.astype(F32)
-    mine = mine.astype(BF16).reshape(steps // 2, slots, block)
-
-    grid_cells = jnp.arange(cells)
-    source_row = jnp.sum(
-        jnp.where(placing[None, :] == grid_cells[:, None], jnp.arange(slots)[None, :], 0), axis=1
-    )
-    back = jnp.take(mine, source_row, axis=1).transpose(1, 0, 2)
-    back = back.reshape(pool_count, CAP * steps // 2, block)
+    swapped = lax.ppermute(given, "tp", swap)
+    mine, *parts = share(where, kept, swapped, z_count)
+    parts = [lax.ppermute(part, "tp", hop) for part, hop in zip(parts, hops)]
+
+    back = pack_back(placing, second, mine, parts)
     back, first = lax.optimization_barrier((back, first))
     back = exchange(back)
-    back, second_send = lax.optimization_barrier((back, second_send))
-    second = exchange(second_send)
-    context = place(0, FIRST_RANKS, arrival, decode_lengths, where, first, piece, feature)
-
-    back = jnp.take(back.reshape(cells, steps // 2, block), arrival, axis=0)
-    parts = jnp.stack([back] + [lax.ppermute(back, "tp", hop(d)) for d in range(1, z_count)])
-    parts = jnp.take(parts, jnp.arange(z_count) ^ z, axis=0)
-    row_half = parts.transpose(1, 2, 0, 3).reshape(slots, steps // 2, out_width)
-    other_half = lax.ppermute(row_half, "tp", swap)
-    decoded = jnp.concatenate(
-        [
-            jnp.where(core == 0, row_half, other_half),
-            jnp.where(core == 0, other_half, row_half),
-        ],
-        axis=1,
-    )
-    context = place(
-        FIRST_RANKS, CAP, arrival, decode_lengths, where, second, piece, feature, context
-    )
+    context = place(0, FIRST_RANKS, arrival, lengths, where, first, piece, feature)
+    back, context = lax.optimization_barrier((back, context))
+
+    own = unpack_back(arrival, back, steps // 2, slots, out_width // z_count)
+    parts = [own] + [lax.ppermute(own, "tp", hop) for hop in hops]
+    parts = parts + [lax.ppermute(part, "tp", swap) for part in parts]
+    context = place(FIRST_RANKS, CAP, arrival, lengths, where, back, piece, feature, context)
+    decoded = assemble(where, parts, slots, steps, out_width)
     return decoded, context
 
 

time: 135 us -> 116 us (0.86)
  waiting for transfers between devices: 32.2 us -> 18.9 us
  Pallas kernels: 47.4 us -> 54.8 us
  other arithmetic: 6.5 us -> 0.65 us
  local copies, waits for them, and re-layouts: 8.11 us -> 3.06 us
  starting transfers between devices: 38.6 us -> 37 us
    all_to_all x4 -> x3, waiting for transfers between devices: 22.6 us -> 11.6 us  [exchange(): return lax.all_to_all(x, 'pool', split_axis=0, concat_axis=0, tiled=True)]
    pallas_call x3 -> x7, Pallas kernels: 12.9 us -> 19.9 us  [the longest x2 10.2 us: place(): pl.pallas_call(functools.partial(place_kernel, low, high), out_shape=jax....]
    all_to_all x4 -> x3, starting transfers between devices: 24 us -> 18.8 us  [exchange(): return lax.all_to_all(x, 'pool', split_axis=0, concat_axis=0, tiled=True)]
    ppermute x8 -> x11, starting transfers between devices: 14.6 us -> 18.2 us  [the longest x4 7.02 us: body(): parts = parts + [lax.ppermute(part, 'tp', swap) for part in parts]]
    gather x3 -> x0, local copies, waits for them, and re-layouts: 2.25 us -> none  [the longest x1 0.91 us: body(): back = jnp.take(mine, source_row, axis=1).transpose(1, 0, 2)]
    ppermute x8 -> x11, waiting for transfers between devices: 9.54 us -> 7.37 us  [the longest x3 5.88 us: body(): parts = [lax.ppermute(part, 'tp', hop) for part, hop in zip(parts, hops)]]
    reduce_sum x3 -> x0, other arithmetic: 1.7 us -> none  [the longest x1 1.42 us: body(): jnp.sum(jnp.where(match, prompt_lengths[None, :], 0), axis=1)]
    dynamic_slice x2 -> x0, local copies, waits for them, and re-layouts: 1.36 us -> none  [the longest x1 1.32 us: body(): lax.dynamic_slice_in_dim(prompt_lengths, pool_index * slots, slots)]
  transfers between devices with their start and end apart: 12 -> 14, of which waited for: 8 -> 5; matrix products, arithmetic and copies ran while one was open for 5% -> 0% of each run, Pallas kernels for 30% -> 40%
where the time goes in v4:
time: 116 us; the launch traced here: 115 us
  Pallas kernels  54.8 us (47%)
  starting transfers between devices  37 us (32%)
  waiting for transfers between devices  18.9 us (16%)
  local copies, waits for them, and re-layouts  3.06 us (3%)
    pallas_call x1, Pallas kernels, attention(): pl.pallas_call(attention_kernel, out_shape=(jax.ShapeDtypeStruct((half, w...  21.5 us
    all_to_all x3, starting transfers between devices, exchange(): return lax.all_to_all(x, 'pool', split_axis=0, concat_axis=0, tiled=True)  18.8 us
    pallas_call x1, Pallas kernels, pack_context(): pl.pallas_call(pack_context_kernel, out_shape=(jax.ShapeDtypeStruct((pool...  13.3 us
    all_to_all x3, waiting for transfers between devices, exchange(): return lax.all_to_all(x, 'pool', split_axis=0, concat_axis=0, tiled=True)  11.6 us
    pallas_call x2, Pallas kernels, place(): pl.pallas_call(functools.partial(place_kernel, low, high), out_shape=jax....  10.2 us
    ppermute x4, starting transfers between devices, body(): parts = parts + [lax.ppermute(part, 'tp', swap) for part in parts]  7.02 us
    ppermute x3, waiting for transfers between devices, body(): parts = [lax.ppermute(part, 'tp', hop) for part, hop in zip(parts, hops)]  5.88 us
    ppermute x3, starting transfers between devices, body(): parts = [lax.ppermute(part, 'tp', hop) for part, hop in zip(parts, hops)]  5.01 us
  transfers between devices with their start and end apart: 14, of which 5 were waited for; matrix products, arithmetic and copies ran while one was open for 0% of the time, Pallas kernels for 40%

profile of v4, /device:TPU:1, one launch (start us, length us, event | category | flops | bytes accessed | tf_op | source)
XLA Modules:
  0.0 115.2 jit_solution(17893008429824963412)
XLA Ops:
  1.3 4.8 %pack_queries.1 = (bf16[16,264,128]{2,1,0:T(8,128)(2,1)}, s32[40]{0:T(128)}, s32[40]{0:T(128)}) custom-call(s32[512]{0:T(512)} %decode_slot.3, s32[512]{0:T(512)} %lengths.1, s32[2]{0:T(128)} %pad_add_fusion.where, bf16[4,32,8,192]{3,2,1,0:T(8,128)(2,1)} %q_hbm.1, bf16[4,32,576]{2,1,0:T(8,128)(2,1)} %n_hbm.1), custom_call_target="tpu_custom_call" | custom-call | flops 1000 | bytes 1000 | tf_op jit(solution)/shard_map/pack_queries/pallas_call | solution.py:92
  6.1 7.6 %all-to-all-start = ((bf16[16,264,128]{2,1,0:T(8,128)(2,1)}), bf16[16,264,128]{2,1,0:T(8,128)(2,1)S(1)}, u32[]{:S(2)}, u32[]{:S(2)}) async-start(bf16[16,264,128]{2,1,0:T(8,128)(2,1)} %get-tuple-element.23), calls=%async_computation | async-start | bytes 2162688 | tf_op jit(solution)/shard_map/all_to_all | solution.py:586
  13.7 13.3 %pack_context.1 = (bf16[16,3,216,128]{3,2,1,0:T(8,128)(2,1)}, bf16[16,216,128]{2,1,0:T(8,128)(2,1)}, s32[32]{0:T(128)}) custom-call(s32[512]{0:T(512)} %decode_slot.3, s32[2]{0:T(128)} %pad_add_fusion.where, bf16[32,576,384]{2,1,0:T(8,128)(2,1)} %bitcast.3), custom_call_target="tpu_custom_call" | custom-call | flops 1000 | bytes 1000 | tf_op jit(solution)/shard_map/pack_context/pallas_call | solution.py:175
  27.0 3.0 %all-to-all-done.payload_hbm = bf16[16,264,128]{2,1,0:T(8,128)(2,1)S(1)} async-done(((bf16[16,264,128]{2,1,0:T(8,128)(2,1)}), bf16[16,264,128]{2,1,0:T(8,128)(2,1)S(1)}, u32[]{:S(2)}, u32[]{:S(2)}) %all-to-all-start) | async-done | bytes 1081376 | tf_op jit(solution)/shard_map/all_to_all | solution.py:586
  30.0 1.0 copy-done.7
  31.0 4.2 %all-to-all-start.1 = ((bf16[16,3,216,128]{3,2,1,0:T(8,128)(2,1)}), bf16[16,3,216,128]{3,2,1,0:T(8,128)(2,1)S(1)}, u32[]{:S(2)}, u32[]{:S(2)}) async-start(bf16[16,3,216,128]{3,2,1,0:T(8,128)(2,1)} %get-tuple-element.32), calls=%async_computation.1 | async-start | bytes 5308416 | tf_op jit(solution)/shard_map/all_to_all | solution.py:586
  35.3 21.5 %attention.1 = (bf16[64,2560]{1,0:T(8,128)(2,1)}, f32[64,2560]{1,0:T(8,128)}) custom-call(s32[32]{0:T(128)} %get-tuple-element.21.placing, s32[512]{0:T(512)} %lengths.1, s32[2]{0:T(128)} %pad_add_fusion.where, bf16[16,264,128]{2,1,0:T(8,128)(2,1)} %copy-done.7, bf16[32,576,384]{2,1,0:T(8,128)(2,1)} %bitcast.4, bf16[8,512,128]{2,1,0:T(8,128)(2,1)} %w_uk_hbm.1, ...), custom_call_target="tpu_custom_call" | custom-call | flops 1000 | bytes 1000 | tf_op jit(solution)/shard_map/attention/pallas_call | solution.py:414
  56.8 2.2 %collective-permute-start = (bf16[64,2560]{1,0:T(8,128)(2,1)}, bf16[64,2560]{1,0:T(8,128)(2,1)S(1)}, u32[]{:S(2)}, u32[]{:S(2)}) collective-permute-start(bf16[64,2560]{1,0:T(8,128)(2,1)} %get-tuple-element.27), channel_id=1, source_target_pairs={{0,1},{1,0},{2,3},{3,2},{4,5},{5,4},{6,7},{7,6},{8,9},{9,8},{10,11... | collective-permute-start | bytes 983048 | tf_op jit(solution)/shard_map/ppermute | solution.py:615
  59.0 1.5 %collective-permute-done.swapped = bf16[64,2560]{1,0:T(8,128)(2,1)S(1)} collective-permute-done((bf16[64,2560]{1,0:T(8,128)(2,1)}, bf16[64,2560]{1,0:T(8,128)(2,1)S(1)}, u32[]{:S(2)}, u32[]{:S(2)}) %collective-permute-start) | collective-permute-done | bytes 327712 | tf_op jit(solution)/shard_map/ppermute | solution.py:615
  60.5 1.1 copy-done.2
  62.2 1.7 %collective-permute-start.1 = (bf16[64,640]{1,0:T(8,128)(2,1)S(1)}, bf16[64,640]{1,0:T(8,128)(2,1)S(1)}, u32[]{:S(2)}, u32[]{:S(2)}) collective-permute-start(bf16[64,640]{1,0:T(8,128)(2,1)S(1)} %get-tuple-element.29), channel_id=1, source_target_pairs={{0,2},{1,3},{2,0},{3,1},{4,6},{5,7},{6,4},{7,5},{8,10},{9,11},{10,... | collective-permute-start | bytes 245768 | tf_op jit(solution)/shard_map/ppermute | solution.py:617
  63.9 3.3 %collective-permute-start.2 = (bf16[64,640]{1,0:T(8,128)(2,1)S(1)}, bf16[64,640]{1,0:T(8,128)(2,1)S(1)}, u32[]{:S(2)}, u32[]{:S(2)}) collective-permute-start(bf16[64,640]{1,0:T(8,128)(2,1)S(1)} %get-tuple-element.30), channel_id=1, source_target_pairs={{0,4},{1,5},{2,6},{3,7},{4,0},{5,1},{6,2},{7,3},{8,12},{9,13},{10,... | collective-permute-start | bytes 245768 | tf_op jit(solution)/shard_map/ppermute | solution.py:617
  67.2 3.9 %collective-permute-done.2.rest_1_ = bf16[64,640]{1,0:T(8,128)(2,1)S(1)} collective-permute-done((bf16[64,640]{1,0:T(8,128)(2,1)S(1)}, bf16[64,640]{1,0:T(8,128)(2,1)S(1)}, u32[]{:S(2)}, u32[]{:S(2)}) %collective-permute-start.2) | collective-permute-done | bytes 81952 | tf_op jit(solution)/shard_map/ppermute | solution.py:617
  71.2 1.9 %collective-permute-done.3.rest_2_ = bf16[64,640]{1,0:T(8,128)(2,1)S(1)} collective-permute-done((bf16[64,640]{1,0:T(8,128)(2,1)S(1)}, bf16[64,640]{1,0:T(8,128)(2,1)S(1)}, u32[]{:S(2)}, u32[]{:S(2)}) %collective-permute-start.3) | collective-permute-done | bytes 81952 | tf_op jit(solution)/shard_map/ppermute | solution.py:617
  74.1 1.0 copy-done
  75.0 6.9 %all-to-all-start.2 = ((bf16[16,256,128]{2,1,0:T(8,128)(2,1)}), bf16[16,256,128]{2,1,0:T(8,128)(2,1)}, u32[]{:S(2)}, u32[]{:S(2)}) async-start(bf16[16,256,128]{2,1,0:T(8,128)(2,1)} %copy-done), calls=%async_computation.2 | async-start | bytes 2097152 | tf_op jit(solution)/shard_map/all_to_all | solution.py:586
  82.0 7.1 %place_context.2.rest_0_ = bf16[32,48,576]{2,1,0:T(8,128)(2,1)} custom-call(s32[40]{0:T(128)S(1)} %copy-done.4, s32[40]{0:T(128)S(1)} %copy-done.6, s32[2]{0:T(128)S(1)} %copy-done.3, bf16[16,3,216,128]{3,2,1,0:T(8,128)(2,1)S(1)} %all-to-all-done.1.packed), custom_call_target="tpu_custom_call" | custom-call | flops 1000 | bytes 12000000 | tf_op jit(solution)/shard_map/place_context/pallas_call | solution.py:247
  89.1 8.6 %all-to-all-done.2.packed = bf16[16,256,128]{2,1,0:T(8,128)(2,1)} async-done(((bf16[16,256,128]{2,1,0:T(8,128)(2,1)}), bf16[16,256,128]{2,1,0:T(8,128)(2,1)}, u32[]{:S(2)}, u32[]{:S(2)}) %all-to-all-start.2) | async-done | bytes 1048608 | tf_op jit(solution)/shard_map/all_to_all | solution.py:586
  97.7 1.5 %unpack_back.1.rest_0_ = bf16[64,640]{1,0:T(8,128)(2,1)S(1)} custom-call(s32[40]{0:T(128)S(1)} %copy-done.4, bf16[16,256,128]{2,1,0:T(8,128)(2,1)} %all-to-all-done.2.packed), custom_call_target="tpu_custom_call" | custom-call | flops 1000 | bytes 1000 | tf_op jit(solution)/shard_map/unpack_back/pallas_call | solution.py:532
  100.1 3.0 %collective-permute-start.5 = (bf16[64,640]{1,0:T(8,128)(2,1)S(1)}, bf16[64,640]{1,0:T(8,128)(2,1)S(1)}, u32[]{:S(2)}, u32[]{:S(2)}) collective-permute-start(bf16[64,640]{1,0:T(8,128)(2,1)S(1)} %unpack_back.1.rest_0_), channel_id=1, source_target_pairs={{0,4},{1,5},{2,6},{3,7},{4,0},{5,1},{6,2},{7,3},{8,12},{9,13},{10,... | collective-permute-start | bytes 245768 | tf_op jit(solution)/shard_map/ppermute | solution.py:626
  103.2 3.7 %collective-permute-start.7 = (bf16[64,640]{1,0:T(8,128)(2,1)S(1)}, bf16[64,640]{1,0:T(8,128)(2,1)S(1)}, u32[]{:S(2)}, u32[]{:S(2)}) collective-permute-start(bf16[64,640]{1,0:T(8,128)(2,1)S(1)} %unpack_back.1.rest_0_), channel_id=1, source_target_pairs={{0,1},{1,0},{2,3},{3,2},{4,5},{5,4},{6,7},{7,6},{8,9},{9,8},{10,11... | collective-permute-start | bytes 245768 | tf_op jit(solution)/shard_map/ppermute | solution.py:627
  107.9 2.3 %collective-permute-start.9 = (bf16[64,640]{1,0:T(8,128)(2,1)S(1)}, bf16[64,640]{1,0:T(8,128)(2,1)S(1)}, u32[]{:S(2)}, u32[]{:S(2)}) collective-permute-start(bf16[64,640]{1,0:T(8,128)(2,1)S(1)} %collective-permute-done.5.rest_2_), channel_id=1, source_target_pairs={{0,1},{1,0},{2,3},{3,2},{4,5},{5,4},{6,7},{7,6},{8,9},{9,8},{10,11... | collective-permute-start | bytes 245768 | tf_op jit(solution)/shard_map/ppermute | solution.py:627
  110.2 3.1 %place_context.3 = bf16[32,48,576]{2,1,0:T(8,128)(2,1)} custom-call(s32[40]{0:T(128)S(1)} %copy-done.4, s32[40]{0:T(128)S(1)} %copy-done.6, s32[2]{0:T(128)S(1)} %copy-done.3, bf16[16,256,128]{2,1,0:T(8,128)(2,1)} %all-to-all-done.2.packed, bf16[32,48,576]{2,1,0:T(8,128)(2,1)} %place_context.2.rest_0_), custom_call_target="tpu_custom_call", output_to_operand_aliasing={{}: (4, {})} | custom-call | flops 1000 | bytes 1000 | tf_op jit(solution)/shard_map/place_context/pallas_call | solution.py:247
  113.3 1.9 %assemble.1 = bf16[32,4,2560]{2,1,0:T(4,128)(2,1)} custom-call(s32[2]{0:T(128)S(1)} %copy-done.3, bf16[64,640]{1,0:T(8,128)(2,1)S(1)} %unpack_back.1.rest_0_, bf16[64,640]{1,0:T(8,128)(2,1)S(1)} %collective-permute-done.4.rest_1_, bf16[64,640]{1,0:T(8,128)(2,1)S(1)} %collective-permute-done.5.rest_2_, bf16[64,640]{1,0:T(8,128)(2,1)S(1)} %collective-permute-done.6.rest_3_, ...), custom_call_target="tpu_custom_call" | custom-call | flops 1000 | bytes 1000 | tf_op jit(solution)/shard_map/assemble/pallas_call | solution.py:570
  (30 shorter events, 4.1 us)
Async XLA Ops:
  6.1 23.9 %all-to-all-start = ((bf16[16,264,128]{2,1,0:T(8,128)(2,1)}), bf16[16,264,128]{2,1,0:T(8,128)(2,1)S(1)}, u32[]{:S(2)}, u32[]{:S(2)}) async-start(bf16[16,264,128]{2,1,0:T(8,128)(2,1)} %get-tuple-element.23), calls=%async_computation | async-start | bytes 2162688 | tf_op jit(solution)/shard_map/all_to_all | solution.py:586
  30.0 1.0 copy-start.7
  31.0 44.1 %all-to-all-start.1 = ((bf16[16,3,216,128]{3,2,1,0:T(8,128)(2,1)}), bf16[16,3,216,128]{3,2,1,0:T(8,128)(2,1)S(1)}, u32[]{:S(2)}, u32[]{:S(2)}) async-start(bf16[16,3,216,128]{3,2,1,0:T(8,128)(2,1)} %get-tuple-element.32), calls=%async_computation.1 | async-start | bytes 5308416 | tf_op jit(solution)/shard_map/all_to_all | solution.py:586
  35.2 25.3 %copy-start.3 = (s32[2]{0:T(128)S(1)}, s32[2]{0:T(128)}, u32[]{:S(2)}) copy-start(s32[2]{0:T(128)} %pad_add_fusion.where) | copy-start | bytes 28
  35.2 37.9 %copy-start.1 = (bf16[16,216,128]{2,1,0:T(8,128)(2,1)S(1)}, bf16[16,216,128]{2,1,0:T(8,128)(2,1)}, u32[]{:S(2)}) copy-start(bf16[16,216,128]{2,1,0:T(8,128)(2,1)} %get-tuple-element.22.second) | copy-start | bytes 2654212
  35.3 37.9 %copy-start.5 = (s32[32]{0:T(128)S(1)}, s32[32]{0:T(128)}, u32[]{:S(2)}) copy-start(s32[32]{0:T(128)} %get-tuple-element.21.placing) | copy-start | bytes 388
  56.8 3.7 %collective-permute-start = (bf16[64,2560]{1,0:T(8,128)(2,1)}, bf16[64,2560]{1,0:T(8,128)(2,1)S(1)}, u32[]{:S(2)}, u32[]{:S(2)}) collective-permute-start(bf16[64,2560]{1,0:T(8,128)(2,1)} %get-tuple-element.27), channel_id=1, source_target_pairs={{0,1},{1,0},{2,3},{3,2},{4,5},{5,4},{6,7},{7,6},{8,9},{9,8},{10,11... | collective-permute-start | bytes 983048 | tf_op jit(solution)/shard_map/ppermute | solution.py:615
  60.5 1.1 copy-start.2
  61.6 20.4 %copy-start.4 = (s32[40]{0:T(128)S(1)}, s32[40]{0:T(128)}, u32[]{:S(2)}) copy-start(s32[40]{0:T(128)} %get-tuple-element.20.arrival) | copy-start | bytes 484
  61.6 20.4 %copy-start.6 = (s32[40]{0:T(128)S(1)}, s32[40]{0:T(128)}, u32[]{:S(2)}) copy-start(s32[40]{0:T(128)} %get-tuple-element.34.lengths) | copy-start | bytes 484
  62.2 5.0 %collective-permute-start.1 = (bf16[64,640]{1,0:T(8,128)(2,1)S(1)}, bf16[64,640]{1,0:T(8,128)(2,1)S(1)}, u32[]{:S(2)}, u32[]{:S(2)}) collective-permute-start(bf16[64,640]{1,0:T(8,128)(2,1)S(1)} %get-tuple-element.29), channel_id=1, source_target_pairs={{0,2},{1,3},{2,0},{3,1},{4,6},{5,7},{6,4},{7,5},{8,10},{9,11},{10,... | collective-permute-start | bytes 245768 | tf_op jit(solution)/shard_map/ppermute | solution.py:617
  63.9 7.2 %collective-permute-start.2 = (bf16[64,640]{1,0:T(8,128)(2,1)S(1)}, bf16[64,640]{1,0:T(8,128)(2,1)S(1)}, u32[]{:S(2)}, u32[]{:S(2)}) collective-permute-start(bf16[64,640]{1,0:T(8,128)(2,1)S(1)} %get-tuple-element.30), channel_id=1, source_target_pairs={{0,4},{1,5},{2,6},{3,7},{4,0},{5,1},{6,2},{7,3},{8,12},{9,13},{10,... | collective-permute-start | bytes 245768 | tf_op jit(solution)/shard_map/ppermute | solution.py:617
  67.2 5.9 %collective-permute-start.3 = (bf16[64,640]{1,0:T(8,128)(2,1)S(1)}, bf16[64,640]{1,0:T(8,128)(2,1)S(1)}, u32[]{:S(2)}, u32[]{:S(2)}) collective-permute-start(bf16[64,640]{1,0:T(8,128)(2,1)S(1)} %get-tuple-element.31), channel_id=1, source_target_pairs={{0,6},{1,7},{2,4},{3,5},{4,2},{5,3},{6,0},{7,1},{8,14},{9,15},{10,... | collective-permute-start | bytes 245768 | tf_op jit(solution)/shard_map/ppermute | solution.py:617
  74.1 1.0 copy-start
  75.0 22.6 %all-to-all-start.2 = ((bf16[16,256,128]{2,1,0:T(8,128)(2,1)}), bf16[16,256,128]{2,1,0:T(8,128)(2,1)}, u32[]{:S(2)}, u32[]{:S(2)}) async-start(bf16[16,256,128]{2,1,0:T(8,128)(2,1)} %copy-done), calls=%async_computation.2 | async-start | bytes 2097152 | tf_op jit(solution)/shard_map/all_to_all | solution.py:586
  99.2 7.7 %collective-permute-start.6 = (bf16[64,640]{1,0:T(8,128)(2,1)S(1)}, bf16[64,640]{1,0:T(8,128)(2,1)S(1)}, u32[]{:S(2)}, u32[]{:S(2)}) collective-permute-start(bf16[64,640]{1,0:T(8,128)(2,1)S(1)} %unpack_back.1.rest_0_), channel_id=1, source_target_pairs={{0,6},{1,7},{2,4},{3,5},{4,2},{5,3},{6,0},{7,1},{8,14},{9,15},{10,... | collective-permute-start | bytes 245768 | tf_op jit(solution)/shard_map/ppermute | solution.py:626
  100.1 7.7 %collective-permute-start.4 = (bf16[64,640]{1,0:T(8,128)(2,1)S(1)}, bf16[64,640]{1,0:T(8,128)(2,1)S(1)}, u32[]{:S(2)}, u32[]{:S(2)}) collective-permute-start(bf16[64,640]{1,0:T(8,128)(2,1)S(1)} %unpack_back.1.rest_0_), channel_id=1, source_target_pairs={{0,2},{1,3},{2,0},{3,1},{4,6},{5,7},{6,4},{7,5},{8,10},{9,11},{10,... | collective-permute-start | bytes 245768 | tf_op jit(solution)/shard_map/ppermute | solution.py:626
  100.1 7.7 %collective-permute-start.5 = (bf16[64,640]{1,0:T(8,128)(2,1)S(1)}, bf16[64,640]{1,0:T(8,128)(2,1)S(1)}, u32[]{:S(2)}, u32[]{:S(2)}) collective-permute-start(bf16[64,640]{1,0:T(8,128)(2,1)S(1)} %unpack_back.1.rest_0_), channel_id=1, source_target_pairs={{0,4},{1,5},{2,6},{3,7},{4,0},{5,1},{6,2},{7,3},{8,12},{9,13},{10,... | collective-permute-start | bytes 245768 | tf_op jit(solution)/shard_map/ppermute | solution.py:626
  103.2 10.1 %collective-permute-start.7 = (bf16[64,640]{1,0:T(8,128)(2,1)S(1)}, bf16[64,640]{1,0:T(8,128)(2,1)S(1)}, u32[]{:S(2)}, u32[]{:S(2)}) collective-permute-start(bf16[64,640]{1,0:T(8,128)(2,1)S(1)} %unpack_back.1.rest_0_), channel_id=1, source_target_pairs={{0,1},{1,0},{2,3},{3,2},{4,5},{5,4},{6,7},{7,6},{8,9},{9,8},{10,11... | collective-permute-start | bytes 245768 | tf_op jit(solution)/shard_map/ppermute | solution.py:627
  106.9 6.4 %collective-permute-start.10 = (bf16[64,640]{1,0:T(8,128)(2,1)S(1)}, bf16[64,640]{1,0:T(8,128)(2,1)S(1)}, u32[]{:S(2)}, u32[]{:S(2)}) collective-permute-start(bf16[64,640]{1,0:T(8,128)(2,1)S(1)} %collective-permute-done.6.rest_3_), channel_id=1, source_target_pairs={{0,1},{1,0},{2,3},{3,2},{4,5},{5,4},{6,7},{7,6},{8,9},{9,8},{10,11... | collective-permute-start | bytes 245768 | tf_op jit(solution)/shard_map/ppermute | solution.py:627
  107.8 5.5 %collective-permute-start.8 = (bf16[64,640]{1,0:T(8,128)(2,1)S(1)}, bf16[64,640]{1,0:T(8,128)(2,1)S(1)}, u32[]{:S(2)}, u32[]{:S(2)}) collective-permute-start(bf16[64,640]{1,0:T(8,128)(2,1)S(1)} %collective-permute-done.4.rest_1_), channel_id=1, source_target_pairs={{0,1},{1,0},{2,3},{3,2},{4,5},{5,4},{6,7},{7,6},{8,9},{9,8},{10,11... | collective-permute-start | bytes 245768 | tf_op jit(solution)/shard_map/ppermute | solution.py:627
  107.9 5.5 %collective-permute-start.9 = (bf16[64,640]{1,0:T(8,128)(2,1)S(1)}, bf16[64,640]{1,0:T(8,128)(2,1)S(1)}, u32[]{:S(2)}, u32[]{:S(2)}) collective-permute-start(bf16[64,640]{1,0:T(8,128)(2,1)S(1)} %collective-permute-done.5.rest_2_), channel_id=1, source_target_pairs={{0,1},{1,0},{2,3},{3,2},{4,5},{5,4},{6,7},{7,6},{8,9},{9,8},{10,11... | collective-permute-start | bytes 245768 | tf_op jit(solution)/shard_map/ppermute | solution.py:627

commit v5 on v4

--- a/solution.py
+++ b/solution.py
@@ -11,7 +11,6 @@
 ROPE = 64
 NOPE = 128
 CAP = 4
-FIRST_RANKS = 3
 GROUP = 4
 FLOOR = -1e30
 BF16 = jnp.bfloat16
@@ -112,11 +111,11 @@
 
 
 def pack_context_kernel(
-    decode_slot, where, p_ref, first_ref, second_ref, placing, counts, buf, sems
+    decode_slot, where, p_ref, out_ref, placing, counts, buf, sems
 ):
     slots, feature, window = buf.shape
     blocks = feature // 128
-    piece = first_ref.shape[2] * 128 // feature
+    piece = out_ref.shape[2] * 128 // feature
     chunk = slots // sems.shape[0]
     row = where[0] * piece
     start = pl.multiple_of(jnp.where(row + piece > window, p_ref.shape[2] - window, 0), 128)
@@ -152,18 +151,9 @@
             turned = lax.dot_general(pick, buf[g], NT, preferred_element_type=F32)
             last = turned[:, 128 * blocks :]
             last = jnp.concatenate([last[: piece // 2], last[piece // 2 :]], axis=1)
-            cell = jnp.concatenate(
+            out_ref[dest, rank] = jnp.concatenate(
                 [turned[:, 128 * b : 128 * b + 128] for b in range(blocks)] + [last], axis=0
             ).astype(BF16)
-
-            @pl.when(rank < FIRST_RANKS)
-            def _():
-                first_ref[dest, rank] = cell
-
-            @pl.when(rank >= FIRST_RANKS)
-            def _():
-                second_ref[dest] = cell
-
             return carry
 
         lax.fori_loop(0, chunk, one, 0, unroll=2)
@@ -175,12 +165,11 @@
     return pl.pallas_call(
         pack_context_kernel,
         out_shape=(
-            jax.ShapeDtypeStruct((pool_count, FIRST_RANKS, rows, 128), BF16),
-            jax.ShapeDtypeStruct((pool_count, rows, 128), BF16),
+            jax.ShapeDtypeStruct((pool_count, CAP, rows, 128), BF16),
             jax.ShapeDtypeStruct((slots,), jnp.int32),
         ),
         in_specs=[SMEM_SPEC, SMEM_SPEC, ANY_SPEC],
-        out_specs=(VMEM_SPEC, VMEM_SPEC, SMEM_SPEC),
+        out_specs=(VMEM_SPEC, SMEM_SPEC),
         scratch_shapes=[
             pltpu.SMEM((pool_count,), jnp.int32),
             pltpu.VMEM((slots, feature, 256), BF16),
@@ -202,30 +191,20 @@
     return jnp.where(position < length, whole.astype(F32), 0.0).astype(BF16)
 
 
-def place_kernel(low, high, arrival, lengths, where, packed, *rest):
-    out_ref, inbox, outbox, in_sems, out_sems = rest[-5:]
+def place_kernel(arrival, lengths, where, packed, out_ref, inbox, outbox, in_sems, out_sems):
     slots, piece, feature = out_ref.shape
     first_row = where[0] * piece
 
     def copy_in(j):
         owner, rank = split(arrival[j])
-        if high - low == 1:
-            source = packed.at[owner]
-        else:
-            source = packed.at[owner, jnp.clip(rank - low, 0, high - low - 1)]
-        return pltpu.make_async_copy(source, inbox.at[j], in_sems.at[j])
+        return pltpu.make_async_copy(packed.at[owner, rank], inbox.at[j], in_sems.at[j])
 
     def copy_out(j):
         return pltpu.make_async_copy(outbox.at[j], out_ref.at[j], out_sems.at[j])
 
     def each(action):
         def step(j, carry):
-            rank = split(arrival[j])[1]
-
-            @pl.when((rank >= low) & (rank < high))
-            def _():
-                action(j)
-
+            action(j)
             return carry
 
         lax.fori_loop(0, slots, step, 0)
@@ -240,14 +219,13 @@
     each(lambda j: copy_out(j).wait())
 
 
-def place(low, high, arrival, lengths, where, packed, piece, feature, context=None):
+def place(arrival, lengths, where, packed, piece, feature):
     slots = arrival.shape[0] - 8
     rows = packed.shape[-2]
-    args = [arrival, lengths, where, packed] + ([] if context is None else [context])
-    return pl.pallas_call(
-        functools.partial(place_kernel, low, high),
+    return pl.pallas_call(
+        place_kernel,
         out_shape=jax.ShapeDtypeStruct((slots, piece, feature), BF16),
-        in_specs=[SMEM_SPEC] * 3 + [ANY_SPEC] * (len(args) - 3),
+        in_specs=[SMEM_SPEC] * 3 + [ANY_SPEC],
         out_specs=ANY_SPEC,
         scratch_shapes=[
             pltpu.VMEM((slots, rows, 128), BF16),
@@ -255,11 +233,10 @@
             pltpu.SemaphoreType.DMA((slots,)),
             pltpu.SemaphoreType.DMA((slots,)),
         ],
-        input_output_aliases={} if context is None else {4: 0},
         compiler_params=params(),
-        cost_estimate=cost(bytes_accessed=12_000_000 if context is None else 1000),
+        cost_estimate=cost(bytes_accessed=12_000_000),
         name="place_context",
-    )(*args)
+    )(arrival, lengths, where, packed)
 
 
 def attention_kernel(
@@ -464,18 +441,16 @@
     )(where, kept, swapped)
 
 
-def pack_back_kernel(placing, second, mine, *rest):
+def pack_back_kernel(placing, mine, *rest):
     parts, (out_ref, total, rows) = rest[:-3], rest[-3:]
     slots = placing.shape[0]
     blocks = mine.shape[1] // 128
     steps = mine.shape[0] // slots
-    context_rows = second.shape[1]
     whole = mine[...]
     for part in parts:
         whole = whole + part[...].astype(F32)
     for b in range(blocks):
         total[b] = whole[:, 128 * b : 128 * b + 128]
-    out_ref[:, :context_rows, :] = second[...]
     rows[...] = jnp.zeros(rows.shape, F32)
 
     def one(i, carry):
@@ -487,18 +462,15 @@
         return carry
 
     lax.fori_loop(0, slots, one, 0, unroll=4)
-    out_ref[:, context_rows:, :] = (
-        rows[...].reshape(out_ref.shape[0], 8 * blocks, 128).astype(BF16)
-    )
-
-
-def pack_back(placing, second, mine, parts):
-    pool_count, context_rows, _ = second.shape
+    out_ref[...] = rows[...].reshape(out_ref.shape).astype(BF16)
+
+
+def pack_back(placing, mine, parts, pool_count):
     blocks = mine.shape[1] // 128
     return pl.pallas_call(
         pack_back_kernel,
-        out_shape=jax.ShapeDtypeStruct((pool_count, context_rows + 8 * blocks, 128), BF16),
-        in_specs=[SMEM_SPEC] + [VMEM_SPEC] * (2 + len(parts)),
+        out_shape=jax.ShapeDtypeStruct((pool_count, 8 * blocks, 128), BF16),
+        in_specs=[SMEM_SPEC] + [VMEM_SPEC] * (1 + len(parts)),
         out_specs=VMEM_SPEC,
         scratch_shapes=[
             pltpu.VMEM((blocks, mine.shape[0], 128), F32),
@@ -507,14 +479,13 @@
         compiler_params=params(),
         cost_estimate=cost(),
         name="pack_back",
-    )(placing, second, mine, *parts)
+    )(placing, mine, *parts)
 
 
 def unpack_back_kernel(steps, arrival, packed, out_ref, rows, total):
     slots = out_ref.shape[0] // steps
     blocks = out_ref.shape[1] // 128
-    first = packed.shape[1] - 8 * blocks
-    rows[...] = packed[:, first:, :].astype(F32).reshape(rows.shape)
+    rows[...] = packed[...].astype(F32).reshape(rows.shape)
 
     def one(j, carry):
         owner, rank = split(arrival[j])
@@ -604,7 +575,7 @@
         decode_slot, prompt_lengths, where, queries, new_latent, pool_count
     )
     payload = exchange(payload)
-    first, second, placing = pack_context(decode_slot, where, latent_t, piece, pool_count)
+    first, placing = pack_context(decode_slot, where, latent_t, piece, pool_count)
     payload, first = lax.optimization_barrier((payload, first))
     first = exchange(first)
 
@@ -616,16 +587,15 @@
     mine, *parts = share(where, kept, swapped, z_count)
     parts = [lax.ppermute(part, "tp", hop) for part, hop in zip(parts, hops)]
 
-    back = pack_back(placing, second, mine, parts)
+    back = pack_back(placing, mine, parts, pool_count)
     back, first = lax.optimization_barrier((back, first))
     back = exchange(back)
-    context = place(0, FIRST_RANKS, arrival, lengths, where, first, piece, feature)
+    context = place(arrival, lengths, where, first, piece, feature)
     back, context = lax.optimization_barrier((back, context))
 
     own = unpack_back(arrival, back, steps // 2, slots, out_width // z_count)
     parts = [own] + [lax.ppermute(own, "tp", hop) for hop in hops]
     parts = parts + [lax.ppermute(part, "tp", swap) for part in parts]
-    context = place(FIRST_RANKS, CAP, arrival, lengths, where, back, piece, feature, context)
     decoded = assemble(where, parts, slots, steps, out_width)
     return decoded, context
 

time: 116 us -> 114 us (0.983)
  Pallas kernels: 54.8 us -> 47.5 us
  waiting for transfers between devices: 18.9 us -> 24.2 us
    all_to_all x3, waiting for transfers between devices: 11.6 us -> 16 us  [exchange(): return lax.all_to_all(x, 'pool', split_axis=0, concat_axis=0, tiled=True)]
    pallas_call x1, Pallas kernels: 13.3 us -> 9.89 us  [pack_context(): pl.pallas_call(pack_context_kernel, out_shape=(jax.ShapeDtypeStruct((pool...]
    pallas_call x2 -> x1, Pallas kernels: 10.2 us -> 6.9 us  [place(): pl.pallas_call(place_kernel, out_shape=jax.ShapeDtypeStruct((slots, piece...]
    all_to_all x3, starting transfers between devices: 18.8 us -> 16 us  [exchange(): return lax.all_to_all(x, 'pool', split_axis=0, concat_axis=0, tiled=True)]
    ppermute x4, starting transfers between devices: 7.02 us -> 9.35 us  [body(): parts = parts + [lax.ppermute(part, 'tp', swap) for part in parts]]
    ppermute x3, starting transfers between devices: 3.94 us -> 5.11 us  [body(): parts = [own] + [lax.ppermute(own, 'tp', hop) for hop in hops]]
    unnamed x16 -> x14, local copies, waits for them, and re-layouts: 3.06 us -> 2.75 us
  transfers between devices with their start and end apart: 14 -> 14, of which waited for: 5 -> 7; matrix products, arithmetic and copies ran while one was open for 0% -> 0% of each run, Pallas kernels for 40% -> 35%
where the time goes in v5:
time: 114 us
  Pallas kernels  47.5 us (42%)
  starting transfers between devices  37.8 us (33%)
  waiting for transfers between devices  24.2 us (21%)
  local copies, waits for them, and re-layouts  2.75 us (2%)
    pallas_call x1, Pallas kernels, attention(): pl.pallas_call(attention_kernel, out_shape=(jax.ShapeDtypeStruct((half, w...  21.3 us
    all_to_all x3, starting transfers between devices, exchange(): return lax.all_to_all(x, 'pool', split_axis=0, concat_axis=0, tiled=True)  16 us
    all_to_all x3, waiting for transfers between devices, exchange(): return lax.all_to_all(x, 'pool', split_axis=0, concat_axis=0, tiled=True)  16 us
    pallas_call x1, Pallas kernels, pack_context(): pl.pallas_call(pack_context_kernel, out_shape=(jax.ShapeDtypeStruct((pool...  9.89 us
    ppermute x4, starting transfers between devices, body(): parts = parts + [lax.ppermute(part, 'tp', swap) for part in parts]  9.35 us
    pallas_call x1, Pallas kernels, place(): pl.pallas_call(place_kernel, out_shape=jax.ShapeDtypeStruct((slots, piece...  6.9 us
    ppermute x3, waiting for transfers between devices, body(): parts = [lax.ppermute(part, 'tp', hop) for part, hop in zip(parts, hops)]  5.88 us
    ppermute x3, starting transfers between devices, body(): parts = [own] + [lax.ppermute(own, 'tp', hop) for hop in hops]  5.11 us
  transfers between devices with their start and end apart: 14, of which 7 were waited for; matrix products, arithmetic and copies ran while one was open for 0% of the time, Pallas kernels for 35%

profile of v5, /device:TPU:1, one launch (start us, length us, event | category | flops | bytes accessed | tf_op | source)
XLA Modules:
  0.0 113.6 jit_solution(436303412895015413)
XLA Ops:
  1.2 4.8 %pack_queries.1 = (bf16[16,264,128]{2,1,0:T(8,128)(2,1)}, s32[40]{0:T(128)}, s32[40]{0:T(128)}) custom-call(s32[512]{0:T(512)} %decode_slot.3, s32[512]{0:T(512)} %lengths.1, s32[2]{0:T(128)} %pad_add_fusion.where, bf16[4,32,8,192]{3,2,1,0:T(8,128)(2,1)} %q_hbm.1, bf16[4,32,576]{2,1,0:T(8,128)(2,1)} %n_hbm.1), custom_call_target="tpu_custom_call" | custom-call | flops 1000 | bytes 1000 | tf_op jit(solution)/shard_map/pack_queries/pallas_call | solution.py:91
  6.0 7.6 %all-to-all-start = ((bf16[16,264,128]{2,1,0:T(8,128)(2,1)}), bf16[16,264,128]{2,1,0:T(8,128)(2,1)S(1)}, u32[]{:S(2)}, u32[]{:S(2)}) async-start(bf16[16,264,128]{2,1,0:T(8,128)(2,1)} %get-tuple-element.21), calls=%async_computation | async-start | bytes 2162688 | tf_op jit(solution)/shard_map/all_to_all | solution.py:557
  13.6 9.9 %pack_context.1 = (bf16[16,4,216,128]{3,2,1,0:T(8,128)(2,1)}, s32[32]{0:T(128)}) custom-call(s32[512]{0:T(512)} %decode_slot.3, s32[2]{0:T(128)} %pad_add_fusion.where, bf16[32,576,384]{2,1,0:T(8,128)(2,1)} %bitcast.3), custom_call_target="tpu_custom_call" | custom-call | flops 1000 | bytes 1000 | tf_op jit(solution)/shard_map/pack_context/pallas_call | solution.py:165
  23.5 6.4 %all-to-all-done.payload_hbm = bf16[16,264,128]{2,1,0:T(8,128)(2,1)S(1)} async-done(((bf16[16,264,128]{2,1,0:T(8,128)(2,1)}), bf16[16,264,128]{2,1,0:T(8,128)(2,1)S(1)}, u32[]{:S(2)}, u32[]{:S(2)}) %all-to-all-start) | async-done | bytes 1081376 | tf_op jit(solution)/shard_map/all_to_all | solution.py:557
  29.9 1.0 copy-done.6
  30.9 4.2 %all-to-all-start.1 = ((bf16[16,4,216,128]{3,2,1,0:T(8,128)(2,1)}), bf16[16,4,216,128]{3,2,1,0:T(8,128)(2,1)S(1)}, u32[]{:S(2)}, u32[]{:S(2)}) async-start(bf16[16,4,216,128]{3,2,1,0:T(8,128)(2,1)} %get-tuple-element.30), calls=%async_computation.1 | async-start | bytes 7077888 | tf_op jit(solution)/shard_map/all_to_all | solution.py:557
  35.2 21.3 %attention.1 = (bf16[64,2560]{1,0:T(8,128)(2,1)}, f32[64,2560]{1,0:T(8,128)}) custom-call(s32[32]{0:T(128)} %get-tuple-element.20.placing, s32[512]{0:T(512)} %lengths.1, s32[2]{0:T(128)} %pad_add_fusion.where, bf16[16,264,128]{2,1,0:T(8,128)(2,1)} %copy-done.6, bf16[32,576,384]{2,1,0:T(8,128)(2,1)} %bitcast.4, bf16[8,512,128]{2,1,0:T(8,128)(2,1)} %w_uk_hbm.1, ...), custom_call_target="tpu_custom_call" | custom-call | flops 1000 | bytes 1000 | tf_op jit(solution)/shard_map/attention/pallas_call | solution.py:391
  56.6 2.3 %collective-permute-start = (bf16[64,2560]{1,0:T(8,128)(2,1)}, bf16[64,2560]{1,0:T(8,128)(2,1)S(1)}, u32[]{:S(2)}, u32[]{:S(2)}) collective-permute-start(bf16[64,2560]{1,0:T(8,128)(2,1)} %get-tuple-element.25), channel_id=1, source_target_pairs={{0,1},{1,0},{2,3},{3,2},{4,5},{5,4},{6,7},{7,6},{8,9},{9,8},{10,11... | collective-permute-start | bytes 983048 | tf_op jit(solution)/shard_map/ppermute | solution.py:586
  58.8 1.5 %collective-permute-done.swapped = bf16[64,2560]{1,0:T(8,128)(2,1)S(1)} collective-permute-done((bf16[64,2560]{1,0:T(8,128)(2,1)}, bf16[64,2560]{1,0:T(8,128)(2,1)S(1)}, u32[]{:S(2)}, u32[]{:S(2)}) %collective-permute-start) | collective-permute-done | bytes 327712 | tf_op jit(solution)/shard_map/ppermute | solution.py:586
  60.3 1.1 copy-done
  62.0 1.7 %collective-permute-start.1 = (bf16[64,640]{1,0:T(8,128)(2,1)S(1)}, bf16[64,640]{1,0:T(8,128)(2,1)S(1)}, u32[]{:S(2)}, u32[]{:S(2)}) collective-permute-start(bf16[64,640]{1,0:T(8,128)(2,1)S(1)} %get-tuple-element.27), channel_id=1, source_target_pairs={{0,2},{1,3},{2,0},{3,1},{4,6},{5,7},{6,4},{7,5},{8,10},{9,11},{10,... | collective-permute-start | bytes 245768 | tf_op jit(solution)/shard_map/ppermute | solution.py:588
  63.7 3.3 %collective-permute-start.2 = (bf16[64,640]{1,0:T(8,128)(2,1)S(1)}, bf16[64,640]{1,0:T(8,128)(2,1)S(1)}, u32[]{:S(2)}, u32[]{:S(2)}) collective-permute-start(bf16[64,640]{1,0:T(8,128)(2,1)S(1)} %get-tuple-element.28), channel_id=1, source_target_pairs={{0,4},{1,5},{2,6},{3,7},{4,0},{5,1},{6,2},{7,3},{8,12},{9,13},{10,... | collective-permute-start | bytes 245768 | tf_op jit(solution)/shard_map/ppermute | solution.py:588
  67.0 3.9 %collective-permute-done.2.rest_1_ = bf16[64,640]{1,0:T(8,128)(2,1)S(1)} collective-permute-done((bf16[64,640]{1,0:T(8,128)(2,1)S(1)}, bf16[64,640]{1,0:T(8,128)(2,1)S(1)}, u32[]{:S(2)}, u32[]{:S(2)}) %collective-permute-start.2) | collective-permute-done | bytes 81952 | tf_op jit(solution)/shard_map/ppermute | solution.py:588
  71.0 1.9 %collective-permute-done.3.rest_2_ = bf16[64,640]{1,0:T(8,128)(2,1)S(1)} collective-permute-done((bf16[64,640]{1,0:T(8,128)(2,1)S(1)}, bf16[64,640]{1,0:T(8,128)(2,1)S(1)}, u32[]{:S(2)}, u32[]{:S(2)}) %collective-permute-start.3) | collective-permute-done | bytes 81952 | tf_op jit(solution)/shard_map/ppermute | solution.py:588
  74.5 9.4 %all-to-all-done.1.packed = bf16[16,4,216,128]{3,2,1,0:T(8,128)(2,1)S(1)} async-done(((bf16[16,4,216,128]{3,2,1,0:T(8,128)(2,1)}), bf16[16,4,216,128]{3,2,1,0:T(8,128)(2,1)S(1)}, u32[]{:S(2)}, u32[]{:S(2)}) %all-to-all-start.1) | async-done | bytes 3538976 | tf_op jit(solution)/shard_map/all_to_all | solution.py:557
  83.9 4.2 %all-to-all-start.2 = ((bf16[16,40,128]{2,1,0:T(8,128)(2,1)}), bf16[16,40,128]{2,1,0:T(8,128)(2,1)}, u32[]{:S(2)}, u32[]{:S(2)}) async-start(bf16[16,40,128]{2,1,0:T(8,128)(2,1)} %copy-done.1), calls=%async_computation.2 | async-start | bytes 327680 | tf_op jit(solution)/shard_map/all_to_all | solution.py:557
  88.1 6.9 %place_context.1 = bf16[32,48,576]{2,1,0:T(8,128)(2,1)} custom-call(s32[40]{0:T(128)S(1)} %copy-done.3, s32[40]{0:T(128)S(1)} %copy-done.5, s32[2]{0:T(128)S(1)} %copy-done.2, bf16[16,4,216,128]{3,2,1,0:T(8,128)(2,1)S(1)} %all-to-all-done.1.packed), custom_call_target="tpu_custom_call" | custom-call | flops 1000 | bytes 12000000 | tf_op jit(solution)/shard_map/place_context/pallas_call | solution.py:225
  95.1 1.2 %unpack_back.1.rest_0_ = bf16[64,640]{1,0:T(8,128)(2,1)S(1)} custom-call(s32[40]{0:T(128)S(1)} %copy-done.3, bf16[16,40,128]{2,1,0:T(8,128)(2,1)} %all-to-all-done.2.packed), custom_call_target="tpu_custom_call" | custom-call | flops 1000 | bytes 1000 | tf_op jit(solution)/shard_map/unpack_back/pallas_call | solution.py:503
  96.4 3.8 %collective-permute-start.6 = (bf16[64,640]{1,0:T(8,128)(2,1)S(1)}, bf16[64,640]{1,0:T(8,128)(2,1)S(1)}, u32[]{:S(2)}, u32[]{:S(2)}) collective-permute-start(bf16[64,640]{1,0:T(8,128)(2,1)S(1)} %unpack_back.1.rest_0_), channel_id=1, source_target_pairs={{0,6},{1,7},{2,4},{3,5},{4,2},{5,3},{6,0},{7,1},{8,14},{9,15},{10,... | collective-permute-start | bytes 245768 | tf_op jit(solution)/shard_map/ppermute | solution.py:597
  100.2 1.3 %collective-permute-start.5 = (bf16[64,640]{1,0:T(8,128)(2,1)S(1)}, bf16[64,640]{1,0:T(8,128)(2,1)S(1)}, u32[]{:S(2)}, u32[]{:S(2)}) collective-permute-start(bf16[64,640]{1,0:T(8,128)(2,1)S(1)} %unpack_back.1.rest_0_), channel_id=1, source_target_pairs={{0,4},{1,5},{2,6},{3,7},{4,0},{5,1},{6,2},{7,3},{8,12},{9,13},{10,... | collective-permute-start | bytes 245768 | tf_op jit(solution)/shard_map/ppermute | solution.py:597
  101.5 5.0 %collective-permute-start.7 = (bf16[64,640]{1,0:T(8,128)(2,1)S(1)}, bf16[64,640]{1,0:T(8,128)(2,1)S(1)}, u32[]{:S(2)}, u32[]{:S(2)}) collective-permute-start(bf16[64,640]{1,0:T(8,128)(2,1)S(1)} %unpack_back.1.rest_0_), channel_id=1, source_target_pairs={{0,1},{1,0},{2,3},{3,2},{4,5},{5,4},{6,7},{7,6},{8,9},{9,8},{10,11... | collective-permute-start | bytes 245768 | tf_op jit(solution)/shard_map/ppermute | solution.py:598
  107.3 2.0 %collective-permute-start.8 = (bf16[64,640]{1,0:T(8,128)(2,1)S(1)}, bf16[64,640]{1,0:T(8,128)(2,1)S(1)}, u32[]{:S(2)}, u32[]{:S(2)}) collective-permute-start(bf16[64,640]{1,0:T(8,128)(2,1)S(1)} %collective-permute-done.4.rest_1_), channel_id=1, source_target_pairs={{0,1},{1,0},{2,3},{3,2},{4,5},{5,4},{6,7},{7,6},{8,9},{9,8},{10,11... | collective-permute-start | bytes 245768 | tf_op jit(solution)/shard_map/ppermute | solution.py:598
  109.3 1.5 %collective-permute-start.9 = (bf16[64,640]{1,0:T(8,128)(2,1)S(1)}, bf16[64,640]{1,0:T(8,128)(2,1)S(1)}, u32[]{:S(2)}, u32[]{:S(2)}) collective-permute-start(bf16[64,640]{1,0:T(8,128)(2,1)S(1)} %collective-permute-done.5.rest_2_), channel_id=1, source_target_pairs={{0,1},{1,0},{2,3},{3,2},{4,5},{5,4},{6,7},{7,6},{8,9},{9,8},{10,11... | collective-permute-start | bytes 245768 | tf_op jit(solution)/shard_map/ppermute | solution.py:598
  111.8 1.9 %assemble.1 = bf16[32,4,2560]{2,1,0:T(4,128)(2,1)} custom-call(s32[2]{0:T(128)S(1)} %copy-done.2, bf16[64,640]{1,0:T(8,128)(2,1)S(1)} %unpack_back.1.rest_0_, bf16[64,640]{1,0:T(8,128)(2,1)S(1)} %collective-permute-done.4.rest_1_, bf16[64,640]{1,0:T(8,128)(2,1)S(1)} %collective-permute-done.5.rest_2_, bf16[64,640]{1,0:T(8,128)(2,1)S(1)} %collective-permute-done.6.rest_3_, ...), custom_call_target="tpu_custom_call" | custom-call | flops 1000 | bytes 1000 | tf_op jit(solution)/shard_map/assemble/pallas_call | solution.py:541
  (27 shorter events, 4.7 us)
Async XLA Ops:
  6.0 23.9 %all-to-all-start = ((bf16[16,264,128]{2,1,0:T(8,128)(2,1)}), bf16[16,264,128]{2,1,0:T(8,128)(2,1)S(1)}, u32[]{:S(2)}, u32[]{:S(2)}) async-start(bf16[16,264,128]{2,1,0:T(8,128)(2,1)} %get-tuple-element.21), calls=%async_computation | async-start | bytes 2162688 | tf_op jit(solution)/shard_map/all_to_all | solution.py:557
  29.9 1.0 copy-start.6
  30.9 53.0 %all-to-all-start.1 = ((bf16[16,4,216,128]{3,2,1,0:T(8,128)(2,1)}), bf16[16,4,216,128]{3,2,1,0:T(8,128)(2,1)S(1)}, u32[]{:S(2)}, u32[]{:S(2)}) async-start(bf16[16,4,216,128]{3,2,1,0:T(8,128)(2,1)} %get-tuple-element.30), calls=%async_computation.1 | async-start | bytes 7077888 | tf_op jit(solution)/shard_map/all_to_all | solution.py:557
  35.2 25.1 %copy-start.2 = (s32[2]{0:T(128)S(1)}, s32[2]{0:T(128)}, u32[]{:S(2)}) copy-start(s32[2]{0:T(128)} %pad_add_fusion.where) | copy-start | bytes 28
  35.2 37.7 %copy-start.4 = (s32[32]{0:T(128)S(1)}, s32[32]{0:T(128)}, u32[]{:S(2)}) copy-start(s32[32]{0:T(128)} %get-tuple-element.20.placing) | copy-start | bytes 388
  35.2 52.9 %copy-start.3 = (s32[40]{0:T(128)S(1)}, s32[40]{0:T(128)}, u32[]{:S(2)}) copy-start(s32[40]{0:T(128)} %get-tuple-element.19.arrival) | copy-start | bytes 484
  35.2 52.9 %copy-start.5 = (s32[40]{0:T(128)S(1)}, s32[40]{0:T(128)}, u32[]{:S(2)}) copy-start(s32[40]{0:T(128)} %get-tuple-element.32.lengths) | copy-start | bytes 484
  56.6 3.7 %collective-permute-start = (bf16[64,2560]{1,0:T(8,128)(2,1)}, bf16[64,2560]{1,0:T(8,128)(2,1)S(1)}, u32[]{:S(2)}, u32[]{:S(2)}) collective-permute-start(bf16[64,2560]{1,0:T(8,128)(2,1)} %get-tuple-element.25), channel_id=1, source_target_pairs={{0,1},{1,0},{2,3},{3,2},{4,5},{5,4},{6,7},{7,6},{8,9},{9,8},{10,11... | collective-permute-start | bytes 983048 | tf_op jit(solution)/shard_map/ppermute | solution.py:586
  60.3 1.1 copy-start
  62.0 5.0 %collective-permute-start.1 = (bf16[64,640]{1,0:T(8,128)(2,1)S(1)}, bf16[64,640]{1,0:T(8,128)(2,1)S(1)}, u32[]{:S(2)}, u32[]{:S(2)}) collective-permute-start(bf16[64,640]{1,0:T(8,128)(2,1)S(1)} %get-tuple-element.27), channel_id=1, source_target_pairs={{0,2},{1,3},{2,0},{3,1},{4,6},{5,7},{6,4},{7,5},{8,10},{9,11},{10,... | collective-permute-start | bytes 245768 | tf_op jit(solution)/shard_map/ppermute | solution.py:588
  63.7 7.3 %collective-permute-start.2 = (bf16[64,640]{1,0:T(8,128)(2,1)S(1)}, bf16[64,640]{1,0:T(8,128)(2,1)S(1)}, u32[]{:S(2)}, u32[]{:S(2)}) collective-permute-start(bf16[64,640]{1,0:T(8,128)(2,1)S(1)} %get-tuple-element.28), channel_id=1, source_target_pairs={{0,4},{1,5},{2,6},{3,7},{4,0},{5,1},{6,2},{7,3},{8,12},{9,13},{10,... | collective-permute-start | bytes 245768 | tf_op jit(solution)/shard_map/ppermute | solution.py:588
  67.0 5.9 %collective-permute-start.3 = (bf16[64,640]{1,0:T(8,128)(2,1)S(1)}, bf16[64,640]{1,0:T(8,128)(2,1)S(1)}, u32[]{:S(2)}, u32[]{:S(2)}) collective-permute-start(bf16[64,640]{1,0:T(8,128)(2,1)S(1)} %get-tuple-element.29), channel_id=1, source_target_pairs={{0,6},{1,7},{2,4},{3,5},{4,2},{5,3},{6,0},{7,1},{8,14},{9,15},{10,... | collective-permute-start | bytes 245768 | tf_op jit(solution)/shard_map/ppermute | solution.py:588
  73.8 0.7 copy-start.1
  83.9 11.2 %all-to-all-start.2 = ((bf16[16,40,128]{2,1,0:T(8,128)(2,1)}), bf16[16,40,128]{2,1,0:T(8,128)(2,1)}, u32[]{:S(2)}, u32[]{:S(2)}) async-start(bf16[16,40,128]{2,1,0:T(8,128)(2,1)} %copy-done.1), calls=%async_computation.2 | async-start | bytes 327680 | tf_op jit(solution)/shard_map/all_to_all | solution.py:557
  96.4 10.1 %collective-permute-start.6 = (bf16[64,640]{1,0:T(8,128)(2,1)S(1)}, bf16[64,640]{1,0:T(8,128)(2,1)S(1)}, u32[]{:S(2)}, u32[]{:S(2)}) collective-permute-start(bf16[64,640]{1,0:T(8,128)(2,1)S(1)} %unpack_back.1.rest_0_), channel_id=1, source_target_pairs={{0,6},{1,7},{2,4},{3,5},{4,2},{5,3},{6,0},{7,1},{8,14},{9,15},{10,... | collective-permute-start | bytes 245768 | tf_op jit(solution)/shard_map/ppermute | solution.py:597
  100.2 7.1 %collective-permute-start.4 = (bf16[64,640]{1,0:T(8,128)(2,1)S(1)}, bf16[64,640]{1,0:T(8,128)(2,1)S(1)}, u32[]{:S(2)}, u32[]{:S(2)}) collective-permute-start(bf16[64,640]{1,0:T(8,128)(2,1)S(1)} %unpack_back.1.rest_0_), channel_id=1, source_target_pairs={{0,2},{1,3},{2,0},{3,1},{4,6},{5,7},{6,4},{7,5},{8,10},{9,11},{10,... | collective-permute-start | bytes 245768 | tf_op jit(solution)/shard_map/ppermute | solution.py:597
  100.2 9.1 %collective-permute-start.5 = (bf16[64,640]{1,0:T(8,128)(2,1)S(1)}, bf16[64,640]{1,0:T(8,128)(2,1)S(1)}, u32[]{:S(2)}, u32[]{:S(2)}) collective-permute-start(bf16[64,640]{1,0:T(8,128)(2,1)S(1)} %unpack_back.1.rest_0_), channel_id=1, source_target_pairs={{0,4},{1,5},{2,6},{3,7},{4,0},{5,1},{6,2},{7,3},{8,12},{9,13},{10,... | collective-permute-start | bytes 245768 | tf_op jit(solution)/shard_map/ppermute | solution.py:597
  101.5 9.4 %collective-permute-start.7 = (bf16[64,640]{1,0:T(8,128)(2,1)S(1)}, bf16[64,640]{1,0:T(8,128)(2,1)S(1)}, u32[]{:S(2)}, u32[]{:S(2)}) collective-permute-start(bf16[64,640]{1,0:T(8,128)(2,1)S(1)} %unpack_back.1.rest_0_), channel_id=1, source_target_pairs={{0,1},{1,0},{2,3},{3,2},{4,5},{5,4},{6,7},{7,6},{8,9},{9,8},{10,11... | collective-permute-start | bytes 245768 | tf_op jit(solution)/shard_map/ppermute | solution.py:598
  106.4 4.4 %collective-permute-start.10 = (bf16[64,640]{1,0:T(8,128)(2,1)S(1)}, bf16[64,640]{1,0:T(8,128)(2,1)S(1)}, u32[]{:S(2)}, u32[]{:S(2)}) collective-permute-start(bf16[64,640]{1,0:T(8,128)(2,1)S(1)} %collective-permute-done.6.rest_3_), channel_id=1, source_target_pairs={{0,1},{1,0},{2,3},{3,2},{4,5},{5,4},{6,7},{7,6},{8,9},{9,8},{10,11... | collective-permute-start | bytes 245768 | tf_op jit(solution)/shard_map/ppermute | solution.py:598
  107.3 3.5 %collective-permute-start.8 = (bf16[64,640]{1,0:T(8,128)(2,1)S(1)}, bf16[64,640]{1,0:T(8,128)(2,1)S(1)}, u32[]{:S(2)}, u32[]{:S(2)}) collective-permute-start(bf16[64,640]{1,0:T(8,128)(2,1)S(1)} %collective-permute-done.4.rest_1_), channel_id=1, source_target_pairs={{0,1},{1,0},{2,3},{3,2},{4,5},{5,4},{6,7},{7,6},{8,9},{9,8},{10,11... | collective-permute-start | bytes 245768 | tf_op jit(solution)/shard_map/ppermute | solution.py:598
  109.3 2.4 %collective-permute-start.9 = (bf16[64,640]{1,0:T(8,128)(2,1)S(1)}, bf16[64,640]{1,0:T(8,128)(2,1)S(1)}, u32[]{:S(2)}, u32[]{:S(2)}) collective-permute-start(bf16[64,640]{1,0:T(8,128)(2,1)S(1)} %collective-permute-done.5.rest_2_), channel_id=1, source_target_pairs={{0,1},{1,0},{2,3},{3,2},{4,5},{5,4},{6,7},{7,6},{8,9},{9,8},{10,11... | collective-permute-start | bytes 245768 | tf_op jit(solution)/shard_map/ppermute | solution.py:598

commit v6 on v5

--- a/solution.py
+++ b/solution.py
@@ -11,6 +11,9 @@
 ROPE = 64
 NOPE = 128
 CAP = 4
+DIRECT = 2
+SPILL = 2
+STRIP = 16
 GROUP = 4
 FLOOR = -1e30
 BF16 = jnp.bfloat16
@@ -110,15 +113,46 @@
     )(decode_slot, prompt_lengths, where, queries, new_latent)
 
 
+def padded_rows(piece, feature):
+    return -(-(piece * feature // 128) // STRIP) * STRIP
+
+
+def window_start(row, piece, window, span):
+    return pl.multiple_of(jnp.where(row + piece > window, span - window, 0), 128)
+
+
+def picker(row, start, piece, window):
+    pick = lax.broadcasted_iota(jnp.int32, (piece, window), 1) - (
+        row - start + lax.broadcasted_iota(jnp.int32, (piece, window), 0)
+    )
+    return jnp.where(pick == 0, 1.0, 0.0).astype(BF16)
+
+
+def packed_piece(pick, latents):
+    piece = pick.shape[0]
+    blocks = latents.shape[0] // 128
+    turned = lax.dot_general(pick, latents, NT, preferred_element_type=F32)
+    last = turned[:, 128 * blocks :]
+    last = jnp.concatenate([last[: piece // 2], last[piece // 2 :]], axis=1)
+    return jnp.concatenate(
+        [turned[:, 128 * b : 128 * b + 128] for b in range(blocks)] + [last], axis=0
+    ).astype(BF16)
+
+
 def pack_context_kernel(
-    decode_slot, where, p_ref, out_ref, placing, counts, buf, sems
+    decode_slot, where, p_ref,
+    out_ref, placing, leaving, coming, relay, rounds,
+    counts, entered, buf, sems,
 ):
     slots, feature, window = buf.shape
-    blocks = feature // 128
-    piece = out_ref.shape[2] * 128 // feature
+    owners = counts.shape[0]
+    padded = (out_ref.shape[1] - SPILL * STRIP) // DIRECT
+    piece = padded * 128 // feature // 16 * 16
+    rows = piece * feature // 128
+    strips = padded // STRIP
     chunk = slots // sems.shape[0]
     row = where[0] * piece
-    start = pl.multiple_of(jnp.where(row + piece > window, p_ref.shape[2] - window, 0), 128)
+    start = window_start(row, piece, window, p_ref.shape[2])
     copies = [
         pltpu.make_async_copy(
             p_ref.at[pl.ds(k * chunk, chunk), :, pl.ds(start, window)],
@@ -130,17 +164,19 @@
     for copy in copies:
         copy.start()
     bits = slots.bit_length() - 1
-    for p in range(counts.shape[0]):
+
+    for p in range(owners):
         counts[p] = 0
+    spilled = jnp.int32(0)
     for g in range(slots):
         owner = decode_slot[where[1] * slots + g] >> bits
         rank = counts[owner]
         counts[owner] = rank + 1
         placing[g] = owner * CAP + rank
-    pick = lax.broadcasted_iota(jnp.int32, (piece, window), 1) - (
-        row - start + lax.broadcasted_iota(jnp.int32, (piece, window), 0)
-    )
-    pick = jnp.where(pick == 0, 1.0, 0.0).astype(BF16)
+        over = rank >= DIRECT
+        leaving[g] = jnp.where(over, spilled, -1)
+        spilled = spilled + over.astype(jnp.int32)
+    pick = picker(row, start, piece, window)
 
     for k, copy in enumerate(copies):
         copy.wait()
@@ -148,29 +184,87 @@
         def one(n, carry):
             g = k * chunk + n
             dest, rank = split(placing[g])
-            turned = lax.dot_general(pick, buf[g], NT, preferred_element_type=F32)
-            last = turned[:, 128 * blocks :]
-            last = jnp.concatenate([last[: piece // 2], last[piece // 2 :]], axis=1)
-            out_ref[dest, rank] = jnp.concatenate(
-                [turned[:, 128 * b : 128 * b + 128] for b in range(blocks)] + [last], axis=0
-            ).astype(BF16)
+            cell = packed_piece(pick, buf[g])
+
+            @pl.when(rank < DIRECT)
+            def _():
+                out_ref[dest, pl.ds(pl.multiple_of(rank * padded, STRIP), rows), :] = cell
+
+            @pl.when((rank >= DIRECT) & (leaving[g] < SPILL))
+            def _():
+                at = DIRECT * padded + leaving[g] * STRIP
+                for m in range(strips):
+                    high = min(STRIP, rows - m * STRIP)
+                    out_ref[m, pl.ds(pl.multiple_of(at, STRIP), high), :] = cell[
+                        m * STRIP : m * STRIP + high
+                    ]
+
             return carry
 
         lax.fori_loop(0, chunk, one, 0, unroll=2)
+
+    for q in range(owners):
+        entered[q] = 0
+        for e in range(SPILL):
+            relay[q * SPILL + e] = 0
+
+    def locate(p, longest):
+        for q in range(owners):
+            counts[q] = 0
+
+        def look(k, state):
+            spilled, left = state
+            slot = decode_slot[p * slots + k]
+            owner = slot >> bits
+            rank = counts[owner]
+            counts[owner] = rank + 1
+            over = rank >= DIRECT
+            hops = over & (spilled < SPILL) & (entered[owner] < SPILL)
+            entry = entered[owner]
+
+            @pl.when(hops)
+            def _():
+                entered[owner] = entry + 1
+                relay[owner * SPILL + entry] = p * SPILL + spilled
+
+            code = jnp.where(hops, entry, SPILL + left)
+            code = jnp.where(over, code, -1)
+
+            @pl.when(owner == where[1])
+            def _():
+                coming[slot & (slots - 1)] = code
+
+            @pl.when(p == where[1])
+            def _():
+                leaving[k] = code
+
+            rest = over & jnp.logical_not(hops)
+            return spilled + over.astype(jnp.int32), left + rest.astype(jnp.int32)
+
+        _, left = lax.fori_loop(0, slots, look, (jnp.int32(0), jnp.int32(0)), unroll=4)
+        return jnp.maximum(longest, left)
+
+    longest = lax.fori_loop(0, owners, locate, jnp.int32(0))
+    rounds[0] = (longest + SPILL - 1) // SPILL
 
 
 def pack_context(decode_slot, where, prompt_latent, piece, pool_count):
     slots, feature, _ = prompt_latent.shape
-    rows = piece * feature // 128
+    rows = padded_rows(piece, feature)
     return pl.pallas_call(
         pack_context_kernel,
         out_shape=(
-            jax.ShapeDtypeStruct((pool_count, CAP, rows, 128), BF16),
+            jax.ShapeDtypeStruct((pool_count, DIRECT * rows + SPILL * STRIP, 128), BF16),
             jax.ShapeDtypeStruct((slots,), jnp.int32),
+            jax.ShapeDtypeStruct((slots,), jnp.int32),
+            jax.ShapeDtypeStruct((slots,), jnp.int32),
+            jax.ShapeDtypeStruct((pool_count * SPILL,), jnp.int32),
+            jax.ShapeDtypeStruct((1,), jnp.int32),
         ),
         in_specs=[SMEM_SPEC, SMEM_SPEC, ANY_SPEC],
-        out_specs=(VMEM_SPEC, SMEM_SPEC),
+        out_specs=(VMEM_SPEC,) + (SMEM_SPEC,) * 5,
         scratch_shapes=[
+            pltpu.SMEM((pool_count,), jnp.int32),
             pltpu.SMEM((pool_count,), jnp.int32),
             pltpu.VMEM((slots, feature, 256), BF16),
             pltpu.SemaphoreType.DMA((4,)),
@@ -181,6 +275,43 @@
     )(decode_slot, where, prompt_latent)
 
 
+def pack_spill_kernel(turn, leaving, where, p_ref, spill_ref, buf, sem):
+    feature, window = buf.shape
+    piece = spill_ref.shape[1] * 128 // feature // 16 * 16
+    row = where[0] * piece
+    start = window_start(row, piece, window, p_ref.shape[2])
+    pick = picker(row, start, piece, window)
+
+    def one(g, carry):
+        at = leaving[g] - SPILL - turn[0] * SPILL
+
+        @pl.when((at >= 0) & (at < SPILL))
+        def _():
+            copy = pltpu.make_async_copy(p_ref.at[g, :, pl.ds(start, window)], buf, sem)
+            copy.start()
+            copy.wait()
+            cell = packed_piece(pick, buf[...])
+            spill_ref[at, : cell.shape[0], :] = cell
+
+        return carry
+
+    lax.fori_loop(0, p_ref.shape[0], one, 0)
+
+
+def pack_spill(turn, leaving, where, prompt_latent, piece):
+    slots, feature, _ = prompt_latent.shape
+    return pl.pallas_call(
+        pack_spill_kernel,
+        out_shape=jax.ShapeDtypeStruct((SPILL, padded_rows(piece, feature), 128), BF16),
+        in_specs=[SMEM_SPEC] * 3 + [ANY_SPEC],
+        out_specs=VMEM_SPEC,
+        scratch_shapes=[pltpu.VMEM((feature, 256), BF16), pltpu.SemaphoreType.DMA],
+        compiler_params=params(),
+        cost_estimate=cost(),
+        name="pack_spill",
+    )(turn, leaving, where, prompt_latent)
+
+
 def unpack_piece(packed, row, first_row, length, piece, feature):
     blocks = feature // 128
     parts = [packed[(*row, pl.ds(b * piece, piece), slice(None))] for b in range(blocks)]
@@ -191,27 +322,34 @@
     return jnp.where(position < length, whole.astype(F32), 0.0).astype(BF16)
 
 
-def place_kernel(arrival, lengths, where, packed, out_ref, inbox, outbox, in_sems, out_sems):
+def place_kernel(
+    arrival, coming, lengths, where, direct, out_ref, inbox, outbox, in_sems, out_sems
+):
     slots, piece, feature = out_ref.shape
-    first_row = where[0] * piece
+    rows = inbox.shape[1]
 
     def copy_in(j):
         owner, rank = split(arrival[j])
-        return pltpu.make_async_copy(packed.at[owner, rank], inbox.at[j], in_sems.at[j])
+        rank = jnp.minimum(rank, DIRECT - 1)
+        source = direct.at[owner, pl.ds(pl.multiple_of(rank * rows, STRIP), rows), :]
+        return pltpu.make_async_copy(source, inbox.at[j], in_sems.at[j])
 
     def copy_out(j):
         return pltpu.make_async_copy(outbox.at[j], out_ref.at[j], out_sems.at[j])
 
     def each(action):
         def step(j, carry):
-            action(j)
+            @pl.when(coming[j] < 0)
+            def _():
+                action(j)
+
             return carry
 
         lax.fori_loop(0, slots, step, 0)
 
     def work(j):
         copy_in(j).wait()
-        outbox[j] = unpack_piece(inbox, (j,), first_row, lengths[j], piece, feature)
+        outbox[j] = unpack_piece(inbox, (j,), where[0] * piece, lengths[j], piece, feature)
         copy_out(j).start()
 
     each(lambda j: copy_in(j).start())
@@ -219,13 +357,13 @@
     each(lambda j: copy_out(j).wait())
 
 
-def place(arrival, lengths, where, packed, piece, feature):
-    slots = arrival.shape[0] - 8
-    rows = packed.shape[-2]
+def place(arrival, coming, lengths, where, direct, piece, feature):
+    slots = coming.shape[0]
+    rows = padded_rows(piece, feature)
     return pl.pallas_call(
         place_kernel,
         out_shape=jax.ShapeDtypeStruct((slots, piece, feature), BF16),
-        in_specs=[SMEM_SPEC] * 3 + [ANY_SPEC],
+        in_specs=[SMEM_SPEC] * 4 + [ANY_SPEC],
         out_specs=ANY_SPEC,
         scratch_shapes=[
             pltpu.VMEM((slots, rows, 128), BF16),
@@ -236,7 +374,115 @@
         compiler_params=params(),
         cost_estimate=cost(bytes_accessed=12_000_000),
         name="place_context",
-    )(arrival, lengths, where, packed)
+    )(arrival, coming, lengths, where, direct)
+
+
+def place_strips_kernel(
+    coming, lengths, where, back, context, out_ref, inbox, whole, outbox, in_sems, out_sems
+):
+    slots, piece, feature = out_ref.shape
+    strips = inbox.shape[1]
+
+    def copy_in(e):
+        source = back.at[pl.ds(0, strips), pl.ds(e * STRIP, STRIP), :]
+        return pltpu.make_async_copy(source, inbox.at[e], in_sems.at[e])
+
+    def copy_out(j, e):
+        return pltpu.make_async_copy(outbox.at[e], out_ref.at[j], out_sems.at[e])
+
+    for e in range(SPILL):
+        copy_in(e).start()
+    for e in range(SPILL):
+        copy_in(e).wait()
+        for m in range(strips):
+            whole[e, m * STRIP : m * STRIP + STRIP, :] = inbox[e, m]
+
+    def each(action):
+        def step(j, carry):
+            for e in range(SPILL):
+
+                @pl.when(coming[j] == e)
+                def _():
+                    action(j, e)
+
+            return carry
+
+        lax.fori_loop(0, slots, step, 0)
+
+    def work(j, e):
+        outbox[e] = unpack_piece(whole, (e,), where[0] * piece, lengths[j], piece, feature)
+        copy_out(j, e).start()
+
+    each(work)
+    each(lambda j, e: copy_out(j, e).wait())
+
+
+def place_strips(coming, lengths, where, back, context):
+    slots, piece, feature = context.shape
+    strips = padded_rows(piece, feature) // STRIP
+    return pl.pallas_call(
+        place_strips_kernel,
+        out_shape=jax.ShapeDtypeStruct(context.shape, BF16),
+        in_specs=[SMEM_SPEC] * 3 + [ANY_SPEC] * 2,
+        out_specs=ANY_SPEC,
+        scratch_shapes=[
+            pltpu.VMEM((SPILL, strips, STRIP, 128), BF16),
+            pltpu.VMEM((SPILL, strips * STRIP, 128), BF16),
+            pltpu.VMEM((SPILL, piece, feature), BF16),
+            pltpu.SemaphoreType.DMA((SPILL,)),
+            pltpu.SemaphoreType.DMA((SPILL,)),
+        ],
+        input_output_aliases={4: 0},
+        compiler_params=params(),
+        cost_estimate=cost(bytes_accessed=6_000_000),
+        name="place_strips",
+    )(coming, lengths, where, back, context)
+
+
+def place_spill_kernel(
+    turn, arrival, coming, lengths, where, spill, context, out_ref, inbox, outbox, sem
+):
+    slots, piece, feature = out_ref.shape
+
+    def one(j, carry):
+        at = coming[j] - SPILL - turn[0] * SPILL
+
+        @pl.when((at >= 0) & (at < SPILL))
+        def _():
+            owner = split(arrival[j])[0]
+            copy = pltpu.make_async_copy(
+                spill.at[owner, jnp.clip(at, 0, SPILL - 1)], inbox.at[0], sem
+            )
+            copy.start()
+            copy.wait()
+            outbox[...] = unpack_piece(
+                inbox, (0,), where[0] * piece, lengths[j], piece, feature
+            )
+            copy = pltpu.make_async_copy(outbox, out_ref.at[j], sem)
+            copy.start()
+            copy.wait()
+
+        return carry
+
+    lax.fori_loop(0, slots, one, 0)
+
+
+def place_spill(turn, arrival, coming, lengths, where, spill, context):
+    return pl.pallas_call(
+        place_spill_kernel,
+        out_shape=jax.ShapeDtypeStruct(context.shape, BF16),
+        in_specs=[SMEM_SPEC] * 5 + [ANY_SPEC] * 2,
+        out_specs=ANY_SPEC,
+        scratch_shapes=[
+            pltpu.VMEM((1,) + spill.shape[-2:], BF16),
+            pltpu.VMEM(context.shape[1:], BF16),
+            pltpu.SemaphoreType.DMA,
+        ],
+        input_output_aliases={6: 0},
+        compiler_params=params(),
+        cost_estimate=cost(),
+        name="place_spill",
+    )(turn, arrival, coming, lengths, where, spill, context)
 
 
 def attention_kernel(
@@ -441,11 +687,16 @@
     )(where, kept, swapped)
 
 
-def pack_back_kernel(placing, mine, *rest):
-    parts, (out_ref, total, rows) = rest[:-3], rest[-3:]
+def pack_back_kernel(placing, relay, direct, mine, *rest):
+    parts, (out_ref, strips, total, rows, sem) = rest[:-5], rest[-5:]
     slots = placing.shape[0]
     blocks = mine.shape[1] // 128
     steps = mine.shape[0] // slots
+    hop = SPILL * STRIP
+    fetch = pltpu.make_async_copy(
+        direct.at[:, pl.ds(direct.shape[1] - hop, hop), :], strips, sem
+    )
+    fetch.start()
     whole = mine[...]
     for part in parts:
         whole = whole + part[...].astype(F32)
@@ -462,30 +713,43 @@
         return carry
 
     lax.fori_loop(0, slots, one, 0, unroll=4)
-    out_ref[...] = rows[...].reshape(out_ref.shape).astype(BF16)
-
-
-def pack_back(placing, mine, parts, pool_count):
+    out_ref[:, hop:, :] = rows[...].reshape(out_ref.shape[0], 8 * blocks, 128).astype(BF16)
+    fetch.wait()
+    for q in range(out_ref.shape[0]):
+        for e in range(SPILL):
+            came = relay[q * SPILL + e]
+            at = pl.multiple_of((came % SPILL) * STRIP, STRIP)
+            out_ref[q, e * STRIP : e * STRIP + STRIP, :] = strips[
+                came // SPILL, pl.ds(at, STRIP), :
+            ]
+
+
+def pack_back(placing, relay, direct, mine, parts):
+    pool_count = direct.shape[0]
     blocks = mine.shape[1] // 128
+    hop = SPILL * STRIP
     return pl.pallas_call(
         pack_back_kernel,
-        out_shape=jax.ShapeDtypeStruct((pool_count, 8 * blocks, 128), BF16),
-        in_specs=[SMEM_SPEC] + [VMEM_SPEC] * (1 + len(parts)),
+        out_shape=jax.ShapeDtypeStruct((pool_count, hop + 8 * blocks, 128), BF16),
+        in_specs=[SMEM_SPEC] * 2 + [ANY_SPEC] + [VMEM_SPEC] * (1 + len(parts)),
         out_specs=VMEM_SPEC,
         scratch_shapes=[
+            pltpu.VMEM((pool_count, hop, 128), BF16),
             pltpu.VMEM((blocks, mine.shape[0], 128), F32),
             pltpu.VMEM((pool_count * 8 * blocks, 128), F32),
+            pltpu.SemaphoreType.DMA,
         ],
         compiler_params=params(),
         cost_estimate=cost(),
         name="pack_back",
-    )(placing, mine, *parts)
+    )(placing, relay, direct, mine, *parts)
 
 
 def unpack_back_kernel(steps, arrival, packed, out_ref, rows, total):
     slots = out_ref.shape[0] // steps
     blocks = out_ref.shape[1] // 128
-    rows[...] = packed[...].astype(F32).reshape(rows.shape)
+    first = packed.shape[1] - 8 * blocks
+    rows[...] = packed[:, first:, :].astype(F32).reshape(rows.shape)
 
     def one(j, carry):
         owner, rank = split(arrival[j])
@@ -575,9 +839,11 @@
         decode_slot, prompt_lengths, where, queries, new_latent, pool_count
     )
     payload = exchange(payload)
-    first, placing = pack_context(decode_slot, where, latent_t, piece, pool_count)
-    payload, first = lax.optimization_barrier((payload, first))
-    first = exchange(first)
+    direct, placing, leaving, coming, relay, rounds = pack_context(
+        decode_slot, where, latent_t, piece, pool_count
+    )
+    payload, direct = lax.optimization_barrier((payload, direct))
+    direct = exchange(direct)
 
     given, kept = attention(
         placing, prompt_lengths, where, payload, latent_t, w_uk, w_uv, w_out, steps
@@ -587,16 +853,25 @@
     mine, *parts = share(where, kept, swapped, z_count)
     parts = [lax.ppermute(part, "tp", hop) for part, hop in zip(parts, hops)]
 
-    back = pack_back(placing, mine, parts, pool_count)
-    back, first = lax.optimization_barrier((back, first))
-    back = exchange(back)
-    context = place(arrival, lengths, where, first, piece, feature)
+    back = exchange(pack_back(placing, relay, direct, mine, parts))
+    context = place(arrival, coming, lengths, where, direct, piece, feature)
     back, context = lax.optimization_barrier((back, context))
-
     own = unpack_back(arrival, back, steps // 2, slots, out_width // z_count)
     parts = [own] + [lax.ppermute(own, "tp", hop) for hop in hops]
     parts = parts + [lax.ppermute(part, "tp", swap) for part in parts]
+    context = place_strips(coming, lengths, where, back, context)
     decoded = assemble(where, parts, slots, steps, out_width)
+
+    def more(state):
+        turn, context = state
+        spill = pack_spill(turn, leaving, where, latent_t, piece)
+        spill = exchange(jnp.broadcast_to(spill[None], (pool_count,) + spill.shape))
+        context = place_spill(turn, arrival, coming, lengths, where, spill, context)
+        return turn + 1, context
+
+    context = lax.while_loop(
+        lambda state: state[0][0] < rounds[0], more, (jnp.zeros((1,), jnp.int32), context)
+    )[1]
     return decoded, context
 
 

time: 114 us -> 109 us (0.956)
  waiting for transfers between devices: 24.2 us -> 8.22 us
  Pallas kernels: 47.5 us -> 59.7 us
    all_to_all x3, waiting for transfers between devices: 16 us -> 0.85 us  [exchange(): return lax.all_to_all(x, 'pool', split_axis=0, concat_axis=0, tiled=True)]
    pallas_call x1, Pallas kernels: 9.89 us -> 19.3 us  [pack_context(): pl.pallas_call(pack_context_kernel, out_shape=(jax.ShapeDtypeStruct((pool...]
    all_to_all x3, starting transfers between devices: 16 us -> 21.2 us  [exchange(): return lax.all_to_all(x, 'pool', split_axis=0, concat_axis=0, tiled=True)]
    ppermute x4, starting transfers between devices: 9.35 us -> 6.42 us  [body(): parts = parts + [lax.ppermute(part, 'tp', swap) for part in parts]]
    pallas_call x0 -> x1, Pallas kernels: none -> 2.02 us  [place_strips(): pl.pallas_call(place_strips_kernel, out_shape=jax.ShapeDtypeStruct(contex...]
    ppermute x3, starting transfers between devices: 5.11 us -> 3.33 us  [body(): parts = [own] + [lax.ppermute(own, 'tp', hop) for hop in hops]]
    unnamed x14 -> x8, local copies, waits for them, and re-layouts: 2.75 us -> 2.1 us
  transfers between devices with their start and end apart: 14 -> 14, of which waited for: 7 -> 4; matrix products, arithmetic and copies ran while one was open for 0% -> 0% of each run, Pallas kernels for 35% -> 46%
where the time goes in v6:
time: 109 us
  Pallas kernels  59.7 us (55%)
  starting transfers between devices  37.5 us (34%)
  waiting for transfers between devices  8.22 us (8%)
  local copies, waits for them, and re-layouts  2.1 us (2%)
    pallas_call x1, Pallas kernels, attention(): pl.pallas_call(attention_kernel, out_shape=(jax.ShapeDtypeStruct((half, w...  21.4 us
    all_to_all x3, starting transfers between devices, exchange(): return lax.all_to_all(x, 'pool', split_axis=0, concat_axis=0, tiled=True)  21.2 us
    pallas_call x1, Pallas kernels, pack_context(): pl.pallas_call(pack_context_kernel, out_shape=(jax.ShapeDtypeStruct((pool...  19.3 us
    pallas_call x1, Pallas kernels, place(): pl.pallas_call(place_kernel, out_shape=jax.ShapeDtypeStruct((slots, piece...  7.01 us
    ppermute x4, starting transfers between devices, body(): parts = parts + [lax.ppermute(part, 'tp', swap) for part in parts]  6.42 us
    ppermute x3, waiting for transfers between devices, body(): parts = [lax.ppermute(part, 'tp', hop) for part, hop in zip(parts, hops)]  5.88 us
    ppermute x3, starting transfers between devices, body(): parts = [lax.ppermute(part, 'tp', hop) for part, hop in zip(parts, hops)]  5.03 us
    pallas_call x1, Pallas kernels, pack_queries(): pl.pallas_call(pack_queries_kernel, out_shape=(jax.ShapeDtypeStruct((pool...  4.79 us
  transfers between devices with their start and end apart: 14, of which 4 were waited for; matrix products, arithmetic and copies ran while one was open for 0% of the time, Pallas kernels for 46%

profile of v6, /device:TPU:1, one launch (start us, length us, event | category | flops | bytes accessed | tf_op | source)
XLA Modules:
  0.0 109.1 jit_solution(12001924607893476848)
XLA Ops:
  0.7 4.8 %pack_queries.1 = (bf16[16,264,128]{2,1,0:T(8,128)(2,1)}, s32[40]{0:T(128)S(1)}, s32[40]{0:T(128)S(1)}) custom-call(s32[512]{0:T(512)} %decode_slot.3, s32[512]{0:T(512)} %lengths.1, s32[2]{0:T(128)S(1)} %pad_add_fusion.where, bf16[4,32,8,192]{3,2,1,0:T(8,128)(2,1)} %q_hbm.1, bf16[4,32,576]{2,1,0:T(8,128)(2,1)} %n_hbm.1), custom_call_target="tpu_custom_call" | custom-call | flops 1000 | bytes 1000 | tf_op jit(solution)/shard_map/pack_queries/pallas_call | solution.py:94
  5.5 7.6 %all-to-all-start.1 = ((bf16[16,264,128]{2,1,0:T(8,128)(2,1)}), bf16[16,264,128]{2,1,0:T(8,128)(2,1)S(1)}, u32[]{:S(2)}, u32[]{:S(2)}) async-start(bf16[16,264,128]{2,1,0:T(8,128)(2,1)} %get-tuple-element.72), calls=%async_computation.1 | async-start | bytes 2162688 | tf_op jit(solution)/shard_map/all_to_all | solution.py:821
  13.1 19.3 %pack_context.1 = (bf16[16,480,128]{2,1,0:T(8,128)(2,1)}, s32[32]{0:T(128)}, s32[32]{0:T(128)S(1)}, s32[32]{0:T(128)S(1)}, s32[32]{0:T(128)}, /*index=5*/s32[1]{0:T(128)}) custom-call(s32[512]{0:T(512)} %decode_slot.3, s32[2]{0:T(128)S(1)} %pad_add_fusion.where, bf16[32,576,384]{2,1,0:T(8,128)(2,1)} %bitcast.5), custom_call_target="tpu_custom_call" | custom-call | flops 1000 | bytes 1000 | tf_op jit(solution)/shard_map/pack_context/pallas_call | solution.py:254
  32.4 1.0 copy-done.3
  33.4 6.6 %all-to-all-start.2 = ((bf16[16,480,128]{2,1,0:T(8,128)(2,1)}), bf16[16,480,128]{2,1,0:T(8,128)(2,1)S(1)}, u32[]{:S(2)}, u32[]{:S(2)}) async-start(bf16[16,480,128]{2,1,0:T(8,128)(2,1)} %get-tuple-element.74), calls=%async_computation.2 | async-start | bytes 3932160 | tf_op jit(solution)/shard_map/all_to_all | solution.py:821
  40.1 21.4 %attention.1 = (bf16[64,2560]{1,0:T(8,128)(2,1)}, f32[64,2560]{1,0:T(8,128)}) custom-call(s32[32]{0:T(128)} %get-tuple-element.70.placing, s32[512]{0:T(512)} %lengths.1, s32[2]{0:T(128)S(1)} %pad_add_fusion.where, bf16[16,264,128]{2,1,0:T(8,128)(2,1)} %copy-done.3, bf16[32,576,384]{2,1,0:T(8,128)(2,1)} %bitcast.6, bf16[8,512,128]{2,1,0:T(8,128)(2,1)} %w_uk_hbm.1, ...), custom_call_target="tpu_custom_call" | custom-call | flops 1000 | bytes 1000 | tf_op jit(solution)/shard_map/attention/pallas_call | solution.py:637
  61.5 1.6 %collective-permute-start = (bf16[64,2560]{1,0:T(8,128)(2,1)}, bf16[64,2560]{1,0:T(8,128)(2,1)S(1)}, u32[]{:S(2)}, u32[]{:S(2)}) collective-permute-start(bf16[64,2560]{1,0:T(8,128)(2,1)} %get-tuple-element.77), channel_id=1, source_target_pairs={{0,1},{1,0},{2,3},{3,2},{4,5},{5,4},{6,7},{7,6},{8,9},{9,8},{10,11... | collective-permute-start | bytes 983048 | tf_op jit(solution)/shard_map/ppermute | solution.py:852
  63.1 1.5 %collective-permute-done.swapped = bf16[64,2560]{1,0:T(8,128)(2,1)S(1)} collective-permute-done((bf16[64,2560]{1,0:T(8,128)(2,1)}, bf16[64,2560]{1,0:T(8,128)(2,1)S(1)}, u32[]{:S(2)}, u32[]{:S(2)}) %collective-permute-start) | collective-permute-done | bytes 327712 | tf_op jit(solution)/shard_map/ppermute | solution.py:852
  64.5 1.1 copy-done
  66.2 1.7 %collective-permute-start.1 = (bf16[64,640]{1,0:T(8,128)(2,1)S(1)}, bf16[64,640]{1,0:T(8,128)(2,1)S(1)}, u32[]{:S(2)}, u32[]{:S(2)}) collective-permute-start(bf16[64,640]{1,0:T(8,128)(2,1)S(1)} %get-tuple-element.79), channel_id=1, source_target_pairs={{0,2},{1,3},{2,0},{3,1},{4,6},{5,7},{6,4},{7,5},{8,10},{9,11},{10,... | collective-permute-start | bytes 245768 | tf_op jit(solution)/shard_map/ppermute | solution.py:854
  68.0 3.3 %collective-permute-start.2 = (bf16[64,640]{1,0:T(8,128)(2,1)S(1)}, bf16[64,640]{1,0:T(8,128)(2,1)S(1)}, u32[]{:S(2)}, u32[]{:S(2)}) collective-permute-start(bf16[64,640]{1,0:T(8,128)(2,1)S(1)} %get-tuple-element.80), channel_id=1, source_target_pairs={{0,4},{1,5},{2,6},{3,7},{4,0},{5,1},{6,2},{7,3},{8,12},{9,13},{10,... | collective-permute-start | bytes 245768 | tf_op jit(solution)/shard_map/ppermute | solution.py:854
  71.3 3.9 %collective-permute-done.2.rest_1_ = bf16[64,640]{1,0:T(8,128)(2,1)S(1)} collective-permute-done((bf16[64,640]{1,0:T(8,128)(2,1)S(1)}, bf16[64,640]{1,0:T(8,128)(2,1)S(1)}, u32[]{:S(2)}, u32[]{:S(2)}) %collective-permute-start.2) | collective-permute-done | bytes 81952 | tf_op jit(solution)/shard_map/ppermute | solution.py:854
  75.2 1.9 %collective-permute-done.3.rest_2_ = bf16[64,640]{1,0:T(8,128)(2,1)S(1)} collective-permute-done((bf16[64,640]{1,0:T(8,128)(2,1)S(1)}, bf16[64,640]{1,0:T(8,128)(2,1)S(1)}, u32[]{:S(2)}, u32[]{:S(2)}) %collective-permute-start.3) | collective-permute-done | bytes 81952 | tf_op jit(solution)/shard_map/ppermute | solution.py:854
  77.2 1.8 %pack_back.1 = bf16[16,72,128]{2,1,0:T(8,128)(2,1)} custom-call(s32[32]{0:T(128)S(1)} %copy-done.1, s32[32]{0:T(128)S(1)} %copy-done.2, bf16[16,480,128]{2,1,0:T(8,128)(2,1)S(1)} %all-to-all-done.2.direct, f32[64,640]{1,0:T(8,128)S(1)} %get-tuple-element.78.mine, bf16[64,640]{1,0:T(8,128)(2,1)S(1)} %collective-permute-done.1.rest_0_, ...), custom_call_target="tpu_custom_call" | custom-call | flops 1000 | bytes 1000 | tf_op jit(solution)/shard_map/pack_back/pallas_call | solution.py:731
  79.0 7.0 %all-to-all-start.3 = ((bf16[16,72,128]{2,1,0:T(8,128)(2,1)}), bf16[16,72,128]{2,1,0:T(8,128)(2,1)S(1)}, u32[]{:S(2)}, u32[]{:S(2)}) async-start(bf16[16,72,128]{2,1,0:T(8,128)(2,1)} %pack_back.1), calls=%async_computation.3 | async-start | bytes 589824 | tf_op jit(solution)/shard_map/all_to_all | solution.py:821
  86.0 7.0 %place_context.1.context = bf16[32,48,576]{2,1,0:T(8,128)(2,1)} custom-call(s32[40]{0:T(128)S(1)} %get-tuple-element.160.arrival, s32[32]{0:T(128)S(1)} %get-tuple-element.161.coming, s32[40]{0:T(128)S(1)} %get-tuple-element.162.lengths, s32[2]{0:T(128)S(1)} %pad_add_fusion.where, bf16[16,480,128]{2,1,0:T(8,128)(2,1)S(1)} %all-to-all-done.2.direct), custom_call_target="tpu_custom_call" | custom-call | flops 1000 | bytes 12000000 | tf_op jit(solution)/shard_map/place_context/pallas_call | solution.py:363
  93.8 0.9 unpack_back.1.rest_0_
  95.5 2.5 %collective-permute-start.4 = (bf16[64,640]{1,0:T(8,128)(2,1)S(1)}, bf16[64,640]{1,0:T(8,128)(2,1)S(1)}, u32[]{:S(2)}, u32[]{:S(2)}) collective-permute-start(bf16[64,640]{1,0:T(8,128)(2,1)S(1)} %unpack_back.1.rest_0_), channel_id=1, source_target_pairs={{0,2},{1,3},{2,0},{3,1},{4,6},{5,7},{6,4},{7,5},{8,10},{9,11},{10,... | collective-permute-start | bytes 245768 | tf_op jit(solution)/shard_map/ppermute | solution.py:860
  98.0 3.1 %collective-permute-start.7 = (bf16[64,640]{1,0:T(8,128)(2,1)S(1)}, bf16[64,640]{1,0:T(8,128)(2,1)S(1)}, u32[]{:S(2)}, u32[]{:S(2)}) collective-permute-start(bf16[64,640]{1,0:T(8,128)(2,1)S(1)} %unpack_back.1.rest_0_), channel_id=1, source_target_pairs={{0,1},{1,0},{2,3},{3,2},{4,5},{5,4},{6,7},{7,6},{8,9},{9,8},{10,11... | collective-permute-start | bytes 245768 | tf_op jit(solution)/shard_map/ppermute | solution.py:861
  101.2 1.6 %collective-permute-start.10 = (bf16[64,640]{1,0:T(8,128)(2,1)S(1)}, bf16[64,640]{1,0:T(8,128)(2,1)S(1)}, u32[]{:S(2)}, u32[]{:S(2)}) collective-permute-start(bf16[64,640]{1,0:T(8,128)(2,1)S(1)} %collective-permute-done.6.rest_3_), channel_id=1, source_target_pairs={{0,1},{1,0},{2,3},{3,2},{4,5},{5,4},{6,7},{7,6},{8,9},{9,8},{10,11... | collective-permute-start | bytes 245768 | tf_op jit(solution)/shard_map/ppermute | solution.py:861
  102.7 0.9 collective-permute-start.9
  103.6 0.9 collective-permute-start.8
  104.5 2.0 %place_strips.1 = bf16[32,48,576]{2,1,0:T(8,128)(2,1)} custom-call(s32[32]{0:T(128)S(1)} %get-tuple-element.161.coming, s32[40]{0:T(128)S(1)} %get-tuple-element.162.lengths, s32[2]{0:T(128)S(1)} %pad_add_fusion.where, bf16[16,72,128]{2,1,0:T(8,128)(2,1)S(1)} %all-to-all-done.3.packed.back, ...), custom_call_target="tpu_custom_call", output_to_operand_aliasing={{}: (4, {})} | custom-call | flops 1000 | bytes 6000000 | tf_op jit(solution)/shard_map/place_strips/pallas_call | solution.py:423
  106.5 1.9 %assemble.1 = bf16[32,4,2560]{2,1,0:T(4,128)(2,1)} custom-call(s32[2]{0:T(128)S(1)} %pad_add_fusion.where, bf16[64,640]{1,0:T(8,128)(2,1)S(1)} %unpack_back.1.rest_0_, bf16[64,640]{1,0:T(8,128)(2,1)S(1)} %collective-permute-done.4.rest_1_, bf16[64,640]{1,0:T(8,128)(2,1)S(1)} %collective-permute-done.5.rest_2_, ...), custom_call_target="tpu_custom_call" | custom-call | flops 1000 | bytes 1000 | tf_op jit(solution)/shard_map/assemble/pallas_call | solution.py:805
  (23 shorter events, 3.1 us)
Async XLA Ops:
  5.5 26.9 %all-to-all-start.1 = ((bf16[16,264,128]{2,1,0:T(8,128)(2,1)}), bf16[16,264,128]{2,1,0:T(8,128)(2,1)S(1)}, u32[]{:S(2)}, u32[]{:S(2)}) async-start(bf16[16,264,128]{2,1,0:T(8,128)(2,1)} %get-tuple-element.72), calls=%async_computation.1 | async-start | bytes 2162688 | tf_op jit(solution)/shard_map/all_to_all | solution.py:821
  32.4 1.0 copy-start.3
  33.4 43.7 %all-to-all-start.2 = ((bf16[16,480,128]{2,1,0:T(8,128)(2,1)}), bf16[16,480,128]{2,1,0:T(8,128)(2,1)S(1)}, u32[]{:S(2)}, u32[]{:S(2)}) async-start(bf16[16,480,128]{2,1,0:T(8,128)(2,1)} %get-tuple-element.74), calls=%async_computation.2 | async-start | bytes 3932160 | tf_op jit(solution)/shard_map/all_to_all | solution.py:821
  40.1 37.1 %copy-start.1 = (s32[32]{0:T(128)S(1)}, s32[32]{0:T(128)}, u32[]{:S(2)}) copy-start(s32[32]{0:T(128)} %get-tuple-element.70.placing) | copy-start | bytes 388
  40.1 37.1 %copy-start.2 = (s32[32]{0:T(128)S(1)}, s32[32]{0:T(128)}, u32[]{:S(2)}) copy-start(s32[32]{0:T(128)} %get-tuple-element.71.relay) | copy-start | bytes 388
  61.5 3.0 %collective-permute-start = (bf16[64,2560]{1,0:T(8,128)(2,1)}, bf16[64,2560]{1,0:T(8,128)(2,1)S(1)}, u32[]{:S(2)}, u32[]{:S(2)}) collective-permute-start(bf16[64,2560]{1,0:T(8,128)(2,1)} %get-tuple-element.77), channel_id=1, source_target_pairs={{0,1},{1,0},{2,3},{3,2},{4,5},{5,4},{6,7},{7,6},{8,9},{9,8},{10,11... | collective-permute-start | bytes 983048 | tf_op jit(solution)/shard_map/ppermute | solution.py:852
  64.5 1.1 copy-start
  66.2 5.0 %collective-permute-start.1 = (bf16[64,640]{1,0:T(8,128)(2,1)S(1)}, bf16[64,640]{1,0:T(8,128)(2,1)S(1)}, u32[]{:S(2)}, u32[]{:S(2)}) collective-permute-start(bf16[64,640]{1,0:T(8,128)(2,1)S(1)} %get-tuple-element.79), channel_id=1, source_target_pairs={{0,2},{1,3},{2,0},{3,1},{4,6},{5,7},{6,4},{7,5},{8,10},{9,11},{10,... | collective-permute-start | bytes 245768 | tf_op jit(solution)/shard_map/ppermute | solution.py:854
  68.0 7.2 %collective-permute-start.2 = (bf16[64,640]{1,0:T(8,128)(2,1)S(1)}, bf16[64,640]{1,0:T(8,128)(2,1)S(1)}, u32[]{:S(2)}, u32[]{:S(2)}) collective-permute-start(bf16[64,640]{1,0:T(8,128)(2,1)S(1)} %get-tuple-element.80), channel_id=1, source_target_pairs={{0,4},{1,5},{2,6},{3,7},{4,0},{5,1},{6,2},{7,3},{8,12},{9,13},{10,... | collective-permute-start | bytes 245768 | tf_op jit(solution)/shard_map/ppermute | solution.py:854
  71.3 5.9 %collective-permute-start.3 = (bf16[64,640]{1,0:T(8,128)(2,1)S(1)}, bf16[64,640]{1,0:T(8,128)(2,1)S(1)}, u32[]{:S(2)}, u32[]{:S(2)}) collective-permute-start(bf16[64,640]{1,0:T(8,128)(2,1)S(1)} %get-tuple-element.81), channel_id=1, source_target_pairs={{0,6},{1,7},{2,4},{3,5},{4,2},{5,3},{6,0},{7,1},{8,14},{9,15},{10,... | collective-permute-start | bytes 245768 | tf_op jit(solution)/shard_map/ppermute | solution.py:854
  79.0 14.8 %all-to-all-start.3 = ((bf16[16,72,128]{2,1,0:T(8,128)(2,1)}), bf16[16,72,128]{2,1,0:T(8,128)(2,1)S(1)}, u32[]{:S(2)}, u32[]{:S(2)}) async-start(bf16[16,72,128]{2,1,0:T(8,128)(2,1)} %pack_back.1), calls=%async_computation.3 | async-start | bytes 589824 | tf_op jit(solution)/shard_map/all_to_all | solution.py:821
  94.7 6.5 %collective-permute-start.6 = (bf16[64,640]{1,0:T(8,128)(2,1)S(1)}, bf16[64,640]{1,0:T(8,128)(2,1)S(1)}, u32[]{:S(2)}, u32[]{:S(2)}) collective-permute-start(bf16[64,640]{1,0:T(8,128)(2,1)S(1)} %unpack_back.1.rest_0_), channel_id=1, source_target_pairs={{0,6},{1,7},{2,4},{3,5},{4,2},{5,3},{6,0},{7,1},{8,14},{9,15},{10,... | collective-permute-start | bytes 245768 | tf_op jit(solution)/shard_map/ppermute | solution.py:860
  95.5 7.2 %collective-permute-start.5 = (bf16[64,640]{1,0:T(8,128)(2,1)S(1)}, bf16[64,640]{1,0:T(8,128)(2,1)S(1)}, u32[]{:S(2)}, u32[]{:S(2)}) collective-permute-start(bf16[64,640]{1,0:T(8,128)(2,1)S(1)} %unpack_back.1.rest_0_), channel_id=1, source_target_pairs={{0,4},{1,5},{2,6},{3,7},{4,0},{5,1},{6,2},{7,3},{8,12},{9,13},{10,... | collective-permute-start | bytes 245768 | tf_op jit(solution)/shard_map/ppermute | solution.py:860
  95.5 8.1 %collective-permute-start.4 = (bf16[64,640]{1,0:T(8,128)(2,1)S(1)}, bf16[64,640]{1,0:T(8,128)(2,1)S(1)}, u32[]{:S(2)}, u32[]{:S(2)}) collective-permute-start(bf16[64,640]{1,0:T(8,128)(2,1)S(1)} %unpack_back.1.rest_0_), channel_id=1, source_target_pairs={{0,2},{1,3},{2,0},{3,1},{4,6},{5,7},{6,4},{7,5},{8,10},{9,11},{10,... | collective-permute-start | bytes 245768 | tf_op jit(solution)/shard_map/ppermute | solution.py:860
  98.0 8.5 %collective-permute-start.7 = (bf16[64,640]{1,0:T(8,128)(2,1)S(1)}, bf16[64,640]{1,0:T(8,128)(2,1)S(1)}, u32[]{:S(2)}, u32[]{:S(2)}) collective-permute-start(bf16[64,640]{1,0:T(8,128)(2,1)S(1)} %unpack_back.1.rest_0_), channel_id=1, source_target_pairs={{0,1},{1,0},{2,3},{3,2},{4,5},{5,4},{6,7},{7,6},{8,9},{9,8},{10,11... | collective-permute-start | bytes 245768 | tf_op jit(solution)/shard_map/ppermute | solution.py:861
  101.2 5.3 %collective-permute-start.10 = (bf16[64,640]{1,0:T(8,128)(2,1)S(1)}, bf16[64,640]{1,0:T(8,128)(2,1)S(1)}, u32[]{:S(2)}, u32[]{:S(2)}) collective-permute-start(bf16[64,640]{1,0:T(8,128)(2,1)S(1)} %collective-permute-done.6.rest_3_), channel_id=1, source_target_pairs={{0,1},{1,0},{2,3},{3,2},{4,5},{5,4},{6,7},{7,6},{8,9},{9,8},{10,11... | collective-permute-start | bytes 245768 | tf_op jit(solution)/shard_map/ppermute | solution.py:861
  102.7 3.8 %collective-permute-start.9 = (bf16[64,640]{1,0:T(8,128)(2,1)S(1)}, bf16[64,640]{1,0:T(8,128)(2,1)S(1)}, u32[]{:S(2)}, u32[]{:S(2)}) collective-permute-start(bf16[64,640]{1,0:T(8,128)(2,1)S(1)} %collective-permute-done.5.rest_2_), channel_id=1, source_target_pairs={{0,1},{1,0},{2,3},{3,2},{4,5},{5,4},{6,7},{7,6},{8,9},{9,8},{10,11... | collective-permute-start | bytes 245768 | tf_op jit(solution)/shard_map/ppermute | solution.py:861
  103.6 2.9 %collective-permute-start.8 = (bf16[64,640]{1,0:T(8,128)(2,1)S(1)}, bf16[64,640]{1,0:T(8,128)(2,1)S(1)}, u32[]{:S(2)}, u32[]{:S(2)}) collective-permute-start(bf16[64,640]{1,0:T(8,128)(2,1)S(1)} %collective-permute-done.4.rest_1_), channel_id=1, source_target_pairs={{0,1},{1,0},{2,3},{3,2},{4,5},{5,4},{6,7},{7,6},{8,9},{9,8},{10,11... | collective-permute-start | bytes 245768 | tf_op jit(solution)/shard_map/ppermute | solution.py:861

commit v7 on v6

--- a/solution.py
+++ b/solution.py
@@ -14,7 +14,7 @@
 DIRECT = 2
 SPILL = 2
 STRIP = 16
-GROUP = 4
+GROUP = 8
 FLOOR = -1e30
 BF16 = jnp.bfloat16
 F32 = jnp.float32
@@ -141,11 +141,11 @@
 
 def pack_context_kernel(
     decode_slot, where, p_ref,
-    out_ref, placing, leaving, coming, relay, rounds,
-    counts, entered, buf, sems,
+    out_ref, placing, later, coming, relay, rounds,
+    leaving, counts, ahead, code, source, buf, sems,
 ):
     slots, feature, window = buf.shape
-    owners = counts.shape[0]
+    owners = out_ref.shape[0]
     padded = (out_ref.shape[1] - SPILL * STRIP) // DIRECT
     piece = padded * 128 // feature // 16 * 16
     rows = piece * feature // 128
@@ -178,6 +178,60 @@
         spilled = spilled + over.astype(jnp.int32)
     pick = picker(row, start, piece, window)
 
+    def clear(n, carry):
+        counts[n] = 0
+        return carry
+
+    lax.fori_loop(0, owners * owners, clear, 0, unroll=16)
+    first = where[1] * slots
+
+    def look(k, spilled):
+        after = []
+        for p in range(owners):
+            slot = decode_slot[p * slots + k]
+            owner = slot >> bits
+            rank = counts[p * owners + owner]
+            counts[p * owners + owner] = rank + 1
+            over = rank >= DIRECT
+            ahead[p * (SPILL + 1) + jnp.where(over, jnp.minimum(spilled[p], SPILL), SPILL)] = owner
+            inner = slot - first
+            at = jnp.where((inner >= 0) & (inner < slots), inner, slots)
+            coming[at] = jnp.where(over, spilled[p], -1)
+            source[at] = p
+            after.append(spilled[p] + over.astype(jnp.int32))
+        return tuple(after)
+
+    spilled = lax.fori_loop(0, slots, look, (jnp.int32(0),) * owners)
+    for q in range(owners):
+        counts[q] = 0
+    for n in range(owners * SPILL):
+        relay[n] = 0
+    longest = jnp.int32(0)
+    for p in range(owners):
+        hopped = jnp.int32(0)
+        for n in range(SPILL):
+            owner = jnp.where(n < spilled[p], ahead[p * (SPILL + 1) + n], 0)
+            entry = counts[owner]
+            hops = (n < spilled[p]) & (entry < SPILL)
+            counts[owner] = entry + hops.astype(jnp.int32)
+            relay[jnp.where(hops, owner * SPILL + entry, owners * SPILL)] = p * SPILL + n
+            code[p * (SPILL + 1) + n] = jnp.where(hops, entry, SPILL + n - hopped)
+            hopped = hopped + hops.astype(jnp.int32)
+        code[p * (SPILL + 1) + SPILL] = SPILL - hopped
+        longest = jnp.maximum(longest, spilled[p] - hopped)
+    rounds[0] = (longest + SPILL - 1) // SPILL
+
+    def coded(p, n):
+        found = code[p * (SPILL + 1) + jnp.clip(n, 0, SPILL)]
+        return jnp.where(n < 0, -1, jnp.where(n < SPILL, found, found + n))
+
+    def finish(n, carry):
+        coming[n] = coded(source[n], coming[n])
+        later[n] = coded(where[1], leaving[n])
+        return carry
+
+    lax.fori_loop(0, slots, finish, 0, unroll=4)
+
     for k, copy in enumerate(copies):
         copy.wait()
 
@@ -201,51 +255,7 @@
 
             return carry
 
-        lax.fori_loop(0, chunk, one, 0, unroll=2)
-
-    for q in range(owners):
-        entered[q] = 0
-        for e in range(SPILL):
-            relay[q * SPILL + e] = 0
-
-    def locate(p, longest):
-        for q in range(owners):
-            counts[q] = 0
-
-        def look(k, state):
-            spilled, left = state
-            slot = decode_slot[p * slots + k]
-            owner = slot >> bits
-            rank = counts[owner]
-            counts[owner] = rank + 1
-            over = rank >= DIRECT
-            hops = over & (spilled < SPILL) & (entered[owner] < SPILL)
-            entry = entered[owner]
-
-            @pl.when(hops)
-            def _():
-                entered[owner] = entry + 1
-                relay[owner * SPILL + entry] = p * SPILL + spilled
-
-            code = jnp.where(hops, entry, SPILL + left)
-            code = jnp.where(over, code, -1)
-
-            @pl.when(owner == where[1])
-            def _():
-                coming[slot & (slots - 1)] = code
-
-            @pl.when(p == where[1])
-            def _():
-                leaving[k] = code
-
-            rest = over & jnp.logical_not(hops)
-            return spilled + over.astype(jnp.int32), left + rest.astype(jnp.int32)
-
-        _, left = lax.fori_loop(0, slots, look, (jnp.int32(0), jnp.int32(0)), unroll=4)
-        return jnp.maximum(longest, left)
-
-    longest = lax.fori_loop(0, owners, locate, jnp.int32(0))
-    rounds[0] = (longest + SPILL - 1) // SPILL
+        lax.fori_loop(0, chunk, one, 0, unroll=4)
 
 
 def pack_context(decode_slot, where, prompt_latent, piece, pool_count):
@@ -257,15 +267,18 @@
             jax.ShapeDtypeStruct((pool_count, DIRECT * rows + SPILL * STRIP, 128), BF16),
             jax.ShapeDtypeStruct((slots,), jnp.int32),
             jax.ShapeDtypeStruct((slots,), jnp.int32),
-            jax.ShapeDtypeStruct((slots,), jnp.int32),
-            jax.ShapeDtypeStruct((pool_count * SPILL,), jnp.int32),
+            jax.ShapeDtypeStruct((slots + 8,), jnp.int32),
+            jax.ShapeDtypeStruct((pool_count * SPILL + 8,), jnp.int32),
             jax.ShapeDtypeStruct((1,), jnp.int32),
         ),
         in_specs=[SMEM_SPEC, SMEM_SPEC, ANY_SPEC],
         out_specs=(VMEM_SPEC,) + (SMEM_SPEC,) * 5,
         scratch_shapes=[
-            pltpu.SMEM((pool_count,), jnp.int32),
-            pltpu.SMEM((pool_count,), jnp.int32),
+            pltpu.SMEM((slots,), jnp.int32),
+            pltpu.SMEM((pool_count * pool_count,), jnp.int32),
+            pltpu.SMEM((pool_count * (SPILL + 1),), jnp.int32),
+            pltpu.SMEM((pool_count * (SPILL + 1),), jnp.int32),
+            pltpu.SMEM((slots + 8,), jnp.int32),
             pltpu.VMEM((slots, feature, 256), BF16),
             pltpu.SemaphoreType.DMA((4,)),
         ],
@@ -312,69 +325,59 @@
     )(turn, leaving, where, prompt_latent)
 
 
-def unpack_piece(packed, row, first_row, length, piece, feature):
+def unpack_piece(out_ref, row, packed, at, start, first_row, length):
+    piece, feature = out_ref.shape[1:]
     blocks = feature // 128
-    parts = [packed[(*row, pl.ds(b * piece, piece), slice(None))] for b in range(blocks)]
-    last = packed[(*row, pl.ds(blocks * piece, piece // 2), slice(None))].astype(F32)
-    last = jnp.concatenate([last[:, :64], last[:, 64:]], axis=0).astype(BF16)
-    whole = jnp.concatenate(parts + [last], axis=1)
-    position = first_row + lax.broadcasted_iota(jnp.int32, whole.shape, 0)
-    return jnp.where(position < length, whole.astype(F32), 0.0).astype(BF16)
-
-
-def place_kernel(
-    arrival, coming, lengths, where, direct, out_ref, inbox, outbox, in_sems, out_sems
-):
+    for b in range(blocks):
+        out_ref[row, :, 128 * b : 128 * b + 128] = packed[at, pl.ds(start + b * piece, piece), :]
+    last = packed[at, pl.ds(start + blocks * piece, piece // 2), :].astype(F32)
+    last = jnp.concatenate([last[:, :64], last[:, 64:]], axis=0)
+    out_ref[row, :, 128 * blocks :] = last.astype(BF16)
+
+    @pl.when(length < first_row + piece)
+    def _():
+        whole = out_ref[row].astype(F32)
+        position = first_row + lax.broadcasted_iota(jnp.int32, whole.shape, 0)
+        out_ref[row] = jnp.where(position < length, whole, 0.0).astype(BF16)
+
+
+def place_kernel(arrival, lengths, where, direct, out_ref, outbox, sems):
     slots, piece, feature = out_ref.shape
-    rows = inbox.shape[1]
-
-    def copy_in(j):
+    padded = (direct.shape[1] - SPILL * STRIP) // DIRECT
+    chunk = slots // sems.shape[0]
+
+    def copy_out(k):
+        part = pl.ds(k * chunk, chunk)
+        return pltpu.make_async_copy(outbox.at[part], out_ref.at[part], sems.at[k])
+
+    def one(j, carry):
         owner, rank = split(arrival[j])
-        rank = jnp.minimum(rank, DIRECT - 1)
-        source = direct.at[owner, pl.ds(pl.multiple_of(rank * rows, STRIP), rows), :]
-        return pltpu.make_async_copy(source, inbox.at[j], in_sems.at[j])
-
-    def copy_out(j):
-        return pltpu.make_async_copy(outbox.at[j], out_ref.at[j], out_sems.at[j])
-
-    def each(action):
-        def step(j, carry):
-            @pl.when(coming[j] < 0)
-            def _():
-                action(j)
-
-            return carry
-
-        lax.fori_loop(0, slots, step, 0)
-
-    def work(j):
-        copy_in(j).wait()
-        outbox[j] = unpack_piece(inbox, (j,), where[0] * piece, lengths[j], piece, feature)
-        copy_out(j).start()
-
-    each(lambda j: copy_in(j).start())
-    each(work)
-    each(lambda j: copy_out(j).wait())
-
-
-def place(arrival, coming, lengths, where, direct, piece, feature):
-    slots = coming.shape[0]
-    rows = padded_rows(piece, feature)
+        at = pl.multiple_of(jnp.minimum(rank, DIRECT - 1) * padded, STRIP)
+        unpack_piece(outbox, j, direct, owner, at, where[0] * piece, lengths[j])
+        return carry
+
+    for k in range(sems.shape[0]):
+        lax.fori_loop(k * chunk, k * chunk + chunk, one, 0, unroll=2)
+        copy_out(k).start()
+    for k in range(sems.shape[0]):
+        copy_out(k).wait()
+
+
+def place(arrival, lengths, where, direct, piece, feature):
+    slots = arrival.shape[0] - 8
     return pl.pallas_call(
         place_kernel,
         out_shape=jax.ShapeDtypeStruct((slots, piece, feature), BF16),
-        in_specs=[SMEM_SPEC] * 4 + [ANY_SPEC],
+        in_specs=[SMEM_SPEC] * 3 + [VMEM_SPEC],
         out_specs=ANY_SPEC,
         scratch_shapes=[
-            pltpu.VMEM((slots, rows, 128), BF16),
             pltpu.VMEM((slots, piece, feature), BF16),
-            pltpu.SemaphoreType.DMA((slots,)),
-            pltpu.SemaphoreType.DMA((slots,)),
+            pltpu.SemaphoreType.DMA((4,)),
         ],
         compiler_params=params(),
         cost_estimate=cost(bytes_accessed=12_000_000),
         name="place_context",
-    )(arrival, coming, lengths, where, direct)
+    )(arrival, lengths, where, direct)
 
 
 def place_strips_kernel(
@@ -410,7 +413,7 @@
         lax.fori_loop(0, slots, step, 0)
 
     def work(j, e):
-        outbox[e] = unpack_piece(whole, (e,), where[0] * piece, lengths[j], piece, feature)
+        unpack_piece(outbox, e, whole, e, 0, where[0] * piece, lengths[j])
         copy_out(j, e).start()
 
     each(work)
@@ -455,10 +458,8 @@
             )
             copy.start()
             copy.wait()
-            outbox[...] = unpack_piece(
-                inbox, (0,), where[0] * piece, lengths[j], piece, feature
-            )
-            copy = pltpu.make_async_copy(outbox, out_ref.at[j], sem)
+            unpack_piece(outbox, 0, inbox, 0, 0, where[0] * piece, lengths[j])
+            copy = pltpu.make_async_copy(outbox.at[0], out_ref.at[j], sem)
             copy.start()
             copy.wait()
 
@@ -475,7 +476,7 @@
         out_specs=ANY_SPEC,
         scratch_shapes=[
             pltpu.VMEM((1,) + spill.shape[-2:], BF16),
-            pltpu.VMEM(context.shape[1:], BF16),
+            pltpu.VMEM((1,) + context.shape[1:], BF16),
             pltpu.SemaphoreType.DMA,
         ],
         input_output_aliases={6: 0},
@@ -609,8 +610,8 @@
         rows = pl.ds(h, many, stride=heads)
         mixed = jnp.dot(fresh_score[rows, :].astype(BF16), values, preferred_element_type=F32)
         mixed = mixed + jnp.concatenate([acc[c, rows, :] for c in range(chunks)], axis=1)
-        part = total[rows, :]
-        mixed = (mixed / jnp.concatenate([part] * chunks, axis=1)).astype(BF16)
+        part = 1.0 / total[rows, :]
+        mixed = (mixed * jnp.concatenate([part] * chunks, axis=1)).astype(BF16)
         head_out[:, h * 128 : h * 128 + 128] = jnp.dot(
             mixed, w_uv[h], preferred_element_type=F32
         ).astype(BF16)
@@ -619,12 +620,12 @@
     core = where[0] % 2
     mine = head_out[pl.ds(pl.multiple_of(core * half, half), half), :]
     theirs = head_out[pl.ds(pl.multiple_of((1 - core) * half, half), half), :]
+    both = jnp.concatenate([theirs, mine], axis=0)
     for b in range(w_out.shape[1] // 512):
         at_b = slice(b * 512, b * 512 + 512)
-        given_ref[:, at_b] = jnp.dot(theirs, w_out[:, at_b], preferred_element_type=F32).astype(
-            BF16
-        )
-        kept_ref[:, at_b] = jnp.dot(mine, w_out[:, at_b], preferred_element_type=F32)
+        summed = jnp.dot(both, w_out[:, at_b], preferred_element_type=F32)
+        given_ref[:, at_b] = summed[:half].astype(BF16)
+        kept_ref[:, at_b] = summed[half:]
 
 
 def attention(placing, lengths, where, payload, prompt_latent, w_uk, w_uv, w_out, steps):
@@ -854,13 +855,12 @@
     parts = [lax.ppermute(part, "tp", hop) for part, hop in zip(parts, hops)]
 
     back = exchange(pack_back(placing, relay, direct, mine, parts))
-    context = place(arrival, coming, lengths, where, direct, piece, feature)
+    context = place(arrival, lengths, where, direct, piece, feature)
     back, context = lax.optimization_barrier((back, context))
     own = unpack_back(arrival, back, steps // 2, slots, out_width // z_count)
     parts = [own] + [lax.ppermute(own, "tp", hop) for hop in hops]
-    parts = parts + [lax.ppermute(part, "tp", swap) for part in parts]
+    swapped = [lax.ppermute(own, "tp", swap)]
     context = place_strips(coming, lengths, where, back, context)
-    decoded = assemble(where, parts, slots, steps, out_width)
 
     def more(state):
         turn, context = state
@@ -872,6 +872,9 @@
     context = lax.while_loop(
         lambda state: state[0][0] < rounds[0], more, (jnp.zeros((1,), jnp.int32), context)
     )[1]
+    context, *parts = lax.optimization_barrier((context, *parts))
+    parts = parts + swapped + [lax.ppermute(part, "tp", swap) for part in parts[1:]]
+    decoded = assemble(where, parts, slots, steps, out_width)
     return decoded, context
 
 

time: 109 us -> 105 us (0.963)
  Pallas kernels: 59.7 us -> 52.5 us
  waiting for transfers between devices: 8.22 us -> 12.4 us
  starting transfers between devices: 37.5 us -> 35.6 us
    all_to_all x3, waiting for transfers between devices: 0.85 us -> 4.1 us  [exchange(): return lax.all_to_all(x, 'pool', split_axis=0, concat_axis=0, tiled=True)]
    pallas_call x1, Pallas kernels: 7.01 us -> 3.76 us  [place(): pl.pallas_call(place_kernel, out_shape=jax.ShapeDtypeStruct((slots, piece...]
    pallas_call x1, Pallas kernels: 19.3 us -> 17.1 us  [pack_context(): pl.pallas_call(pack_context_kernel, out_shape=(jax.ShapeDtypeStruct((pool...]
    ppermute x4, starting transfers between devices: 6.42 us -> 4.44 us  [the longest x1 3.14 us: body(): swapped = [lax.ppermute(own, 'tp', swap)]]
    pallas_call x1, Pallas kernels: 21.4 us -> 19.9 us  [attention(): pl.pallas_call(attention_kernel, out_shape=(jax.ShapeDtypeStruct((half, w...]
  transfers between devices with their start and end apart: 14 -> 14, of which waited for: 4 -> 7; matrix products, arithmetic and copies ran while one was open for 0% -> 0% of each run, Pallas kernels for 46% -> 41%
where the time goes in v7:
time: 105 us; the launch traced here: 104 us
  Pallas kernels  52.5 us (50%)
  starting transfers between devices  35.6 us (34%)
  waiting for transfers between devices  12.4 us (12%)
  local copies, waits for them, and re-layouts  2.1 us (2%)
    all_to_all x3, starting transfers between devices, exchange(): return lax.all_to_all(x, 'pool', split_axis=0, concat_axis=0, tiled=True)  21.2 us
    pallas_call x1, Pallas kernels, attention(): pl.pallas_call(attention_kernel, out_shape=(jax.ShapeDtypeStruct((half, w...  19.9 us
    pallas_call x1, Pallas kernels, pack_context(): pl.pallas_call(pack_context_kernel, out_shape=(jax.ShapeDtypeStruct((pool...  17.1 us
    ppermute x3, waiting for transfers between devices, body(): parts = [lax.ppermute(part, 'tp', hop) for part, hop in zip(parts, hops)]  5.88 us
    ppermute x3, starting transfers between devices, body(): parts = [lax.ppermute(part, 'tp', hop) for part, hop in zip(parts, hops)]  5.02 us
    pallas_call x1, Pallas kernels, pack_queries(): pl.pallas_call(pack_queries_kernel, out_shape=(jax.ShapeDtypeStruct((pool...  4.79 us
    all_to_all x3, waiting for transfers between devices, exchange(): return lax.all_to_all(x, 'pool', split_axis=0, concat_axis=0, tiled=True)  4.1 us
    pallas_call x1, Pallas kernels, place(): pl.pallas_call(place_kernel, out_shape=jax.ShapeDtypeStruct((slots, piece...  3.76 us
  transfers between devices with their start and end apart: 14, of which 7 were waited for; matrix products, arithmetic and copies ran while one was open for 0% of the time, Pallas kernels for 41%

profile of v7, /device:TPU:1, one launch (start us, length us, event | category | flops | bytes accessed | tf_op | source)
XLA Modules:
  0.0 104.1 jit_solution(2158361674364832300)
XLA Ops:
  0.7 4.8 %pack_queries.1 = (bf16[16,264,128]{2,1,0:T(8,128)(2,1)}, s32[40]{0:T(128)S(1)}, s32[40]{0:T(128)S(1)}) custom-call(s32[512]{0:T(512)} %decode_slot.3, s32[512]{0:T(512)} %lengths.1, s32[2]{0:T(128)S(1)} %pad_add_fusion.where, bf16[4,32,8,192]{3,2,1,0:T(8,128)(2,1)} %q_hbm.1, bf16[4,32,576]{2,1,0:T(8,128)(2,1)} %n_hbm.1), custom_call_target="tpu_custom_call" | custom-call | flops 1000 | bytes 1000 | tf_op jit(solution)/shard_map/pack_queries/pallas_call | solution.py:94
  5.5 7.6 %all-to-all-start.1 = ((bf16[16,264,128]{2,1,0:T(8,128)(2,1)}), bf16[16,264,128]{2,1,0:T(8,128)(2,1)S(1)}, u32[]{:S(2)}, u32[]{:S(2)}) async-start(bf16[16,264,128]{2,1,0:T(8,128)(2,1)} %get-tuple-element.78), calls=%async_computation.1 | async-start | bytes 2162688 | tf_op jit(solution)/shard_map/all_to_all | solution.py:822
  13.1 17.1 %pack_context.1 = (bf16[16,480,128]{2,1,0:T(8,128)(2,1)}, s32[32]{0:T(128)}, s32[32]{0:T(128)S(1)}, s32[40]{0:T(128)S(1)}, s32[40]{0:T(128)}, /*index=5*/s32[1]{0:T(128)}) custom-call(s32[512]{0:T(512)} %decode_slot.3, s32[2]{0:T(128)S(1)} %pad_add_fusion.where, bf16[32,576,384]{2,1,0:T(8,128)(2,1)} %bitcast.5), custom_call_target="tpu_custom_call" | custom-call | flops 1000 | bytes 1000 | tf_op jit(solution)/shard_map/pack_context/pallas_call | solution.py:264
  30.2 1.0 copy-done.3
  31.2 6.6 %all-to-all-start.2 = ((bf16[16,480,128]{2,1,0:T(8,128)(2,1)}), bf16[16,480,128]{2,1,0:T(8,128)(2,1)S(1)}, u32[]{:S(2)}, u32[]{:S(2)}) async-start(bf16[16,480,128]{2,1,0:T(8,128)(2,1)} %get-tuple-element.80), calls=%async_computation.2 | async-start | bytes 3932160 | tf_op jit(solution)/shard_map/all_to_all | solution.py:822
  37.9 19.9 %attention.1 = (bf16[64,2560]{1,0:T(8,128)(2,1)}, f32[64,2560]{1,0:T(8,128)}) custom-call(s32[32]{0:T(128)} %get-tuple-element.76.placing, s32[512]{0:T(512)} %lengths.1, s32[2]{0:T(128)S(1)} %pad_add_fusion.where, bf16[16,264,128]{2,1,0:T(8,128)(2,1)} %copy-done.3, bf16[32,576,384]{2,1,0:T(8,128)(2,1)} %bitcast.6, bf16[8,512,128]{2,1,0:T(8,128)(2,1)} %w_uk_hbm.1, ...), custom_call_target="tpu_custom_call" | custom-call | flops 1000 | bytes 1000 | tf_op jit(solution)/shard_map/attention/pallas_call | solution.py:638
  57.8 1.6 %collective-permute-start = (bf16[64,2560]{1,0:T(8,128)(2,1)}, bf16[64,2560]{1,0:T(8,128)(2,1)S(1)}, u32[]{:S(2)}, u32[]{:S(2)}) collective-permute-start(bf16[64,2560]{1,0:T(8,128)(2,1)} %get-tuple-element.83), channel_id=1, source_target_pairs={{0,1},{1,0},{2,3},{3,2},{4,5},{5,4},{6,7},{7,6},{8,9},{9,8},{10,11... | collective-permute-start | bytes 983048 | tf_op jit(solution)/shard_map/ppermute | solution.py:853
  59.4 1.5 %collective-permute-done.swapped = bf16[64,2560]{1,0:T(8,128)(2,1)S(1)} collective-permute-done((bf16[64,2560]{1,0:T(8,128)(2,1)}, bf16[64,2560]{1,0:T(8,128)(2,1)S(1)}, u32[]{:S(2)}, u32[]{:S(2)}) %collective-permute-start) | collective-permute-done | bytes 327712 | tf_op jit(solution)/shard_map/ppermute | solution.py:853
  60.8 1.1 %copy-done = f32[64,2560]{1,0:T(8,128)S(1)} copy-done((f32[64,2560]{1,0:T(8,128)S(1)}, f32[64,2560]{1,0:T(8,128)}, u32[]{:S(2)}) %copy-start) | copy-done | bytes 655384
  62.5 1.7 %collective-permute-start.1 = (bf16[64,640]{1,0:T(8,128)(2,1)S(1)}, bf16[64,640]{1,0:T(8,128)(2,1)S(1)}, u32[]{:S(2)}, u32[]{:S(2)}) collective-permute-start(bf16[64,640]{1,0:T(8,128)(2,1)S(1)} %get-tuple-element.85), channel_id=1, source_target_pairs={{0,2},{1,3},{2,0},{3,1},{4,6},{5,7},{6,4},{7,5},{8,10},{9,11},{10,... | collective-permute-start | bytes 245768 | tf_op jit(solution)/shard_map/ppermute | solution.py:855
  64.3 3.3 %collective-permute-start.2 = (bf16[64,640]{1,0:T(8,128)(2,1)S(1)}, bf16[64,640]{1,0:T(8,128)(2,1)S(1)}, u32[]{:S(2)}, u32[]{:S(2)}) collective-permute-start(bf16[64,640]{1,0:T(8,128)(2,1)S(1)} %get-tuple-element.86), channel_id=1, source_target_pairs={{0,4},{1,5},{2,6},{3,7},{4,0},{5,1},{6,2},{7,3},{8,12},{9,13},{10,... | collective-permute-start | bytes 245768 | tf_op jit(solution)/shard_map/ppermute | solution.py:855
  67.6 3.9 %collective-permute-done.2.rest_1_ = bf16[64,640]{1,0:T(8,128)(2,1)S(1)} collective-permute-done((bf16[64,640]{1,0:T(8,128)(2,1)S(1)}, bf16[64,640]{1,0:T(8,128)(2,1)S(1)}, u32[]{:S(2)}, u32[]{:S(2)}) %collective-permute-start.2) | collective-permute-done | bytes 81952 | tf_op jit(solution)/shard_map/ppermute | solution.py:855
  71.5 1.9 %collective-permute-done.3.rest_2_ = bf16[64,640]{1,0:T(8,128)(2,1)S(1)} collective-permute-done((bf16[64,640]{1,0:T(8,128)(2,1)S(1)}, bf16[64,640]{1,0:T(8,128)(2,1)S(1)}, u32[]{:S(2)}, u32[]{:S(2)}) %collective-permute-start.3) | collective-permute-done | bytes 81952 | tf_op jit(solution)/shard_map/ppermute | solution.py:855
  73.5 1.8 %pack_back.1 = bf16[16,72,128]{2,1,0:T(8,128)(2,1)} custom-call(s32[32]{0:T(128)S(1)} %copy-done.1, s32[40]{0:T(128)S(1)} %copy-done.2, bf16[16,480,128]{2,1,0:T(8,128)(2,1)S(1)} %all-to-all-done.2.direct, f32[64,640]{1,0:T(8,128)S(1)} %get-tuple-element.84.mine, bf16[64,640]{1,0:T(8,128)(2,1)S(1)} %collective-permute-done.1.rest_0_, ...), custom_call_target="tpu_custom_call" | custom-call | flops 1000 | bytes 1000 | tf_op jit(solution)/shard_map/pack_back/pallas_call | solution.py:732
  75.3 7.0 %all-to-all-start.3 = ((bf16[16,72,128]{2,1,0:T(8,128)(2,1)}), bf16[16,72,128]{2,1,0:T(8,128)(2,1)S(1)}, u32[]{:S(2)}, u32[]{:S(2)}) async-start(bf16[16,72,128]{2,1,0:T(8,128)(2,1)} %pack_back.1), calls=%async_computation.3 | async-start | bytes 589824 | tf_op jit(solution)/shard_map/all_to_all | solution.py:822
  82.3 3.8 %place_context.1.context = bf16[32,48,576]{2,1,0:T(8,128)(2,1)} custom-call(s32[40]{0:T(128)S(1)} %get-tuple-element.170.arrival, s32[40]{0:T(128)S(1)} %get-tuple-element.172.lengths, s32[2]{0:T(128)S(1)} %pad_add_fusion.where, bf16[16,480,128]{2,1,0:T(8,128)(2,1)S(1)} %all-to-all-done.2.direct), custom_call_target="tpu_custom_call" | custom-call | flops 1000 | bytes 12000000 | tf_op jit(solution)/shard_map/place_context/pallas_call | solution.py:368
  86.0 4.1 %all-to-all-done.3.back.packed = bf16[16,72,128]{2,1,0:T(8,128)(2,1)S(1)} async-done(((bf16[16,72,128]{2,1,0:T(8,128)(2,1)}), bf16[16,72,128]{2,1,0:T(8,128)(2,1)S(1)}, u32[]{:S(2)}, u32[]{:S(2)}) %all-to-all-start.3) | async-done | bytes 294944 | tf_op jit(solution)/shard_map/all_to_all | solution.py:822
  90.1 0.9 unpack_back.1.rest_0_
  91.0 0.8 collective-permute-start.6
  91.8 2.5 %collective-permute-start.4 = (bf16[64,640]{1,0:T(8,128)(2,1)S(1)}, bf16[64,640]{1,0:T(8,128)(2,1)S(1)}, u32[]{:S(2)}, u32[]{:S(2)}) collective-permute-start(bf16[64,640]{1,0:T(8,128)(2,1)S(1)} %unpack_back.1.rest_0_), channel_id=1, source_target_pairs={{0,2},{1,3},{2,0},{3,1},{4,6},{5,7},{6,4},{7,5},{8,10},{9,11},{10,... | collective-permute-start | bytes 245768 | tf_op jit(solution)/shard_map/ppermute | solution.py:861
  94.3 3.1 %collective-permute-start.7 = (bf16[64,640]{1,0:T(8,128)(2,1)S(1)}, bf16[64,640]{1,0:T(8,128)(2,1)S(1)}, u32[]{:S(2)}, u32[]{:S(2)}) collective-permute-start(bf16[64,640]{1,0:T(8,128)(2,1)S(1)} %unpack_back.1.rest_0_), channel_id=1, source_target_pairs={{0,1},{1,0},{2,3},{3,2},{4,5},{5,4},{6,7},{7,6},{8,9},{9,8},{10,11... | collective-permute-start | bytes 245768 | tf_op jit(solution)/shard_map/ppermute | solution.py:862
  97.5 1.8 %place_strips.1 = bf16[32,48,576]{2,1,0:T(8,128)(2,1)} custom-call(s32[40]{0:T(128)S(1)} %get-tuple-element.171.coming, s32[40]{0:T(128)S(1)} %get-tuple-element.172.lengths, s32[2]{0:T(128)S(1)} %pad_add_fusion.where, bf16[16,72,128]{2,1,0:T(8,128)(2,1)S(1)} %all-to-all-done.3.back.packed, ...), custom_call_target="tpu_custom_call", output_to_operand_aliasing={{}: (4, {})} | custom-call | flops 1000 | bytes 6000000 | tf_op jit(solution)/shard_map/place_strips/pallas_call | solution.py:426
  100.0 0.8 collective-permute-start.8
  102.2 1.9 %assemble.1 = bf16[32,4,2560]{2,1,0:T(4,128)(2,1)} custom-call(s32[2]{0:T(128)S(1)} %get-tuple-element.225, bf16[64,640]{1,0:T(8,128)(2,1)S(1)} %unpack_back.1.rest_0_, bf16[64,640]{1,0:T(8,128)(2,1)S(1)} %collective-permute-done.4.rest_1_, bf16[64,640]{1,0:T(8,128)(2,1)S(1)} %collective-permute-done.5.rest_2_, ...), custom_call_target="tpu_custom_call" | custom-call | flops 1000 | bytes 1000 | tf_op jit(solution)/shard_map/assemble/pallas_call | solution.py:806
  (23 shorter events, 2.8 us)
Async XLA Ops:
  5.5 24.7 %all-to-all-start.1 = ((bf16[16,264,128]{2,1,0:T(8,128)(2,1)}), bf16[16,264,128]{2,1,0:T(8,128)(2,1)S(1)}, u32[]{:S(2)}, u32[]{:S(2)}) async-start(bf16[16,264,128]{2,1,0:T(8,128)(2,1)} %get-tuple-element.78), calls=%async_computation.1 | async-start | bytes 2162688 | tf_op jit(solution)/shard_map/all_to_all | solution.py:822
  30.2 1.0 copy-start.3
  31.2 42.2 %all-to-all-start.2 = ((bf16[16,480,128]{2,1,0:T(8,128)(2,1)}), bf16[16,480,128]{2,1,0:T(8,128)(2,1)S(1)}, u32[]{:S(2)}, u32[]{:S(2)}) async-start(bf16[16,480,128]{2,1,0:T(8,128)(2,1)} %get-tuple-element.80), calls=%async_computation.2 | async-start | bytes 3932160 | tf_op jit(solution)/shard_map/all_to_all | solution.py:822
  37.9 35.6 %copy-start.1 = (s32[32]{0:T(128)S(1)}, s32[32]{0:T(128)}, u32[]{:S(2)}) copy-start(s32[32]{0:T(128)} %get-tuple-element.76.placing) | copy-start | bytes 388
  37.9 35.6 %copy-start.2 = (s32[40]{0:T(128)S(1)}, s32[40]{0:T(128)}, u32[]{:S(2)}) copy-start(s32[40]{0:T(128)} %get-tuple-element.77.relay) | copy-start | bytes 484
  57.8 3.1 %collective-permute-start = (bf16[64,2560]{1,0:T(8,128)(2,1)}, bf16[64,2560]{1,0:T(8,128)(2,1)S(1)}, u32[]{:S(2)}, u32[]{:S(2)}) collective-permute-start(bf16[64,2560]{1,0:T(8,128)(2,1)} %get-tuple-element.83), channel_id=1, source_target_pairs={{0,1},{1,0},{2,3},{3,2},{4,5},{5,4},{6,7},{7,6},{8,9},{9,8},{10,11... | collective-permute-start | bytes 983048 | tf_op jit(solution)/shard_map/ppermute | solution.py:853
  60.8 1.1 %copy-start = (f32[64,2560]{1,0:T(8,128)S(1)}, f32[64,2560]{1,0:T(8,128)}, u32[]{:S(2)}) copy-start(f32[64,2560]{1,0:T(8,128)} %get-tuple-element.82.kept) | copy-start | bytes 1966084
  62.5 5.0 %collective-permute-start.1 = (bf16[64,640]{1,0:T(8,128)(2,1)S(1)}, bf16[64,640]{1,0:T(8,128)(2,1)S(1)}, u32[]{:S(2)}, u32[]{:S(2)}) collective-permute-start(bf16[64,640]{1,0:T(8,128)(2,1)S(1)} %get-tuple-element.85), channel_id=1, source_target_pairs={{0,2},{1,3},{2,0},{3,1},{4,6},{5,7},{6,4},{7,5},{8,10},{9,11},{10,... | collective-permute-start | bytes 245768 | tf_op jit(solution)/shard_map/ppermute | solution.py:855
  64.3 7.2 %collective-permute-start.2 = (bf16[64,640]{1,0:T(8,128)(2,1)S(1)}, bf16[64,640]{1,0:T(8,128)(2,1)S(1)}, u32[]{:S(2)}, u32[]{:S(2)}) collective-permute-start(bf16[64,640]{1,0:T(8,128)(2,1)S(1)} %get-tuple-element.86), channel_id=1, source_target_pairs={{0,4},{1,5},{2,6},{3,7},{4,0},{5,1},{6,2},{7,3},{8,12},{9,13},{10,... | collective-permute-start | bytes 245768 | tf_op jit(solution)/shard_map/ppermute | solution.py:855
  67.6 5.9 %collective-permute-start.3 = (bf16[64,640]{1,0:T(8,128)(2,1)S(1)}, bf16[64,640]{1,0:T(8,128)(2,1)S(1)}, u32[]{:S(2)}, u32[]{:S(2)}) collective-permute-start(bf16[64,640]{1,0:T(8,128)(2,1)S(1)} %get-tuple-element.87), channel_id=1, source_target_pairs={{0,6},{1,7},{2,4},{3,5},{4,2},{5,3},{6,0},{7,1},{8,14},{9,15},{10,... | collective-permute-start | bytes 245768 | tf_op jit(solution)/shard_map/ppermute | solution.py:855
  75.3 14.8 %all-to-all-start.3 = ((bf16[16,72,128]{2,1,0:T(8,128)(2,1)}), bf16[16,72,128]{2,1,0:T(8,128)(2,1)S(1)}, u32[]{:S(2)}, u32[]{:S(2)}) async-start(bf16[16,72,128]{2,1,0:T(8,128)(2,1)} %pack_back.1), calls=%async_computation.3 | async-start | bytes 589824 | tf_op jit(solution)/shard_map/all_to_all | solution.py:822
  91.0 8.9 %collective-permute-start.6 = (bf16[64,640]{1,0:T(8,128)(2,1)S(1)}, bf16[64,640]{1,0:T(8,128)(2,1)S(1)}, u32[]{:S(2)}, u32[]{:S(2)}) collective-permute-start(bf16[64,640]{1,0:T(8,128)(2,1)S(1)} %unpack_back.1.rest_0_), channel_id=1, source_target_pairs={{0,6},{1,7},{2,4},{3,5},{4,2},{5,3},{6,0},{7,1},{8,14},{9,15},{10,... | collective-permute-start | bytes 245768 | tf_op jit(solution)/shard_map/ppermute | solution.py:861
  91.8 8.1 %collective-permute-start.5 = (bf16[64,640]{1,0:T(8,128)(2,1)S(1)}, bf16[64,640]{1,0:T(8,128)(2,1)S(1)}, u32[]{:S(2)}, u32[]{:S(2)}) collective-permute-start(bf16[64,640]{1,0:T(8,128)(2,1)S(1)} %unpack_back.1.rest_0_), channel_id=1, source_target_pairs={{0,4},{1,5},{2,6},{3,7},{4,0},{5,1},{6,2},{7,3},{8,12},{9,13},{10,... | collective-permute-start | bytes 245768 | tf_op jit(solution)/shard_map/ppermute | solution.py:861
  91.8 8.1 %collective-permute-start.4 = (bf16[64,640]{1,0:T(8,128)(2,1)S(1)}, bf16[64,640]{1,0:T(8,128)(2,1)S(1)}, u32[]{:S(2)}, u32[]{:S(2)}) collective-permute-start(bf16[64,640]{1,0:T(8,128)(2,1)S(1)} %unpack_back.1.rest_0_), channel_id=1, source_target_pairs={{0,2},{1,3},{2,0},{3,1},{4,6},{5,7},{6,4},{7,5},{8,10},{9,11},{10,... | collective-permute-start | bytes 245768 | tf_op jit(solution)/shard_map/ppermute | solution.py:861
  94.3 6.9 %collective-permute-start.7 = (bf16[64,640]{1,0:T(8,128)(2,1)S(1)}, bf16[64,640]{1,0:T(8,128)(2,1)S(1)}, u32[]{:S(2)}, u32[]{:S(2)}) collective-permute-start(bf16[64,640]{1,0:T(8,128)(2,1)S(1)} %unpack_back.1.rest_0_), channel_id=1, source_target_pairs={{0,1},{1,0},{2,3},{3,2},{4,5},{5,4},{6,7},{7,6},{8,9},{9,8},{10,11... | collective-permute-start | bytes 245768 | tf_op jit(solution)/shard_map/ppermute | solution.py:862
  100.0 1.7 %collective-permute-start.8 = (bf16[64,640]{1,0:T(8,128)(2,1)S(1)}, bf16[64,640]{1,0:T(8,128)(2,1)S(1)}, u32[]{:S(2)}, u32[]{:S(2)}) collective-permute-start(bf16[64,640]{1,0:T(8,128)(2,1)S(1)} %collective-permute-done.4.rest_1_), channel_id=1, source_target_pairs={{0,1},{1,0},{2,3},{3,2},{4,5},{5,4},{6,7},{7,6},{8,9},{9,8},{10,11... | collective-permute-start | bytes 245768 | tf_op jit(solution)/shard_map/ppermute | solution.py:876
  100.8 1.3 %collective-permute-start.9 = (bf16[64,640]{1,0:T(8,128)(2,1)S(1)}, bf16[64,640]{1,0:T(8,128)(2,1)S(1)}, u32[]{:S(2)}, u32[]{:S(2)}) collective-permute-start(bf16[64,640]{1,0:T(8,128)(2,1)S(1)} %collective-permute-done.5.rest_2_), channel_id=1, source_target_pairs={{0,1},{1,0},{2,3},{3,2},{4,5},{5,4},{6,7},{7,6},{8,9},{9,8},{10,11... | collective-permute-start | bytes 245768 | tf_op jit(solution)/shard_map/ppermute | solution.py:876
  100.8 1.4 %collective-permute-start.10 = (bf16[64,640]{1,0:T(8,128)(2,1)S(1)}, bf16[64,640]{1,0:T(8,128)(2,1)S(1)}, u32[]{:S(2)}, u32[]{:S(2)}) collective-permute-start(bf16[64,640]{1,0:T(8,128)(2,1)S(1)} %collective-permute-done.6.rest_3_), channel_id=1, source_target_pairs={{0,1},{1,0},{2,3},{3,2},{4,5},{5,4},{6,7},{7,6},{8,9},{9,8},{10,11... | collective-permute-start | bytes 245768 | tf_op jit(solution)/shard_map/ppermute | solution.py:876

commit v8 on v7

--- a/solution.py
+++ b/solution.py
@@ -282,7 +282,7 @@
             pltpu.VMEM((slots, feature, 256), BF16),
             pltpu.SemaphoreType.DMA((4,)),
         ],
-        compiler_params=params(60),
+        compiler_params=params(63),
         cost_estimate=cost(),
         name="pack_context",
     )(decode_slot, where, prompt_latent)
@@ -549,7 +549,7 @@
         )
         return carry
 
-    lax.fori_loop(0, slots, unpack, 0, unroll=4)
+    lax.fori_loop(0, slots, unpack, 0, unroll=8)
     copy_uk.wait()
     for h in range(heads):
         rows = pl.ds(h, many, stride=heads)
@@ -569,7 +569,7 @@
         fresh_score[rows, :] = scale * lax.dot_general(q, keys, NT, preferred_element_type=F32)
         return carry
 
-    lax.fori_loop(0, per_step * steps // 128, score, 0)
+    lax.fori_loop(0, per_step * steps // 128, score, 0, unroll=2)
 
     def one(i):
         q = jnp.concatenate(
@@ -625,7 +625,7 @@
         at_b = slice(b * 512, b * 512 + 512)
         summed = jnp.dot(both, w_out[:, at_b], preferred_element_type=F32)
         given_ref[:, at_b] = summed[:half].astype(BF16)
-        kept_ref[:, at_b] = summed[half:]
+        kept_ref[:, at_b] = summed[half:].astype(BF16)
 
 
 def attention(placing, lengths, where, payload, prompt_latent, w_uk, w_uv, w_out, steps):
@@ -639,7 +639,7 @@
         attention_kernel,
         out_shape=(
             jax.ShapeDtypeStruct((half, width), BF16),
-            jax.ShapeDtypeStruct((half, width), F32),
+            jax.ShapeDtypeStruct((half, width), BF16),
         ),
         in_specs=[SMEM_SPEC] * 3 + [ANY_SPEC] * 5,
         out_specs=(VMEM_SPEC, VMEM_SPEC),
@@ -670,7 +670,7 @@
     z = where[0] >> 1
     for d, part in enumerate((mine,) + parts):
         at = pl.ds(pl.multiple_of((z ^ d) * block, 128), block)
-        part[...] = (kept[:, at] + swapped[:, at].astype(F32)).astype(part.dtype)
+        part[...] = (kept[:, at].astype(F32) + swapped[:, at].astype(F32)).astype(part.dtype)
 
 
 def share(where, kept, swapped, z_count):
@@ -703,8 +703,6 @@
         whole = whole + part[...].astype(F32)
     for b in range(blocks):
         total[b] = whole[:, 128 * b : 128 * b + 128]
-    rows[...] = jnp.zeros(rows.shape, F32)
-
     def one(i, carry):
         dest, rank = split(placing[i])
         for s in range(steps):
@@ -795,11 +793,10 @@
                 whole[start + b, pl.ds((steps // 2) * side + s, slots, stride=steps), :] = part[
                     pl.ds(s, slots, stride=steps // 2), :
                 ]
-    for j in range(slots):
-        for b in range(width // 128):
-            out_ref[j, :, 128 * b : 128 * b + 128] = whole[
-                b, steps * j : steps * j + steps, :
-            ].astype(BF16)
+    for b in range(width // 128):
+        out_ref[:, :, 128 * b : 128 * b + 128] = (
+            whole[b].reshape(slots, steps, 128).astype(BF16)
+        )
 
 
 def assemble(where, parts, slots, steps, width):

time: 105 us -> 102 us (0.971)
  local copies, waits for them, and re-layouts: 2.1 us -> 0.98 us
    unnamed x8 -> x6, local copies, waits for them, and re-layouts: 2.1 us -> 0.98 us
  transfers between devices with their start and end apart: 14 -> 14, of which waited for: 7 -> 7; matrix products, arithmetic and copies ran while one was open for 0% -> 0% of each run, Pallas kernels for 41% -> 42%
where the time goes in v8:
time: 102 us
  Pallas kernels  51.6 us (51%)
  starting transfers between devices  35.4 us (35%)
  waiting for transfers between devices  12.4 us (12%)
    all_to_all x3, starting transfers between devices, exchange(): return lax.all_to_all(x, 'pool', split_axis=0, concat_axis=0, tiled=True)  21.2 us
    pallas_call x1, Pallas kernels, attention(): pl.pallas_call(attention_kernel, out_shape=(jax.ShapeDtypeStruct((half, w...  19 us
    pallas_call x1, Pallas kernels, pack_context(): pl.pallas_call(pack_context_kernel, out_shape=(jax.ShapeDtypeStruct((pool...  17.1 us
    ppermute x3, waiting for transfers between devices, body(): parts = [lax.ppermute(part, 'tp', hop) for part, hop in zip(parts, hops)]  5.88 us
    ppermute x3, starting transfers between devices, body(): parts = [lax.ppermute(part, 'tp', hop) for part, hop in zip(parts, hops)]  5.02 us
    pallas_call x1, Pallas kernels, pack_queries(): pl.pallas_call(pack_queries_kernel, out_shape=(jax.ShapeDtypeStruct((pool...  4.76 us
    all_to_all x3, waiting for transfers between devices, exchange(): return lax.all_to_all(x, 'pool', split_axis=0, concat_axis=0, tiled=True)  4.1 us
    pallas_call x1, Pallas kernels, place(): pl.pallas_call(place_kernel, out_shape=jax.ShapeDtypeStruct((slots, piece...  3.76 us
  transfers between devices with their start and end apart: 14, of which 7 were waited for; matrix products, arithmetic and copies ran while one was open for 0% of the time, Pallas kernels for 42%

profile of v8, /device:TPU:1, one launch (start us, length us, event | category | flops | bytes accessed | tf_op | source)
XLA Modules:
  0.0 102.0 jit_solution(16302971666225267242)
XLA Ops:
  0.7 4.8 %pack_queries.1 = (bf16[16,264,128]{2,1,0:T(8,128)(2,1)}, s32[40]{0:T(128)S(1)}, s32[40]{0:T(128)S(1)}) custom-call(s32[512]{0:T(512)} %decode_slot.3, s32[512]{0:T(512)} %lengths.1, s32[2]{0:T(128)S(1)} %pad_add_fusion.where, bf16[4,32,8,192]{3,2,1,0:T(8,128)(2,1)} %q_hbm.1, bf16[4,32,576]{2,1,0:T(8,128)(2,1)} %n_hbm.1), custom_call_target="tpu_custom_call" | custom-call | flops 1000 | bytes 1000 | tf_op jit(solution)/shard_map/pack_queries/pallas_call | solution.py:94
  5.5 7.6 %all-to-all-start.1 = ((bf16[16,264,128]{2,1,0:T(8,128)(2,1)}), bf16[16,264,128]{2,1,0:T(8,128)(2,1)}, u32[]{:S(2)}, u32[]{:S(2)}) async-start(bf16[16,264,128]{2,1,0:T(8,128)(2,1)} %get-tuple-element.78), calls=%async_computation.1 | async-start | bytes 2162688 | tf_op jit(solution)/shard_map/all_to_all | solution.py:819
  13.1 17.1 %pack_context.1 = (bf16[16,480,128]{2,1,0:T(8,128)(2,1)}, s32[32]{0:T(128)}, s32[32]{0:T(128)S(1)}, s32[40]{0:T(128)S(1)}, s32[40]{0:T(128)}, /*index=5*/s32[1]{0:T(128)}) custom-call(s32[512]{0:T(512)} %decode_slot.3, s32[2]{0:T(128)S(1)} %pad_add_fusion.where, bf16[32,576,384]{2,1,0:T(8,128)(2,1)} %bitcast.5), custom_call_target="tpu_custom_call" | custom-call | flops 1000 | bytes 1000 | tf_op jit(solution)/shard_map/pack_context/pallas_call | solution.py:264
  30.2 6.6 %all-to-all-start.2 = ((bf16[16,480,128]{2,1,0:T(8,128)(2,1)}), bf16[16,480,128]{2,1,0:T(8,128)(2,1)S(1)}, u32[]{:S(2)}, u32[]{:S(2)}) async-start(bf16[16,480,128]{2,1,0:T(8,128)(2,1)} %get-tuple-element.80), calls=%async_computation.2 | async-start | bytes 3932160 | tf_op jit(solution)/shard_map/all_to_all | solution.py:819
  36.9 19.0 %attention.1 = (bf16[64,2560]{1,0:T(8,128)(2,1)}, bf16[64,2560]{1,0:T(8,128)(2,1)}) custom-call(s32[32]{0:T(128)} %get-tuple-element.76.placing, s32[512]{0:T(512)} %lengths.1, s32[2]{0:T(128)S(1)} %pad_add_fusion.where, bf16[16,264,128]{2,1,0:T(8,128)(2,1)} %all-to-all-done.1.payload_hbm, bf16[32,576,384]{2,1,0:T(8,128)(2,1)} %bitcast.6, ...), custom_call_target="tpu_custom_call" | custom-call | flops 1000 | bytes 1000 | tf_op jit(solution)/shard_map/attention/pallas_call | solution.py:638
  55.8 1.6 %collective-permute-start = (bf16[64,2560]{1,0:T(8,128)(2,1)}, bf16[64,2560]{1,0:T(8,128)(2,1)S(1)}, u32[]{:S(2)}, u32[]{:S(2)}) collective-permute-start(bf16[64,2560]{1,0:T(8,128)(2,1)} %get-tuple-element.83), channel_id=1, source_target_pairs={{0,1},{1,0},{2,3},{3,2},{4,5},{5,4},{6,7},{7,6},{8,9},{9,8},{10,11... | collective-permute-start | bytes 983048 | tf_op jit(solution)/shard_map/ppermute | solution.py:850
  57.4 1.5 %collective-permute-done.swapped = bf16[64,2560]{1,0:T(8,128)(2,1)S(1)} collective-permute-done((bf16[64,2560]{1,0:T(8,128)(2,1)}, bf16[64,2560]{1,0:T(8,128)(2,1)S(1)}, u32[]{:S(2)}, u32[]{:S(2)}) %collective-permute-start) | collective-permute-done | bytes 327712 | tf_op jit(solution)/shard_map/ppermute | solution.py:850
  58.9 1.0 copy-done
  59.9 0.6 share.1
  60.5 1.7 %collective-permute-start.1 = (bf16[64,640]{1,0:T(8,128)(2,1)S(1)}, bf16[64,640]{1,0:T(8,128)(2,1)S(1)}, u32[]{:S(2)}, u32[]{:S(2)}) collective-permute-start(bf16[64,640]{1,0:T(8,128)(2,1)S(1)} %get-tuple-element.85), channel_id=1, source_target_pairs={{0,2},{1,3},{2,0},{3,1},{4,6},{5,7},{6,4},{7,5},{8,10},{9,11},{10,... | collective-permute-start | bytes 245768 | tf_op jit(solution)/shard_map/ppermute | solution.py:852
  62.2 3.3 %collective-permute-start.2 = (bf16[64,640]{1,0:T(8,128)(2,1)S(1)}, bf16[64,640]{1,0:T(8,128)(2,1)S(1)}, u32[]{:S(2)}, u32[]{:S(2)}) collective-permute-start(bf16[64,640]{1,0:T(8,128)(2,1)S(1)} %get-tuple-element.86), channel_id=1, source_target_pairs={{0,4},{1,5},{2,6},{3,7},{4,0},{5,1},{6,2},{7,3},{8,12},{9,13},{10,... | collective-permute-start | bytes 245768 | tf_op jit(solution)/shard_map/ppermute | solution.py:852
  65.5 3.9 %collective-permute-done.2.rest_1_ = bf16[64,640]{1,0:T(8,128)(2,1)S(1)} collective-permute-done((bf16[64,640]{1,0:T(8,128)(2,1)S(1)}, bf16[64,640]{1,0:T(8,128)(2,1)S(1)}, u32[]{:S(2)}, u32[]{:S(2)}) %collective-permute-start.2) | collective-permute-done | bytes 81952 | tf_op jit(solution)/shard_map/ppermute | solution.py:852
  69.5 1.9 %collective-permute-done.3.rest_2_ = bf16[64,640]{1,0:T(8,128)(2,1)S(1)} collective-permute-done((bf16[64,640]{1,0:T(8,128)(2,1)S(1)}, bf16[64,640]{1,0:T(8,128)(2,1)S(1)}, u32[]{:S(2)}, u32[]{:S(2)}) %collective-permute-start.3) | collective-permute-done | bytes 81952 | tf_op jit(solution)/shard_map/ppermute | solution.py:852
  71.4 1.8 %pack_back.1 = bf16[16,72,128]{2,1,0:T(8,128)(2,1)} custom-call(s32[32]{0:T(128)S(1)} %copy-done.1, s32[40]{0:T(128)S(1)} %copy-done.2, bf16[16,480,128]{2,1,0:T(8,128)(2,1)S(1)} %all-to-all-done.2.direct, f32[64,640]{1,0:T(8,128)S(1)} %get-tuple-element.84.mine, bf16[64,640]{1,0:T(8,128)(2,1)S(1)} %collective-permute-done.1.rest_0_, ...), custom_call_target="tpu_custom_call" | custom-call | flops 1000 | bytes 1000 | tf_op jit(solution)/shard_map/pack_back/pallas_call | solution.py:730
  73.3 7.0 %all-to-all-start.3 = ((bf16[16,72,128]{2,1,0:T(8,128)(2,1)}), bf16[16,72,128]{2,1,0:T(8,128)(2,1)S(1)}, u32[]{:S(2)}, u32[]{:S(2)}) async-start(bf16[16,72,128]{2,1,0:T(8,128)(2,1)} %pack_back.1), calls=%async_computation.3 | async-start | bytes 589824 | tf_op jit(solution)/shard_map/all_to_all | solution.py:819
  80.2 3.8 %place_context.1.context = bf16[32,48,576]{2,1,0:T(8,128)(2,1)} custom-call(s32[40]{0:T(128)S(1)} %get-tuple-element.170.arrival, s32[40]{0:T(128)S(1)} %get-tuple-element.172.lengths, s32[2]{0:T(128)S(1)} %pad_add_fusion.where, bf16[16,480,128]{2,1,0:T(8,128)(2,1)S(1)} %all-to-all-done.2.direct), custom_call_target="tpu_custom_call" | custom-call | flops 1000 | bytes 12000000 | tf_op jit(solution)/shard_map/place_context/pallas_call | solution.py:368
  84.0 4.1 %all-to-all-done.3.back.packed = bf16[16,72,128]{2,1,0:T(8,128)(2,1)S(1)} async-done(((bf16[16,72,128]{2,1,0:T(8,128)(2,1)}), bf16[16,72,128]{2,1,0:T(8,128)(2,1)S(1)}, u32[]{:S(2)}, u32[]{:S(2)}) %all-to-all-start.3) | async-done | bytes 294944 | tf_op jit(solution)/shard_map/all_to_all | solution.py:819
  88.1 0.9 unpack_back.1.rest_0_
  88.9 0.8 collective-permute-start.6
  89.8 2.5 %collective-permute-start.4 = (bf16[64,640]{1,0:T(8,128)(2,1)S(1)}, bf16[64,640]{1,0:T(8,128)(2,1)S(1)}, u32[]{:S(2)}, u32[]{:S(2)}) collective-permute-start(bf16[64,640]{1,0:T(8,128)(2,1)S(1)} %unpack_back.1.rest_0_), channel_id=1, source_target_pairs={{0,2},{1,3},{2,0},{3,1},{4,6},{5,7},{6,4},{7,5},{8,10},{9,11},{10,... | collective-permute-start | bytes 245768 | tf_op jit(solution)/shard_map/ppermute | solution.py:858
  92.3 3.1 %collective-permute-start.7 = (bf16[64,640]{1,0:T(8,128)(2,1)S(1)}, bf16[64,640]{1,0:T(8,128)(2,1)S(1)}, u32[]{:S(2)}, u32[]{:S(2)}) collective-permute-start(bf16[64,640]{1,0:T(8,128)(2,1)S(1)} %unpack_back.1.rest_0_), channel_id=1, source_target_pairs={{0,1},{1,0},{2,3},{3,2},{4,5},{5,4},{6,7},{7,6},{8,9},{9,8},{10,11... | collective-permute-start | bytes 245768 | tf_op jit(solution)/shard_map/ppermute | solution.py:859
  95.4 2.0 %place_strips.1 = bf16[32,48,576]{2,1,0:T(8,128)(2,1)} custom-call(s32[40]{0:T(128)S(1)} %get-tuple-element.171.coming, s32[40]{0:T(128)S(1)} %get-tuple-element.172.lengths, s32[2]{0:T(128)S(1)} %pad_add_fusion.where, bf16[16,72,128]{2,1,0:T(8,128)(2,1)S(1)} %all-to-all-done.3.back.packed, ...), custom_call_target="tpu_custom_call", output_to_operand_aliasing={{}: (4, {})} | custom-call | flops 1000 | bytes 6000000 | tf_op jit(solution)/shard_map/place_strips/pallas_call | solution.py:426
  97.4 0.7 while.10
  100.1 1.8 %assemble.1 = bf16[32,4,2560]{2,1,0:T(4,128)(2,1)} custom-call(s32[2]{0:T(128)S(1)} %get-tuple-element.224, bf16[64,640]{1,0:T(8,128)(2,1)S(1)} %unpack_back.1.rest_0_, bf16[64,640]{1,0:T(8,128)(2,1)S(1)} %collective-permute-done.4.rest_1_, bf16[64,640]{1,0:T(8,128)(2,1)S(1)} %collective-permute-done.5.rest_2_, ...), custom_call_target="tpu_custom_call" | custom-call | flops 1000 | bytes 1000 | tf_op jit(solution)/shard_map/assemble/pallas_call | solution.py:803
  (21 shorter events, 2.1 us)
Async XLA Ops:
  5.5 24.7 %all-to-all-start.1 = ((bf16[16,264,128]{2,1,0:T(8,128)(2,1)}), bf16[16,264,128]{2,1,0:T(8,128)(2,1)}, u32[]{:S(2)}, u32[]{:S(2)}) async-start(bf16[16,264,128]{2,1,0:T(8,128)(2,1)} %get-tuple-element.78), calls=%async_computation.1 | async-start | bytes 2162688 | tf_op jit(solution)/shard_map/all_to_all | solution.py:819
  30.2 41.2 %all-to-all-start.2 = ((bf16[16,480,128]{2,1,0:T(8,128)(2,1)}), bf16[16,480,128]{2,1,0:T(8,128)(2,1)S(1)}, u32[]{:S(2)}, u32[]{:S(2)}) async-start(bf16[16,480,128]{2,1,0:T(8,128)(2,1)} %get-tuple-element.80), calls=%async_computation.2 | async-start | bytes 3932160 | tf_op jit(solution)/shard_map/all_to_all | solution.py:819
  36.8 34.6 %copy-start.1 = (s32[32]{0:T(128)S(1)}, s32[32]{0:T(128)}, u32[]{:S(2)}) copy-start(s32[32]{0:T(128)} %get-tuple-element.76.placing) | copy-start | bytes 388
  36.8 34.6 %copy-start.2 = (s32[40]{0:T(128)S(1)}, s32[40]{0:T(128)}, u32[]{:S(2)}) copy-start(s32[40]{0:T(128)} %get-tuple-element.77.relay) | copy-start | bytes 484
  55.8 3.1 %collective-permute-start = (bf16[64,2560]{1,0:T(8,128)(2,1)}, bf16[64,2560]{1,0:T(8,128)(2,1)S(1)}, u32[]{:S(2)}, u32[]{:S(2)}) collective-permute-start(bf16[64,2560]{1,0:T(8,128)(2,1)} %get-tuple-element.83), channel_id=1, source_target_pairs={{0,1},{1,0},{2,3},{3,2},{4,5},{5,4},{6,7},{7,6},{8,9},{9,8},{10,11... | collective-permute-start | bytes 983048 | tf_op jit(solution)/shard_map/ppermute | solution.py:850
  58.9 1.0 copy-start
  60.5 5.0 %collective-permute-start.1 = (bf16[64,640]{1,0:T(8,128)(2,1)S(1)}, bf16[64,640]{1,0:T(8,128)(2,1)S(1)}, u32[]{:S(2)}, u32[]{:S(2)}) collective-permute-start(bf16[64,640]{1,0:T(8,128)(2,1)S(1)} %get-tuple-element.85), channel_id=1, source_target_pairs={{0,2},{1,3},{2,0},{3,1},{4,6},{5,7},{6,4},{7,5},{8,10},{9,11},{10,... | collective-permute-start | bytes 245768 | tf_op jit(solution)/shard_map/ppermute | solution.py:852
  62.2 7.3 %collective-permute-start.2 = (bf16[64,640]{1,0:T(8,128)(2,1)S(1)}, bf16[64,640]{1,0:T(8,128)(2,1)S(1)}, u32[]{:S(2)}, u32[]{:S(2)}) collective-permute-start(bf16[64,640]{1,0:T(8,128)(2,1)S(1)} %get-tuple-element.86), channel_id=1, source_target_pairs={{0,4},{1,5},{2,6},{3,7},{4,0},{5,1},{6,2},{7,3},{8,12},{9,13},{10,... | collective-permute-start | bytes 245768 | tf_op jit(solution)/shard_map/ppermute | solution.py:852
  65.5 5.9 %collective-permute-start.3 = (bf16[64,640]{1,0:T(8,128)(2,1)S(1)}, bf16[64,640]{1,0:T(8,128)(2,1)S(1)}, u32[]{:S(2)}, u32[]{:S(2)}) collective-permute-start(bf16[64,640]{1,0:T(8,128)(2,1)S(1)} %get-tuple-element.87), channel_id=1, source_target_pairs={{0,6},{1,7},{2,4},{3,5},{4,2},{5,3},{6,0},{7,1},{8,14},{9,15},{10,... | collective-permute-start | bytes 245768 | tf_op jit(solution)/shard_map/ppermute | solution.py:852
  73.3 14.8 %all-to-all-start.3 = ((bf16[16,72,128]{2,1,0:T(8,128)(2,1)}), bf16[16,72,128]{2,1,0:T(8,128)(2,1)S(1)}, u32[]{:S(2)}, u32[]{:S(2)}) async-start(bf16[16,72,128]{2,1,0:T(8,128)(2,1)} %pack_back.1), calls=%async_computation.3 | async-start | bytes 589824 | tf_op jit(solution)/shard_map/all_to_all | solution.py:819
  88.9 9.1 %collective-permute-start.6 = (bf16[64,640]{1,0:T(8,128)(2,1)S(1)}, bf16[64,640]{1,0:T(8,128)(2,1)S(1)}, u32[]{:S(2)}, u32[]{:S(2)}) collective-permute-start(bf16[64,640]{1,0:T(8,128)(2,1)S(1)} %unpack_back.1.rest_0_), channel_id=1, source_target_pairs={{0,6},{1,7},{2,4},{3,5},{4,2},{5,3},{6,0},{7,1},{8,14},{9,15},{10,... | collective-permute-start | bytes 245768 | tf_op jit(solution)/shard_map/ppermute | solution.py:858
  89.8 8.3 %collective-permute-start.5 = (bf16[64,640]{1,0:T(8,128)(2,1)S(1)}, bf16[64,640]{1,0:T(8,128)(2,1)S(1)}, u32[]{:S(2)}, u32[]{:S(2)}) collective-permute-start(bf16[64,640]{1,0:T(8,128)(2,1)S(1)} %unpack_back.1.rest_0_), channel_id=1, source_target_pairs={{0,4},{1,5},{2,6},{3,7},{4,0},{5,1},{6,2},{7,3},{8,12},{9,13},{10,... | collective-permute-start | bytes 245768 | tf_op jit(solution)/shard_map/ppermute | solution.py:858
  89.8 8.3 %collective-permute-start.4 = (bf16[64,640]{1,0:T(8,128)(2,1)S(1)}, bf16[64,640]{1,0:T(8,128)(2,1)S(1)}, u32[]{:S(2)}, u32[]{:S(2)}) collective-permute-start(bf16[64,640]{1,0:T(8,128)(2,1)S(1)} %unpack_back.1.rest_0_), channel_id=1, source_target_pairs={{0,2},{1,3},{2,0},{3,1},{4,6},{5,7},{6,4},{7,5},{8,10},{9,11},{10,... | collective-permute-start | bytes 245768 | tf_op jit(solution)/shard_map/ppermute | solution.py:858
  92.3 6.9 %collective-permute-start.7 = (bf16[64,640]{1,0:T(8,128)(2,1)S(1)}, bf16[64,640]{1,0:T(8,128)(2,1)S(1)}, u32[]{:S(2)}, u32[]{:S(2)}) collective-permute-start(bf16[64,640]{1,0:T(8,128)(2,1)S(1)} %unpack_back.1.rest_0_), channel_id=1, source_target_pairs={{0,1},{1,0},{2,3},{3,2},{4,5},{5,4},{6,7},{7,6},{8,9},{9,8},{10,11... | collective-permute-start | bytes 245768 | tf_op jit(solution)/shard_map/ppermute | solution.py:859
  98.1 1.5 %collective-permute-start.8 = (bf16[64,640]{1,0:T(8,128)(2,1)S(1)}, bf16[64,640]{1,0:T(8,128)(2,1)S(1)}, u32[]{:S(2)}, u32[]{:S(2)}) collective-permute-start(bf16[64,640]{1,0:T(8,128)(2,1)S(1)} %collective-permute-done.4.rest_1_), channel_id=1, source_target_pairs={{0,1},{1,0},{2,3},{3,2},{4,5},{5,4},{6,7},{7,6},{8,9},{9,8},{10,11... | collective-permute-start | bytes 245768 | tf_op jit(solution)/shard_map/ppermute | solution.py:873
  98.7 1.3 %collective-permute-start.9 = (bf16[64,640]{1,0:T(8,128)(2,1)S(1)}, bf16[64,640]{1,0:T(8,128)(2,1)S(1)}, u32[]{:S(2)}, u32[]{:S(2)}) collective-permute-start(bf16[64,640]{1,0:T(8,128)(2,1)S(1)} %collective-permute-done.5.rest_2_), channel_id=1, source_target_pairs={{0,1},{1,0},{2,3},{3,2},{4,5},{5,4},{6,7},{7,6},{8,9},{9,8},{10,11... | collective-permute-start | bytes 245768 | tf_op jit(solution)/shard_map/ppermute | solution.py:873
  98.7 1.4 %collective-permute-start.10 = (bf16[64,640]{1,0:T(8,128)(2,1)S(1)}, bf16[64,640]{1,0:T(8,128)(2,1)S(1)}, u32[]{:S(2)}, u32[]{:S(2)}) collective-permute-start(bf16[64,640]{1,0:T(8,128)(2,1)S(1)} %collective-permute-done.6.rest_3_), channel_id=1, source_target_pairs={{0,1},{1,0},{2,3},{3,2},{4,5},{5,4},{6,7},{7,6},{8,9},{9,8},{10,11... | collective-permute-start | bytes 245768 | tf_op jit(solution)/shard_map/ppermute | solution.py:873

commit v9 on v8

--- a/solution.py
+++ b/solution.py
@@ -14,7 +14,7 @@
 DIRECT = 2
 SPILL = 2
 STRIP = 16
-GROUP = 8
+GROUP = 16
 FLOOR = -1e30
 BF16 = jnp.bfloat16
 F32 = jnp.float32
@@ -39,8 +39,8 @@
 
 
 def pack_queries_kernel(
-    decode_slot, prompt_lengths, where, q_hbm, n_hbm,
-    out_ref, arrival, lengths,
+    decode_slot, where, q_hbm, n_hbm,
+    out_ref, arrival,
     q_ref, n_ref, new_rows, tails, sems,
 ):
     steps, slots, heads, width = q_ref.shape
@@ -59,7 +59,6 @@
             hit = (inner >= 0) & (inner < slots)
             at = jnp.where(hit, inner, slots)
             arrival[at] = p * CAP + rank
-            lengths[at] = prompt_lengths[p * slots + k]
             rank = rank + hit.astype(jnp.int32)
         return carry
 
@@ -89,17 +88,16 @@
     out_ref[:, 256:264, :] = tails[...].reshape(out_ref.shape[0], 8, 128).astype(BF16)
 
 
-def pack_queries(decode_slot, prompt_lengths, where, queries, new_latent, pool_count):
+def pack_queries(decode_slot, where, queries, new_latent, pool_count):
     slots = queries.shape[1]
     return pl.pallas_call(
         pack_queries_kernel,
         out_shape=(
             jax.ShapeDtypeStruct((pool_count, 264, 128), BF16),
             jax.ShapeDtypeStruct((slots + 8,), jnp.int32),
-            jax.ShapeDtypeStruct((slots + 8,), jnp.int32),
         ),
-        in_specs=[SMEM_SPEC] * 3 + [ANY_SPEC] * 2,
-        out_specs=(VMEM_SPEC, SMEM_SPEC, SMEM_SPEC),
+        in_specs=[SMEM_SPEC] * 2 + [ANY_SPEC] * 2,
+        out_specs=(VMEM_SPEC, SMEM_SPEC),
         scratch_shapes=[
             pltpu.VMEM(queries.shape, BF16),
             pltpu.VMEM(new_latent.shape, BF16),
@@ -110,7 +108,7 @@
         compiler_params=params(60),
         cost_estimate=cost(),
         name="pack_queries",
-    )(decode_slot, prompt_lengths, where, queries, new_latent)
+    )(decode_slot, where, queries, new_latent)
 
 
 def padded_rows(piece, feature):
@@ -255,7 +253,7 @@
 
             return carry
 
-        lax.fori_loop(0, chunk, one, 0, unroll=4)
+        lax.fori_loop(0, chunk, one, 0, unroll=8)
 
 
 def pack_context(decode_slot, where, prompt_latent, piece, pool_count):
@@ -271,7 +269,7 @@
             jax.ShapeDtypeStruct((pool_count * SPILL + 8,), jnp.int32),
             jax.ShapeDtypeStruct((1,), jnp.int32),
         ),
-        in_specs=[SMEM_SPEC, SMEM_SPEC, ANY_SPEC],
+        in_specs=[SMEM_SPEC] * 2 + [ANY_SPEC],
         out_specs=(VMEM_SPEC,) + (SMEM_SPEC,) * 5,
         scratch_shapes=[
             pltpu.SMEM((slots,), jnp.int32),
@@ -341,8 +339,20 @@
         out_ref[row] = jnp.where(position < length, whole, 0.0).astype(BF16)
 
 
-def place_kernel(arrival, lengths, where, direct, out_ref, outbox, sems):
+def place_kernel(
+    decode_slot, prompt_lengths, arrival, where, direct, out_ref, lengths, outbox, sems
+):
     slots, piece, feature = out_ref.shape
+    first = where[1] * slots
+
+    def measure(p, carry):
+        for k in range(slots):
+            inner = decode_slot[p * slots + k] - first
+            at = jnp.where((inner >= 0) & (inner < slots), inner, slots)
+            lengths[at] = prompt_lengths[p * slots + k]
+        return carry
+
+    lax.fori_loop(0, direct.shape[0], measure, 0)
     padded = (direct.shape[1] - SPILL * STRIP) // DIRECT
     chunk = slots // sems.shape[0]
 
@@ -363,13 +373,16 @@
         copy_out(k).wait()
 
 
-def place(arrival, lengths, where, direct, piece, feature):
+def place(decode_slot, prompt_lengths, arrival, where, direct, piece, feature):
     slots = arrival.shape[0] - 8
     return pl.pallas_call(
         place_kernel,
-        out_shape=jax.ShapeDtypeStruct((slots, piece, feature), BF16),
-        in_specs=[SMEM_SPEC] * 3 + [VMEM_SPEC],
-        out_specs=ANY_SPEC,
+        out_shape=(
+            jax.ShapeDtypeStruct((slots, piece, feature), BF16),
+            jax.ShapeDtypeStruct((slots + 8,), jnp.int32),
+        ),
+        in_specs=[SMEM_SPEC] * 4 + [VMEM_SPEC],
+        out_specs=(ANY_SPEC, SMEM_SPEC),
         scratch_shapes=[
             pltpu.VMEM((slots, piece, feature), BF16),
             pltpu.SemaphoreType.DMA((4,)),
@@ -377,7 +390,7 @@
         compiler_params=params(),
         cost_estimate=cost(bytes_accessed=12_000_000),
         name="place_context",
-    )(arrival, lengths, where, direct)
+    )(decode_slot, prompt_lengths, arrival, where, direct)
 
 
 def place_strips_kernel(
@@ -833,9 +846,7 @@
     swap = [(i, i ^ 1) for i in range(tp_count)]
     hops = [[(i, i ^ (2 * d)) for i in range(tp_count)] for d in range(1, z_count)]
 
-    payload, arrival, lengths = pack_queries(
-        decode_slot, prompt_lengths, where, queries, new_latent, pool_count
-    )
+    payload, arrival = pack_queries(decode_slot, where, queries, new_latent, pool_count)
     payload = exchange(payload)
     direct, placing, leaving, coming, relay, rounds = pack_context(
         decode_slot, where, latent_t, piece, pool_count
@@ -852,7 +863,9 @@
     parts = [lax.ppermute(part, "tp", hop) for part, hop in zip(parts, hops)]
 
     back = exchange(pack_back(placing, relay, direct, mine, parts))
-    context = place(arrival, lengths, where, direct, piece, feature)
+    context, lengths = place(
+        decode_slot, prompt_lengths, arrival, where, direct, piece, feature
+    )
     back, context = lax.optimization_barrier((back, context))
     own = unpack_back(arrival, back, steps // 2, slots, out_width // z_count)
     parts = [own] + [lax.ppermute(own, "tp", hop) for hop in hops]

time: 102 us -> 102 us (level)
  waiting for transfers between devices: 12.4 us -> 10.3 us
  Pallas kernels: 51.6 us -> 52.9 us
    all_to_all x3, waiting for transfers between devices: 4.1 us -> 2.03 us  [exchange(): return lax.all_to_all(x, 'pool', split_axis=0, concat_axis=0, tiled=True)]
    pallas_call x1, Pallas kernels: 3.76 us -> 5.8 us  [place(): pl.pallas_call(place_kernel, out_shape=(jax.ShapeDtypeStruct((slots, piec...]
  transfers between devices with their start and end apart: 14 -> 14, of which waited for: 7 -> 7; matrix products, arithmetic and copies ran while one was open for 0% -> 0% of each run, Pallas kernels for 42% -> 43%
where the time goes in v9:
time: 102 us; the launch traced here: 101 us
  Pallas kernels  52.9 us (52%)
  starting transfers between devices  35.7 us (35%)
  waiting for transfers between devices  10.3 us (10%)
    all_to_all x3, starting transfers between devices, exchange(): return lax.all_to_all(x, 'pool', split_axis=0, concat_axis=0, tiled=True)  21.2 us
    pallas_call x1, Pallas kernels, attention(): pl.pallas_call(attention_kernel, out_shape=(jax.ShapeDtypeStruct((half, w...  18.9 us
    pallas_call x1, Pallas kernels, pack_context(): pl.pallas_call(pack_context_kernel, out_shape=(jax.ShapeDtypeStruct((pool...  17.1 us
    ppermute x3, waiting for transfers between devices, body(): parts = [lax.ppermute(part, 'tp', hop) for part, hop in zip(parts, hops)]  5.88 us
    pallas_call x1, Pallas kernels, place(): pl.pallas_call(place_kernel, out_shape=(jax.ShapeDtypeStruct((slots, piec...  5.8 us
    ppermute x3, starting transfers between devices, body(): parts = [lax.ppermute(part, 'tp', hop) for part, hop in zip(parts, hops)]  5.02 us
    pallas_call x1, Pallas kernels, pack_queries(): pl.pallas_call(pack_queries_kernel, out_shape=(jax.ShapeDtypeStruct((pool...  4.31 us
    ppermute x3, starting transfers between devices, body(): parts = [own] + [lax.ppermute(own, 'tp', hop) for hop in hops]  3.33 us
  transfers between devices with their start and end apart: 14, of which 7 were waited for; matrix products, arithmetic and copies ran while one was open for 0% of the time, Pallas kernels for 43%

profile of v9, /device:TPU:1, one launch (start us, length us, event | category | flops | bytes accessed | tf_op | source)
XLA Modules:
  0.0 101.4 jit_solution(399401594943417028)
XLA Ops:
  0.7 4.3 %pack_queries.1 = (bf16[16,264,128]{2,1,0:T(8,128)(2,1)}, s32[40]{0:T(128)S(1)}) custom-call(s32[512]{0:T(512)} %decode_slot.5, s32[2]{0:T(128)S(1)} %pad_add_fusion.where, bf16[4,32,8,192]{3,2,1,0:T(8,128)(2,1)} %q_hbm.1, bf16[4,32,576]{2,1,0:T(8,128)(2,1)} %n_hbm.1), custom_call_target="tpu_custom_call" | custom-call | flops 1000 | bytes 1000 | tf_op jit(solution)/shard_map/pack_queries/pallas_call | solution.py:93
  5.0 7.6 %all-to-all-start.1 = ((bf16[16,264,128]{2,1,0:T(8,128)(2,1)}), bf16[16,264,128]{2,1,0:T(8,128)(2,1)}, u32[]{:S(2)}, u32[]{:S(2)}) async-start(bf16[16,264,128]{2,1,0:T(8,128)(2,1)} %get-tuple-element.77), calls=%async_computation.1 | async-start | bytes 2162688 | tf_op jit(solution)/shard_map/all_to_all | solution.py:832
  12.7 17.1 %pack_context.1 = (bf16[16,480,128]{2,1,0:T(8,128)(2,1)}, s32[32]{0:T(128)}, s32[32]{0:T(128)S(1)}, s32[40]{0:T(128)S(1)}, s32[40]{0:T(128)}, /*index=5*/s32[1]{0:T(128)}) custom-call(s32[512]{0:T(512)} %decode_slot.5, s32[2]{0:T(128)S(1)} %pad_add_fusion.where, bf16[32,576,384]{2,1,0:T(8,128)(2,1)} %bitcast.5), custom_call_target="tpu_custom_call" | custom-call | flops 1000 | bytes 1000 | tf_op jit(solution)/shard_map/pack_context/pallas_call | solution.py:262
  29.7 6.6 %all-to-all-start.2 = ((bf16[16,480,128]{2,1,0:T(8,128)(2,1)}), bf16[16,480,128]{2,1,0:T(8,128)(2,1)S(1)}, u32[]{:S(2)}, u32[]{:S(2)}) async-start(bf16[16,480,128]{2,1,0:T(8,128)(2,1)} %get-tuple-element.79), calls=%async_computation.2 | async-start | bytes 3932160 | tf_op jit(solution)/shard_map/all_to_all | solution.py:832
  36.4 18.9 %attention.1 = (bf16[64,2560]{1,0:T(8,128)(2,1)}, bf16[64,2560]{1,0:T(8,128)(2,1)}) custom-call(s32[32]{0:T(128)} %get-tuple-element.81.placing, s32[512]{0:T(512)} %lengths.1, s32[2]{0:T(128)S(1)} %pad_add_fusion.where, bf16[16,264,128]{2,1,0:T(8,128)(2,1)} %all-to-all-done.1.payload_hbm, bf16[32,576,384]{2,1,0:T(8,128)(2,1)} %bitcast.6, ...), custom_call_target="tpu_custom_call" | custom-call | flops 1000 | bytes 1000 | tf_op jit(solution)/shard_map/attention/pallas_call | solution.py:651
  55.3 1.6 %collective-permute-start = (bf16[64,2560]{1,0:T(8,128)(2,1)}, bf16[64,2560]{1,0:T(8,128)(2,1)S(1)}, u32[]{:S(2)}, u32[]{:S(2)}) collective-permute-start(bf16[64,2560]{1,0:T(8,128)(2,1)} %get-tuple-element.85), channel_id=1, source_target_pairs={{0,1},{1,0},{2,3},{3,2},{4,5},{5,4},{6,7},{7,6},{8,9},{9,8},{10,11... | collective-permute-start | bytes 983048 | tf_op jit(solution)/shard_map/ppermute | solution.py:861
  56.9 1.5 %collective-permute-done.swapped = bf16[64,2560]{1,0:T(8,128)(2,1)S(1)} collective-permute-done((bf16[64,2560]{1,0:T(8,128)(2,1)}, bf16[64,2560]{1,0:T(8,128)(2,1)S(1)}, u32[]{:S(2)}, u32[]{:S(2)}) %collective-permute-start) | collective-permute-done | bytes 327712 | tf_op jit(solution)/shard_map/ppermute | solution.py:861
  58.3 1.0 copy-done
  59.3 0.6 share.1
  59.9 1.7 %collective-permute-start.1 = (bf16[64,640]{1,0:T(8,128)(2,1)S(1)}, bf16[64,640]{1,0:T(8,128)(2,1)S(1)}, u32[]{:S(2)}, u32[]{:S(2)}) collective-permute-start(bf16[64,640]{1,0:T(8,128)(2,1)S(1)} %get-tuple-element.87), channel_id=1, source_target_pairs={{0,2},{1,3},{2,0},{3,1},{4,6},{5,7},{6,4},{7,5},{8,10},{9,11},{10,... | collective-permute-start | bytes 245768 | tf_op jit(solution)/shard_map/ppermute | solution.py:863
  61.7 3.3 %collective-permute-start.2 = (bf16[64,640]{1,0:T(8,128)(2,1)S(1)}, bf16[64,640]{1,0:T(8,128)(2,1)S(1)}, u32[]{:S(2)}, u32[]{:S(2)}) collective-permute-start(bf16[64,640]{1,0:T(8,128)(2,1)S(1)} %get-tuple-element.88), channel_id=1, source_target_pairs={{0,4},{1,5},{2,6},{3,7},{4,0},{5,1},{6,2},{7,3},{8,12},{9,13},{10,... | collective-permute-start | bytes 245768 | tf_op jit(solution)/shard_map/ppermute | solution.py:863
  65.0 3.9 %collective-permute-done.2.rest_1_ = bf16[64,640]{1,0:T(8,128)(2,1)S(1)} collective-permute-done((bf16[64,640]{1,0:T(8,128)(2,1)S(1)}, bf16[64,640]{1,0:T(8,128)(2,1)S(1)}, u32[]{:S(2)}, u32[]{:S(2)}) %collective-permute-start.2) | collective-permute-done | bytes 81952 | tf_op jit(solution)/shard_map/ppermute | solution.py:863
  68.9 1.9 %collective-permute-done.3.rest_2_ = bf16[64,640]{1,0:T(8,128)(2,1)S(1)} collective-permute-done((bf16[64,640]{1,0:T(8,128)(2,1)S(1)}, bf16[64,640]{1,0:T(8,128)(2,1)S(1)}, u32[]{:S(2)}, u32[]{:S(2)}) %collective-permute-start.3) | collective-permute-done | bytes 81952 | tf_op jit(solution)/shard_map/ppermute | solution.py:863
  70.9 1.8 %pack_back.1 = bf16[16,72,128]{2,1,0:T(8,128)(2,1)} custom-call(s32[32]{0:T(128)S(1)} %copy-done.3, s32[40]{0:T(128)S(1)} %copy-done.4, bf16[16,480,128]{2,1,0:T(8,128)(2,1)S(1)} %all-to-all-done.2.direct, f32[64,640]{1,0:T(8,128)S(1)} %get-tuple-element.86.mine, bf16[64,640]{1,0:T(8,128)(2,1)S(1)} %collective-permute-done.1.rest_0_, ...), custom_call_target="tpu_custom_call" | custom-call | flops 1000 | bytes 1000 | tf_op jit(solution)/shard_map/pack_back/pallas_call | solution.py:743
  72.7 7.0 %all-to-all-start.3 = ((bf16[16,72,128]{2,1,0:T(8,128)(2,1)}), bf16[16,72,128]{2,1,0:T(8,128)(2,1)S(1)}, u32[]{:S(2)}, u32[]{:S(2)}) async-start(bf16[16,72,128]{2,1,0:T(8,128)(2,1)} %pack_back.1), calls=%async_computation.3 | async-start | bytes 589824 | tf_op jit(solution)/shard_map/all_to_all | solution.py:832
  79.7 5.8 %place_context.1 = (bf16[32,48,576]{2,1,0:T(8,128)(2,1)}, s32[40]{0:T(128)S(1)}) custom-call(s32[512]{0:T(512)S(1)} %copy-done.1, s32[512]{0:T(512)S(1)} %copy-done.2, s32[40]{0:T(128)S(1)} %get-tuple-element.172.arrival, s32[2]{0:T(128)S(1)} %pad_add_fusion.where, bf16[16,480,128]{2,1,0:T(8,128)(2,1)S(1)} %all-to-all-done.2.direct), custom_call_target="tpu_custom_call" | custom-call | flops 1000 | bytes 12000000 | tf_op jit(solution)/shard_map/place_context/pallas_call | solution.py:378
  85.5 2.0 %all-to-all-done.3.back.packed = bf16[16,72,128]{2,1,0:T(8,128)(2,1)S(1)} async-done(((bf16[16,72,128]{2,1,0:T(8,128)(2,1)}), bf16[16,72,128]{2,1,0:T(8,128)(2,1)S(1)}, u32[]{:S(2)}, u32[]{:S(2)}) %all-to-all-start.3) | async-done | bytes 294944 | tf_op jit(solution)/shard_map/all_to_all | solution.py:832
  87.5 0.9 unpack_back.1.rest_0_
  88.4 0.8 collective-permute-start.6
  89.2 2.5 %collective-permute-start.4 = (bf16[64,640]{1,0:T(8,128)(2,1)S(1)}, bf16[64,640]{1,0:T(8,128)(2,1)S(1)}, u32[]{:S(2)}, u32[]{:S(2)}) collective-permute-start(bf16[64,640]{1,0:T(8,128)(2,1)S(1)} %unpack_back.1.rest_0_), channel_id=1, source_target_pairs={{0,2},{1,3},{2,0},{3,1},{4,6},{5,7},{6,4},{7,5},{8,10},{9,11},{10,... | collective-permute-start | bytes 245768 | tf_op jit(solution)/shard_map/ppermute | solution.py:871
  91.7 3.1 %collective-permute-start.7 = (bf16[64,640]{1,0:T(8,128)(2,1)S(1)}, bf16[64,640]{1,0:T(8,128)(2,1)S(1)}, u32[]{:S(2)}, u32[]{:S(2)}) collective-permute-start(bf16[64,640]{1,0:T(8,128)(2,1)S(1)} %unpack_back.1.rest_0_), channel_id=1, source_target_pairs={{0,1},{1,0},{2,3},{3,2},{4,5},{5,4},{6,7},{7,6},{8,9},{9,8},{10,11... | collective-permute-start | bytes 245768 | tf_op jit(solution)/shard_map/ppermute | solution.py:872
  94.9 1.8 %place_strips.1 = bf16[32,48,576]{2,1,0:T(8,128)(2,1)} custom-call(s32[40]{0:T(128)S(1)} %get-tuple-element.173.coming, s32[40]{0:T(128)S(1)} %get-tuple-element.174.lengths, s32[2]{0:T(128)S(1)} %pad_add_fusion.where, bf16[16,72,128]{2,1,0:T(8,128)(2,1)S(1)} %all-to-all-done.3.back.packed, ...), custom_call_target="tpu_custom_call", output_to_operand_aliasing={{}: (4, {})} | custom-call | flops 1000 | bytes 6000000 | tf_op jit(solution)/shard_map/place_strips/pallas_call | solution.py:439
  97.2 0.9 collective-permute-start.8
  99.6 1.8 %assemble.1 = bf16[32,4,2560]{2,1,0:T(4,128)(2,1)} custom-call(s32[2]{0:T(128)S(1)} %get-tuple-element.226, bf16[64,640]{1,0:T(8,128)(2,1)S(1)} %unpack_back.1.rest_0_, bf16[64,640]{1,0:T(8,128)(2,1)S(1)} %collective-permute-done.4.rest_1_, bf16[64,640]{1,0:T(8,128)(2,1)S(1)} %collective-permute-done.5.rest_2_, ...), custom_call_target="tpu_custom_call" | custom-call | flops 1000 | bytes 1000 | tf_op jit(solution)/shard_map/assemble/pallas_call | solution.py:816
  (25 shorter events, 2.1 us)
Async XLA Ops:
  5.0 24.7 %all-to-all-start.1 = ((bf16[16,264,128]{2,1,0:T(8,128)(2,1)}), bf16[16,264,128]{2,1,0:T(8,128)(2,1)}, u32[]{:S(2)}, u32[]{:S(2)}) async-start(bf16[16,264,128]{2,1,0:T(8,128)(2,1)} %get-tuple-element.77), calls=%async_computation.1 | async-start | bytes 2162688 | tf_op jit(solution)/shard_map/all_to_all | solution.py:832
  29.7 41.1 %all-to-all-start.2 = ((bf16[16,480,128]{2,1,0:T(8,128)(2,1)}), bf16[16,480,128]{2,1,0:T(8,128)(2,1)S(1)}, u32[]{:S(2)}, u32[]{:S(2)}) async-start(bf16[16,480,128]{2,1,0:T(8,128)(2,1)} %get-tuple-element.79), calls=%async_computation.2 | async-start | bytes 3932160 | tf_op jit(solution)/shard_map/all_to_all | solution.py:832
  36.4 34.5 %copy-start.3 = (s32[32]{0:T(128)S(1)}, s32[32]{0:T(128)}, u32[]{:S(2)}) copy-start(s32[32]{0:T(128)} %get-tuple-element.81.placing) | copy-start | bytes 388
  36.4 34.5 %copy-start.4 = (s32[40]{0:T(128)S(1)}, s32[40]{0:T(128)}, u32[]{:S(2)}) copy-start(s32[40]{0:T(128)} %get-tuple-element.82.relay) | copy-start | bytes 484
  36.4 43.3 %copy-start.2 = (s32[512]{0:T(512)S(1)}, s32[512]{0:T(512)}, u32[]{:S(2)}) copy-start(s32[512]{0:T(512)} %lengths.1) | copy-start | bytes 6148
  55.3 24.4 %copy-start.1 = (s32[512]{0:T(512)S(1)}, s32[512]{0:T(512)}, u32[]{:S(2)}) copy-start(s32[512]{0:T(512)} %decode_slot.5) | copy-start | bytes 6148
  55.3 3.1 %collective-permute-start = (bf16[64,2560]{1,0:T(8,128)(2,1)}, bf16[64,2560]{1,0:T(8,128)(2,1)S(1)}, u32[]{:S(2)}, u32[]{:S(2)}) collective-permute-start(bf16[64,2560]{1,0:T(8,128)(2,1)} %get-tuple-element.85), channel_id=1, source_target_pairs={{0,1},{1,0},{2,3},{3,2},{4,5},{5,4},{6,7},{7,6},{8,9},{9,8},{10,11... | collective-permute-start | bytes 983048 | tf_op jit(solution)/shard_map/ppermute | solution.py:861
  58.3 1.0 copy-start
  59.9 5.0 %collective-permute-start.1 = (bf16[64,640]{1,0:T(8,128)(2,1)S(1)}, bf16[64,640]{1,0:T(8,128)(2,1)S(1)}, u32[]{:S(2)}, u32[]{:S(2)}) collective-permute-start(bf16[64,640]{1,0:T(8,128)(2,1)S(1)} %get-tuple-element.87), channel_id=1, source_target_pairs={{0,2},{1,3},{2,0},{3,1},{4,6},{5,7},{6,4},{7,5},{8,10},{9,11},{10,... | collective-permute-start | bytes 245768 | tf_op jit(solution)/shard_map/ppermute | solution.py:863
  61.7 7.3 %collective-permute-start.2 = (bf16[64,640]{1,0:T(8,128)(2,1)S(1)}, bf16[64,640]{1,0:T(8,128)(2,1)S(1)}, u32[]{:S(2)}, u32[]{:S(2)}) collective-permute-start(bf16[64,640]{1,0:T(8,128)(2,1)S(1)} %get-tuple-element.88), channel_id=1, source_target_pairs={{0,4},{1,5},{2,6},{3,7},{4,0},{5,1},{6,2},{7,3},{8,12},{9,13},{10,... | collective-permute-start | bytes 245768 | tf_op jit(solution)/shard_map/ppermute | solution.py:863
  65.0 5.9 %collective-permute-start.3 = (bf16[64,640]{1,0:T(8,128)(2,1)S(1)}, bf16[64,640]{1,0:T(8,128)(2,1)S(1)}, u32[]{:S(2)}, u32[]{:S(2)}) collective-permute-start(bf16[64,640]{1,0:T(8,128)(2,1)S(1)} %get-tuple-element.89), channel_id=1, source_target_pairs={{0,6},{1,7},{2,4},{3,5},{4,2},{5,3},{6,0},{7,1},{8,14},{9,15},{10,... | collective-permute-start | bytes 245768 | tf_op jit(solution)/shard_map/ppermute | solution.py:863
  72.7 14.8 %all-to-all-start.3 = ((bf16[16,72,128]{2,1,0:T(8,128)(2,1)}), bf16[16,72,128]{2,1,0:T(8,128)(2,1)S(1)}, u32[]{:S(2)}, u32[]{:S(2)}) async-start(bf16[16,72,128]{2,1,0:T(8,128)(2,1)} %pack_back.1), calls=%async_computation.3 | async-start | bytes 589824 | tf_op jit(solution)/shard_map/all_to_all | solution.py:832
  88.4 8.8 %collective-permute-start.6 = (bf16[64,640]{1,0:T(8,128)(2,1)S(1)}, bf16[64,640]{1,0:T(8,128)(2,1)S(1)}, u32[]{:S(2)}, u32[]{:S(2)}) collective-permute-start(bf16[64,640]{1,0:T(8,128)(2,1)S(1)} %unpack_back.1.rest_0_), channel_id=1, source_target_pairs={{0,6},{1,7},{2,4},{3,5},{4,2},{5,3},{6,0},{7,1},{8,14},{9,15},{10,... | collective-permute-start | bytes 245768 | tf_op jit(solution)/shard_map/ppermute | solution.py:871
  89.2 8.0 %collective-permute-start.5 = (bf16[64,640]{1,0:T(8,128)(2,1)S(1)}, bf16[64,640]{1,0:T(8,128)(2,1)S(1)}, u32[]{:S(2)}, u32[]{:S(2)}) collective-permute-start(bf16[64,640]{1,0:T(8,128)(2,1)S(1)} %unpack_back.1.rest_0_), channel_id=1, source_target_pairs={{0,4},{1,5},{2,6},{3,7},{4,0},{5,1},{6,2},{7,3},{8,12},{9,13},{10,... | collective-permute-start | bytes 245768 | tf_op jit(solution)/shard_map/ppermute | solution.py:871
  89.2 8.0 %collective-permute-start.4 = (bf16[64,640]{1,0:T(8,128)(2,1)S(1)}, bf16[64,640]{1,0:T(8,128)(2,1)S(1)}, u32[]{:S(2)}, u32[]{:S(2)}) collective-permute-start(bf16[64,640]{1,0:T(8,128)(2,1)S(1)} %unpack_back.1.rest_0_), channel_id=1, source_target_pairs={{0,2},{1,3},{2,0},{3,1},{4,6},{5,7},{6,4},{7,5},{8,10},{9,11},{10,... | collective-permute-start | bytes 245768 | tf_op jit(solution)/shard_map/ppermute | solution.py:871
  91.7 6.9 %collective-permute-start.7 = (bf16[64,640]{1,0:T(8,128)(2,1)S(1)}, bf16[64,640]{1,0:T(8,128)(2,1)S(1)}, u32[]{:S(2)}, u32[]{:S(2)}) collective-permute-start(bf16[64,640]{1,0:T(8,128)(2,1)S(1)} %unpack_back.1.rest_0_), channel_id=1, source_target_pairs={{0,1},{1,0},{2,3},{3,2},{4,5},{5,4},{6,7},{7,6},{8,9},{9,8},{10,11... | collective-permute-start | bytes 245768 | tf_op jit(solution)/shard_map/ppermute | solution.py:872
  97.2 1.8 %collective-permute-start.8 = (bf16[64,640]{1,0:T(8,128)(2,1)S(1)}, bf16[64,640]{1,0:T(8,128)(2,1)S(1)}, u32[]{:S(2)}, u32[]{:S(2)}) collective-permute-start(bf16[64,640]{1,0:T(8,128)(2,1)S(1)} %collective-permute-done.4.rest_1_), channel_id=1, source_target_pairs={{0,1},{1,0},{2,3},{3,2},{4,5},{5,4},{6,7},{7,6},{8,9},{9,8},{10,11... | collective-permute-start | bytes 245768 | tf_op jit(solution)/shard_map/ppermute | solution.py:886
  98.1 1.3 %collective-permute-start.9 = (bf16[64,640]{1,0:T(8,128)(2,1)S(1)}, bf16[64,640]{1,0:T(8,128)(2,1)S(1)}, u32[]{:S(2)}, u32[]{:S(2)}) collective-permute-start(bf16[64,640]{1,0:T(8,128)(2,1)S(1)} %collective-permute-done.5.rest_2_), channel_id=1, source_target_pairs={{0,1},{1,0},{2,3},{3,2},{4,5},{5,4},{6,7},{7,6},{8,9},{9,8},{10,11... | collective-permute-start | bytes 245768 | tf_op jit(solution)/shard_map/ppermute | solution.py:886
  98.2 1.4 %collective-permute-start.10 = (bf16[64,640]{1,0:T(8,128)(2,1)S(1)}, bf16[64,640]{1,0:T(8,128)(2,1)S(1)}, u32[]{:S(2)}, u32[]{:S(2)}) collective-permute-start(bf16[64,640]{1,0:T(8,128)(2,1)S(1)} %collective-permute-done.6.rest_3_), channel_id=1, source_target_pairs={{0,1},{1,0},{2,3},{3,2},{4,5},{5,4},{6,7},{7,6},{8,9},{9,8},{10,11... | collective-permute-start | bytes 245768 | tf_op jit(solution)/shard_map/ppermute | solution.py:886

commit v10 on v9

--- a/solution.py
+++ b/solution.py
@@ -84,7 +84,7 @@
         )
         return carry
 
-    lax.fori_loop(0, slots, one, 0, unroll=4)
+    lax.fori_loop(0, slots, one, 0, unroll=8)
     out_ref[:, 256:264, :] = tails[...].reshape(out_ref.shape[0], 8, 128).astype(BF16)
 
 
@@ -724,7 +724,7 @@
                 rows[pl.ds(at, 1), :] = total[b, pl.ds(slots * s + i, 1), :]
         return carry
 
-    lax.fori_loop(0, slots, one, 0, unroll=4)
+    lax.fori_loop(0, slots, one, 0, unroll=8)
     out_ref[:, hop:, :] = rows[...].reshape(out_ref.shape[0], 8 * blocks, 128).astype(BF16)
     fetch.wait()
     for q in range(out_ref.shape[0]):
@@ -770,7 +770,7 @@
             total[b, pl.ds(steps * j, steps), :] = rows[pl.ds(at, steps), :]
         return carry
 
-    lax.fori_loop(0, slots, one, 0, unroll=4)
+    lax.fori_loop(0, slots, one, 0, unroll=8)
     for b in range(blocks):
         out_ref[:, 128 * b : 128 * b + 128] = total[b].astype(BF16)
 

time: 102 us -> 102 us (level)
  transfers between devices with their start and end apart: 14 -> 14, of which waited for: 7 -> 7; matrix products, arithmetic and copies ran while one was open for 0% -> 0% of each run, Pallas kernels for 43% -> 44%
where the time goes in v10:
time: 102 us; the launch traced here: 101 us
  Pallas kernels  52.6 us (52%)
  starting transfers between devices  35.7 us (35%)
  waiting for transfers between devices  10.3 us (10%)
    all_to_all x3, starting transfers between devices, exchange(): return lax.all_to_all(x, 'pool', split_axis=0, concat_axis=0, tiled=True)  21.2 us
    pallas_call x1, Pallas kernels, attention(): pl.pallas_call(attention_kernel, out_shape=(jax.ShapeDtypeStruct((half, w...  18.9 us
    pallas_call x1, Pallas kernels, pack_context(): pl.pallas_call(pack_context_kernel, out_shape=(jax.ShapeDtypeStruct((pool...  17.1 us
    ppermute x3, waiting for transfers between devices, body(): parts = [lax.ppermute(part, 'tp', hop) for part, hop in zip(parts, hops)]  5.88 us
    pallas_call x1, Pallas kernels, place(): pl.pallas_call(place_kernel, out_shape=(jax.ShapeDtypeStruct((slots, piec...  5.8 us
    ppermute x3, starting transfers between devices, body(): parts = [lax.ppermute(part, 'tp', hop) for part, hop in zip(parts, hops)]  5.02 us
    pallas_call x1, Pallas kernels, pack_queries(): pl.pallas_call(pack_queries_kernel, out_shape=(jax.ShapeDtypeStruct((pool...  4.03 us
    ppermute x3, starting transfers between devices, body(): parts = [own] + [lax.ppermute(own, 'tp', hop) for hop in hops]  3.33 us
  transfers between devices with their start and end apart: 14, of which 7 were waited for; matrix products, arithmetic and copies ran while one was open for 0% of the time, Pallas kernels for 44%

profile of v10, /device:TPU:1, one launch (start us, length us, event | category | flops | bytes accessed | tf_op | source)
XLA Modules:
  0.0 101.1 jit_solution(15586851489943566303)
XLA Ops:
  0.7 4.0 %pack_queries.1 = (bf16[16,264,128]{2,1,0:T(8,128)(2,1)}, s32[40]{0:T(128)S(1)}) custom-call(s32[512]{0:T(512)} %decode_slot.5, s32[2]{0:T(128)S(1)} %pad_add_fusion.where, bf16[4,32,8,192]{3,2,1,0:T(8,128)(2,1)} %q_hbm.1, bf16[4,32,576]{2,1,0:T(8,128)(2,1)} %n_hbm.1), custom_call_target="tpu_custom_call" | custom-call | flops 1000 | bytes 1000 | tf_op jit(solution)/shard_map/pack_queries/pallas_call | solution.py:93
  4.7 7.6 %all-to-all-start.1 = ((bf16[16,264,128]{2,1,0:T(8,128)(2,1)}), bf16[16,264,128]{2,1,0:T(8,128)(2,1)}, u32[]{:S(2)}, u32[]{:S(2)}) async-start(bf16[16,264,128]{2,1,0:T(8,128)(2,1)} %get-tuple-element.77), calls=%async_computation.1 | async-start | bytes 2162688 | tf_op jit(solution)/shard_map/all_to_all | solution.py:832
  12.4 17.1 %pack_context.1 = (bf16[16,480,128]{2,1,0:T(8,128)(2,1)}, s32[32]{0:T(128)}, s32[32]{0:T(128)S(1)}, s32[40]{0:T(128)S(1)}, s32[40]{0:T(128)}, /*index=5*/s32[1]{0:T(128)}) custom-call(s32[512]{0:T(512)} %decode_slot.5, s32[2]{0:T(128)S(1)} %pad_add_fusion.where, bf16[32,576,384]{2,1,0:T(8,128)(2,1)} %bitcast.5), custom_call_target="tpu_custom_call" | custom-call | flops 1000 | bytes 1000 | tf_op jit(solution)/shard_map/pack_context/pallas_call | solution.py:262
  29.5 6.6 %all-to-all-start.2 = ((bf16[16,480,128]{2,1,0:T(8,128)(2,1)}), bf16[16,480,128]{2,1,0:T(8,128)(2,1)S(1)}, u32[]{:S(2)}, u32[]{:S(2)}) async-start(bf16[16,480,128]{2,1,0:T(8,128)(2,1)} %get-tuple-element.79), calls=%async_computation.2 | async-start | bytes 3932160 | tf_op jit(solution)/shard_map/all_to_all | solution.py:832
  36.1 18.9 %attention.1 = (bf16[64,2560]{1,0:T(8,128)(2,1)}, bf16[64,2560]{1,0:T(8,128)(2,1)}) custom-call(s32[32]{0:T(128)} %get-tuple-element.81.placing, s32[512]{0:T(512)} %lengths.1, s32[2]{0:T(128)S(1)} %pad_add_fusion.where, bf16[16,264,128]{2,1,0:T(8,128)(2,1)} %all-to-all-done.1.payload_hbm, bf16[32,576,384]{2,1,0:T(8,128)(2,1)} %bitcast.6, ...), custom_call_target="tpu_custom_call" | custom-call | flops 1000 | bytes 1000 | tf_op jit(solution)/shard_map/attention/pallas_call | solution.py:651
  55.0 1.6 %collective-permute-start = (bf16[64,2560]{1,0:T(8,128)(2,1)}, bf16[64,2560]{1,0:T(8,128)(2,1)S(1)}, u32[]{:S(2)}, u32[]{:S(2)}) collective-permute-start(bf16[64,2560]{1,0:T(8,128)(2,1)} %get-tuple-element.85), channel_id=1, source_target_pairs={{0,1},{1,0},{2,3},{3,2},{4,5},{5,4},{6,7},{7,6},{8,9},{9,8},{10,11... | collective-permute-start | bytes 983048 | tf_op jit(solution)/shard_map/ppermute | solution.py:861
  56.6 1.5 %collective-permute-done.swapped = bf16[64,2560]{1,0:T(8,128)(2,1)S(1)} collective-permute-done((bf16[64,2560]{1,0:T(8,128)(2,1)}, bf16[64,2560]{1,0:T(8,128)(2,1)S(1)}, u32[]{:S(2)}, u32[]{:S(2)}) %collective-permute-start) | collective-permute-done | bytes 327712 | tf_op jit(solution)/shard_map/ppermute | solution.py:861
  58.1 1.0 copy-done
  59.0 0.6 share.1
  59.7 1.7 %collective-permute-start.1 = (bf16[64,640]{1,0:T(8,128)(2,1)S(1)}, bf16[64,640]{1,0:T(8,128)(2,1)S(1)}, u32[]{:S(2)}, u32[]{:S(2)}) collective-permute-start(bf16[64,640]{1,0:T(8,128)(2,1)S(1)} %get-tuple-element.87), channel_id=1, source_target_pairs={{0,2},{1,3},{2,0},{3,1},{4,6},{5,7},{6,4},{7,5},{8,10},{9,11},{10,... | collective-permute-start | bytes 245768 | tf_op jit(solution)/shard_map/ppermute | solution.py:863
  61.4 3.3 %collective-permute-start.2 = (bf16[64,640]{1,0:T(8,128)(2,1)S(1)}, bf16[64,640]{1,0:T(8,128)(2,1)S(1)}, u32[]{:S(2)}, u32[]{:S(2)}) collective-permute-start(bf16[64,640]{1,0:T(8,128)(2,1)S(1)} %get-tuple-element.88), channel_id=1, source_target_pairs={{0,4},{1,5},{2,6},{3,7},{4,0},{5,1},{6,2},{7,3},{8,12},{9,13},{10,... | collective-permute-start | bytes 245768 | tf_op jit(solution)/shard_map/ppermute | solution.py:863
  64.7 3.9 %collective-permute-done.2.rest_1_ = bf16[64,640]{1,0:T(8,128)(2,1)S(1)} collective-permute-done((bf16[64,640]{1,0:T(8,128)(2,1)S(1)}, bf16[64,640]{1,0:T(8,128)(2,1)S(1)}, u32[]{:S(2)}, u32[]{:S(2)}) %collective-permute-start.2) | collective-permute-done | bytes 81952 | tf_op jit(solution)/shard_map/ppermute | solution.py:863
  68.6 1.9 %collective-permute-done.3.rest_2_ = bf16[64,640]{1,0:T(8,128)(2,1)S(1)} collective-permute-done((bf16[64,640]{1,0:T(8,128)(2,1)S(1)}, bf16[64,640]{1,0:T(8,128)(2,1)S(1)}, u32[]{:S(2)}, u32[]{:S(2)}) %collective-permute-start.3) | collective-permute-done | bytes 81952 | tf_op jit(solution)/shard_map/ppermute | solution.py:863
  70.6 1.8 %pack_back.1 = bf16[16,72,128]{2,1,0:T(8,128)(2,1)} custom-call(s32[32]{0:T(128)S(1)} %copy-done.3, s32[40]{0:T(128)S(1)} %copy-done.4, bf16[16,480,128]{2,1,0:T(8,128)(2,1)S(1)} %all-to-all-done.2.direct, f32[64,640]{1,0:T(8,128)S(1)} %get-tuple-element.86.mine, bf16[64,640]{1,0:T(8,128)(2,1)S(1)} %collective-permute-done.1.rest_0_, ...), custom_call_target="tpu_custom_call" | custom-call | flops 1000 | bytes 1000 | tf_op jit(solution)/shard_map/pack_back/pallas_call | solution.py:743
  72.4 7.0 %all-to-all-start.3 = ((bf16[16,72,128]{2,1,0:T(8,128)(2,1)}), bf16[16,72,128]{2,1,0:T(8,128)(2,1)S(1)}, u32[]{:S(2)}, u32[]{:S(2)}) async-start(bf16[16,72,128]{2,1,0:T(8,128)(2,1)} %pack_back.1), calls=%async_computation.3 | async-start | bytes 589824 | tf_op jit(solution)/shard_map/all_to_all | solution.py:832
  79.4 5.8 %place_context.1 = (bf16[32,48,576]{2,1,0:T(8,128)(2,1)}, s32[40]{0:T(128)S(1)}) custom-call(s32[512]{0:T(512)S(1)} %copy-done.1, s32[512]{0:T(512)S(1)} %copy-done.2, s32[40]{0:T(128)S(1)} %get-tuple-element.172.arrival, s32[2]{0:T(128)S(1)} %pad_add_fusion.where, bf16[16,480,128]{2,1,0:T(8,128)(2,1)S(1)} %all-to-all-done.2.direct), custom_call_target="tpu_custom_call" | custom-call | flops 1000 | bytes 12000000 | tf_op jit(solution)/shard_map/place_context/pallas_call | solution.py:378
  85.2 2.0 %all-to-all-done.3.back.packed = bf16[16,72,128]{2,1,0:T(8,128)(2,1)S(1)} async-done(((bf16[16,72,128]{2,1,0:T(8,128)(2,1)}), bf16[16,72,128]{2,1,0:T(8,128)(2,1)S(1)}, u32[]{:S(2)}, u32[]{:S(2)}) %all-to-all-start.3) | async-done | bytes 294944 | tf_op jit(solution)/shard_map/all_to_all | solution.py:832
  87.2 0.8 unpack_back.1.rest_0_
  88.1 0.8 collective-permute-start.6
  88.9 2.5 %collective-permute-start.4 = (bf16[64,640]{1,0:T(8,128)(2,1)S(1)}, bf16[64,640]{1,0:T(8,128)(2,1)S(1)}, u32[]{:S(2)}, u32[]{:S(2)}) collective-permute-start(bf16[64,640]{1,0:T(8,128)(2,1)S(1)} %unpack_back.1.rest_0_), channel_id=1, source_target_pairs={{0,2},{1,3},{2,0},{3,1},{4,6},{5,7},{6,4},{7,5},{8,10},{9,11},{10,... | collective-permute-start | bytes 245768 | tf_op jit(solution)/shard_map/ppermute | solution.py:871
  91.4 3.1 %collective-permute-start.7 = (bf16[64,640]{1,0:T(8,128)(2,1)S(1)}, bf16[64,640]{1,0:T(8,128)(2,1)S(1)}, u32[]{:S(2)}, u32[]{:S(2)}) collective-permute-start(bf16[64,640]{1,0:T(8,128)(2,1)S(1)} %unpack_back.1.rest_0_), channel_id=1, source_target_pairs={{0,1},{1,0},{2,3},{3,2},{4,5},{5,4},{6,7},{7,6},{8,9},{9,8},{10,11... | collective-permute-start | bytes 245768 | tf_op jit(solution)/shard_map/ppermute | solution.py:872
  94.5 1.8 %place_strips.1 = bf16[32,48,576]{2,1,0:T(8,128)(2,1)} custom-call(s32[40]{0:T(128)S(1)} %get-tuple-element.173.coming, s32[40]{0:T(128)S(1)} %get-tuple-element.174.lengths, s32[2]{0:T(128)S(1)} %pad_add_fusion.where, bf16[16,72,128]{2,1,0:T(8,128)(2,1)S(1)} %all-to-all-done.3.back.packed, ...), custom_call_target="tpu_custom_call", output_to_operand_aliasing={{}: (4, {})} | custom-call | flops 1000 | bytes 6000000 | tf_op jit(solution)/shard_map/place_strips/pallas_call | solution.py:439
  96.9 0.9 collective-permute-start.8
  99.3 1.8 %assemble.1 = bf16[32,4,2560]{2,1,0:T(4,128)(2,1)} custom-call(s32[2]{0:T(128)S(1)} %get-tuple-element.226, bf16[64,640]{1,0:T(8,128)(2,1)S(1)} %unpack_back.1.rest_0_, bf16[64,640]{1,0:T(8,128)(2,1)S(1)} %collective-permute-done.4.rest_1_, bf16[64,640]{1,0:T(8,128)(2,1)S(1)} %collective-permute-done.5.rest_2_, ...), custom_call_target="tpu_custom_call" | custom-call | flops 1000 | bytes 1000 | tf_op jit(solution)/shard_map/assemble/pallas_call | solution.py:816
  (25 shorter events, 2.1 us)
Async XLA Ops:
  4.7 24.7 %all-to-all-start.1 = ((bf16[16,264,128]{2,1,0:T(8,128)(2,1)}), bf16[16,264,128]{2,1,0:T(8,128)(2,1)}, u32[]{:S(2)}, u32[]{:S(2)}) async-start(bf16[16,264,128]{2,1,0:T(8,128)(2,1)} %get-tuple-element.77), calls=%async_computation.1 | async-start | bytes 2162688 | tf_op jit(solution)/shard_map/all_to_all | solution.py:832
  29.5 41.1 %all-to-all-start.2 = ((bf16[16,480,128]{2,1,0:T(8,128)(2,1)}), bf16[16,480,128]{2,1,0:T(8,128)(2,1)S(1)}, u32[]{:S(2)}, u32[]{:S(2)}) async-start(bf16[16,480,128]{2,1,0:T(8,128)(2,1)} %get-tuple-element.79), calls=%async_computation.2 | async-start | bytes 3932160 | tf_op jit(solution)/shard_map/all_to_all | solution.py:832
  36.1 34.5 %copy-start.3 = (s32[32]{0:T(128)S(1)}, s32[32]{0:T(128)}, u32[]{:S(2)}) copy-start(s32[32]{0:T(128)} %get-tuple-element.81.placing) | copy-start | bytes 388
  36.1 34.5 %copy-start.4 = (s32[40]{0:T(128)S(1)}, s32[40]{0:T(128)}, u32[]{:S(2)}) copy-start(s32[40]{0:T(128)} %get-tuple-element.82.relay) | copy-start | bytes 484
  36.1 43.3 %copy-start.2 = (s32[512]{0:T(512)S(1)}, s32[512]{0:T(512)}, u32[]{:S(2)}) copy-start(s32[512]{0:T(512)} %lengths.1) | copy-start | bytes 6148
  55.0 24.4 %copy-start.1 = (s32[512]{0:T(512)S(1)}, s32[512]{0:T(512)}, u32[]{:S(2)}) copy-start(s32[512]{0:T(512)} %decode_slot.5) | copy-start | bytes 6148
  55.0 3.1 %collective-permute-start = (bf16[64,2560]{1,0:T(8,128)(2,1)}, bf16[64,2560]{1,0:T(8,128)(2,1)S(1)}, u32[]{:S(2)}, u32[]{:S(2)}) collective-permute-start(bf16[64,2560]{1,0:T(8,128)(2,1)} %get-tuple-element.85), channel_id=1, source_target_pairs={{0,1},{1,0},{2,3},{3,2},{4,5},{5,4},{6,7},{7,6},{8,9},{9,8},{10,11... | collective-permute-start | bytes 983048 | tf_op jit(solution)/shard_map/ppermute | solution.py:861
  58.1 1.0 copy-start
  59.7 5.0 %collective-permute-start.1 = (bf16[64,640]{1,0:T(8,128)(2,1)S(1)}, bf16[64,640]{1,0:T(8,128)(2,1)S(1)}, u32[]{:S(2)}, u32[]{:S(2)}) collective-permute-start(bf16[64,640]{1,0:T(8,128)(2,1)S(1)} %get-tuple-element.87), channel_id=1, source_target_pairs={{0,2},{1,3},{2,0},{3,1},{4,6},{5,7},{6,4},{7,5},{8,10},{9,11},{10,... | collective-permute-start | bytes 245768 | tf_op jit(solution)/shard_map/ppermute | solution.py:863
  61.4 7.3 %collective-permute-start.2 = (bf16[64,640]{1,0:T(8,128)(2,1)S(1)}, bf16[64,640]{1,0:T(8,128)(2,1)S(1)}, u32[]{:S(2)}, u32[]{:S(2)}) collective-permute-start(bf16[64,640]{1,0:T(8,128)(2,1)S(1)} %get-tuple-element.88), channel_id=1, source_target_pairs={{0,4},{1,5},{2,6},{3,7},{4,0},{5,1},{6,2},{7,3},{8,12},{9,13},{10,... | collective-permute-start | bytes 245768 | tf_op jit(solution)/shard_map/ppermute | solution.py:863
  64.7 5.9 %collective-permute-start.3 = (bf16[64,640]{1,0:T(8,128)(2,1)S(1)}, bf16[64,640]{1,0:T(8,128)(2,1)S(1)}, u32[]{:S(2)}, u32[]{:S(2)}) collective-permute-start(bf16[64,640]{1,0:T(8,128)(2,1)S(1)} %get-tuple-element.89), channel_id=1, source_target_pairs={{0,6},{1,7},{2,4},{3,5},{4,2},{5,3},{6,0},{7,1},{8,14},{9,15},{10,... | collective-permute-start | bytes 245768 | tf_op jit(solution)/shard_map/ppermute | solution.py:863
  72.4 14.8 %all-to-all-start.3 = ((bf16[16,72,128]{2,1,0:T(8,128)(2,1)}), bf16[16,72,128]{2,1,0:T(8,128)(2,1)S(1)}, u32[]{:S(2)}, u32[]{:S(2)}) async-start(bf16[16,72,128]{2,1,0:T(8,128)(2,1)} %pack_back.1), calls=%async_computation.3 | async-start | bytes 589824 | tf_op jit(solution)/shard_map/all_to_all | solution.py:832
  88.1 8.8 %collective-permute-start.6 = (bf16[64,640]{1,0:T(8,128)(2,1)S(1)}, bf16[64,640]{1,0:T(8,128)(2,1)S(1)}, u32[]{:S(2)}, u32[]{:S(2)}) collective-permute-start(bf16[64,640]{1,0:T(8,128)(2,1)S(1)} %unpack_back.1.rest_0_), channel_id=1, source_target_pairs={{0,6},{1,7},{2,4},{3,5},{4,2},{5,3},{6,0},{7,1},{8,14},{9,15},{10,... | collective-permute-start | bytes 245768 | tf_op jit(solution)/shard_map/ppermute | solution.py:871
  88.9 8.0 %collective-permute-start.5 = (bf16[64,640]{1,0:T(8,128)(2,1)S(1)}, bf16[64,640]{1,0:T(8,128)(2,1)S(1)}, u32[]{:S(2)}, u32[]{:S(2)}) collective-permute-start(bf16[64,640]{1,0:T(8,128)(2,1)S(1)} %unpack_back.1.rest_0_), channel_id=1, source_target_pairs={{0,4},{1,5},{2,6},{3,7},{4,0},{5,1},{6,2},{7,3},{8,12},{9,13},{10,... | collective-permute-start | bytes 245768 | tf_op jit(solution)/shard_map/ppermute | solution.py:871
  88.9 8.0 %collective-permute-start.4 = (bf16[64,640]{1,0:T(8,128)(2,1)S(1)}, bf16[64,640]{1,0:T(8,128)(2,1)S(1)}, u32[]{:S(2)}, u32[]{:S(2)}) collective-permute-start(bf16[64,640]{1,0:T(8,128)(2,1)S(1)} %unpack_back.1.rest_0_), channel_id=1, source_target_pairs={{0,2},{1,3},{2,0},{3,1},{4,6},{5,7},{6,4},{7,5},{8,10},{9,11},{10,... | collective-permute-start | bytes 245768 | tf_op jit(solution)/shard_map/ppermute | solution.py:871
  91.4 6.9 %collective-permute-start.7 = (bf16[64,640]{1,0:T(8,128)(2,1)S(1)}, bf16[64,640]{1,0:T(8,128)(2,1)S(1)}, u32[]{:S(2)}, u32[]{:S(2)}) collective-permute-start(bf16[64,640]{1,0:T(8,128)(2,1)S(1)} %unpack_back.1.rest_0_), channel_id=1, source_target_pairs={{0,1},{1,0},{2,3},{3,2},{4,5},{5,4},{6,7},{7,6},{8,9},{9,8},{10,11... | collective-permute-start | bytes 245768 | tf_op jit(solution)/shard_map/ppermute | solution.py:872
  96.9 1.8 %collective-permute-start.8 = (bf16[64,640]{1,0:T(8,128)(2,1)S(1)}, bf16[64,640]{1,0:T(8,128)(2,1)S(1)}, u32[]{:S(2)}, u32[]{:S(2)}) collective-permute-start(bf16[64,640]{1,0:T(8,128)(2,1)S(1)} %collective-permute-done.4.rest_1_), channel_id=1, source_target_pairs={{0,1},{1,0},{2,3},{3,2},{4,5},{5,4},{6,7},{7,6},{8,9},{9,8},{10,11... | collective-permute-start | bytes 245768 | tf_op jit(solution)/shard_map/ppermute | solution.py:886
  97.8 1.3 %collective-permute-start.9 = (bf16[64,640]{1,0:T(8,128)(2,1)S(1)}, bf16[64,640]{1,0:T(8,128)(2,1)S(1)}, u32[]{:S(2)}, u32[]{:S(2)}) collective-permute-start(bf16[64,640]{1,0:T(8,128)(2,1)S(1)} %collective-permute-done.5.rest_2_), channel_id=1, source_target_pairs={{0,1},{1,0},{2,3},{3,2},{4,5},{5,4},{6,7},{7,6},{8,9},{9,8},{10,11... | collective-permute-start | bytes 245768 | tf_op jit(solution)/shard_map/ppermute | solution.py:886
  97.8 1.4 %collective-permute-start.10 = (bf16[64,640]{1,0:T(8,128)(2,1)S(1)}, bf16[64,640]{1,0:T(8,128)(2,1)S(1)}, u32[]{:S(2)}, u32[]{:S(2)}) collective-permute-start(bf16[64,640]{1,0:T(8,128)(2,1)S(1)} %collective-permute-done.6.rest_3_), channel_id=1, source_target_pairs={{0,1},{1,0},{2,3},{3,2},{4,5},{5,4},{6,7},{7,6},{8,9},{9,8},{10,11... | collective-permute-start | bytes 245768 | tf_op jit(solution)/shard_map/ppermute | solution.py:886
